TPU v7x, 512 devices: a whole 4x8x8 slice. The times are simulated.
512 devices in a mesh: dp: 32 (over z_hi, y, core), tensor: 16 (over z_lo, x).
Axes of the slice: x: 4, y: 8, z: 8 (z_hi: 2, z_lo: 4; z = z_hi * 4 + z_lo), core: 2. Of those that a mesh axis runs over, the one named last changes fastest.
Arguments:
- activ: bfloat16 [8192, 4096], P('tensor', 'dp'), may hold values from -6 to 6
- random_sign_flags: int32 [8192], P('tensor'), may hold values from 0 to 1
- codes: int32 [8192, 1024], P('tensor'), may hold values from 0 to 65535
- scales: bfloat16 [64, 4096], P('tensor'), may hold values from 0.0009994507 to 0.0039978027
- adapter_down_map: bfloat16 [8192, 64], P('tensor'), may hold values from -0.0625 to 0.0625
- adapter_up_map: bfloat16 [64, 4096], replicated, may hold values from -0.75 to 0.75
- cotangent: bfloat16 [4096, 4096], P('tensor', 'dp'), may hold values from -6 to 6
Outputs:
- out: bfloat16 [4096, 4096], P('tensor', 'dp')
- input_gradient: bfloat16 [8192, 4096], P('tensor', 'dp')
- down_map_gradient: float32 [8192, 64], P('tensor')
- up_map_gradient: float32 [64, 4096], P(None, 'tensor')
Inputs may be any that keep to these rules, and one draw needn't show every extreme that they name: Each word packs the codes of four consecutive output features, the lowest four bits for the first.
All inputs are finite; a program needn't handle non-finite values.
Results may differ from a plain program's by a relative error of at most 0.0055.
Values may be sent and summed in bfloat16 or wider, within the bound.
No kernel may reach another device: no remote copies, remote signals or barrier semaphores. Data moves between devices by JAX's collectives and lax.ppermute only.
A program may use at most 128 MiB of HBM per device.

v0:
```python
import math

import jax
import jax.numpy as jnp
from jax import lax
from jax.sharding import PartitionSpec as P

HEADS = 64
OUTPUT_FEATURES = 4096
GROUP = 128


ADAPTER_SCALE = 0.5


def partner_2(value, axis, distance):
    mask = 2**distance
    pairs = [(source, source ^ mask) for source in range(lax.axis_size(axis))]
    return lax.ppermute(value, axis, pairs)


def hadamard(order):
    counter = jnp.arange(order, dtype=jnp.int32)
    parity = jnp.zeros((order, order), jnp.int32)
    for bit_index in range(order.bit_length() - 1):
        parity = parity + (counter[:, None] >> bit_index & 1) * (counter[None, :] >> bit_index & 1)
    return (1 - 2 * (parity % 2)).astype(jnp.float32)


def dequant(codes, scales):
    offsets = jnp.arange(4, dtype=jnp.int32) * 4
    nibbles = codes[:, :, None] >> offsets & 15
    nibbles = nibbles.reshape(codes.shape[0], codes.shape[1] * 4)
    in_count = nibbles.shape[0]
    output_feature_count = nibbles.shape[1]
    values = (
        (nibbles - 8).astype(jnp.float32).reshape(in_count // GROUP, GROUP, output_feature_count)
    )
    values = values * scales.astype(jnp.float32)[:, None, :]
    return values.reshape(in_count, output_feature_count).astype(jnp.bfloat16)


def local(activ, random_sign_flags, codes, scales, adapter_down_map, adapter_up_map, cotangent):
    maximum_precision = lax.Precision.HIGHEST
    local_feat = activ.shape[0]
    token_count = activ.shape[1]
    groups = lax.axis_size("tensor")
    heads_local = HEADS // groups
    feature_position = lax.axis_index("tensor")
    root = math.sqrt(HEADS)
    flips = (2 * random_sign_flags - 1).astype(jnp.float32)[:, None]
    local_table = hadamard(heads_local)
    current = activ.astype(jnp.float32) * flips
    current = jnp.dot(local_table, current.reshape(heads_local, -1), precision=maximum_precision)
    for bit_index in range(groups.bit_length() - 1):
        partner = partner_2(current, "tensor", bit_index)
        high_side = feature_position >> bit_index & 1 == 1
        current = jnp.where(high_side, partner - current, current + partner)
    rotated_input = (current / root).reshape(local_feat, token_count).astype(jnp.bfloat16)
    weight = dequant(codes, scales)
    down_product_piece = jnp.einsum(
        "yi,ym->im", adapter_down_map, rotated_input, preferred_element_type=jnp.float32
    )
    down_product = lax.psum(down_product_piece, "tensor")
    output_feature_count = OUTPUT_FEATURES // groups
    w_cols = weight
    quantized_output = lax.psum_scatter(
        jnp.einsum("fo,ft->ot", w_cols, rotated_input, preferred_element_type=jnp.float32),
        "tensor",
        scatter_dimension=0,
        tiled=True,
    )
    up_matrix_wide = adapter_up_map.astype(jnp.float32)
    b_own = lax.dynamic_slice_in_dim(
        up_matrix_wide, feature_position * output_feature_count, output_feature_count, 1
    )
    adapter_output = jnp.einsum("ro,rt->ot", b_own, down_product, precision=maximum_precision)
    out = (quantized_output + ADAPTER_SCALE * adapter_output).astype(jnp.bfloat16)
    up_matrix_narrow = lax.dynamic_slice_in_dim(
        adapter_up_map, feature_position * output_feature_count, output_feature_count, 1
    )
    back_part = jnp.dot(up_matrix_narrow, cotangent, preferred_element_type=jnp.float32)
    reverse_rows = lax.psum(back_part, "tensor")
    w_cols = weight
    rotated_gradient = jnp.dot(
        w_cols,
        lax.all_gather(cotangent, "tensor", axis=0, tiled=True),
        preferred_element_type=jnp.float32,
    )
    rotated_gradient = rotated_gradient + ADAPTER_SCALE * jnp.dot(
        adapter_down_map.astype(jnp.float32), reverse_rows, precision=maximum_precision
    )
    current = jnp.dot(
        local_table, rotated_gradient.reshape(heads_local, -1), precision=maximum_precision
    )
    for bit_index in range(groups.bit_length() - 1):
        partner = partner_2(current, "tensor", bit_index)
        high_side = feature_position >> bit_index & 1 == 1
        current = jnp.where(high_side, partner - current, current + partner)
    turned = (current / root).reshape(local_feat, token_count)
    input_gradient = (flips * turned).astype(jnp.bfloat16)
    multiplier = ADAPTER_SCALE / math.sqrt(token_count * lax.axis_size("dp"))
    down_gradient_piece = multiplier * jnp.einsum(
        "ft,rt->fr", rotated_input.astype(jnp.float32), reverse_rows, precision=maximum_precision
    )
    up_gradient_piece = multiplier * jnp.einsum(
        "rt,ot->ro", down_product, cotangent.astype(jnp.float32), precision=maximum_precision
    )
    down_map_gradient, up_map_gradient = lax.psum((down_gradient_piece, up_gradient_piece), "dp")
    return (out, input_gradient, down_map_gradient, up_map_gradient)


def solution(mesh):
    in_specs = (
        P("tensor", "dp"),
        P("tensor"),
        P("tensor", None),
        P("tensor", None),
        P("tensor", None),
        P(),
        P("tensor", "dp"),
    )
    out_specs = (P("tensor", "dp"), P("tensor", "dp"), P("tensor", None), P(None, "tensor"))
    return jax.shard_map(local, mesh=mesh, in_specs=in_specs, out_specs=out_specs, check_vma=False)
```

profile of v0, /device:TPU:6, one launch (start us, length us, event | category | flops | bytes accessed | tf_op | source)
XLA Modules:
  0.0 750.0 jit_solution(12299962535572417774)
XLA Ops:
  7.3 0.7 add_convert_fusion
  8.0 0.6 copy-done.7
  8.6 1.0 convert_multiply_fusion
  9.6 0.1 reshape.98
  9.7 0.6 fusion.19
  10.4 2.7 collective-permute-start
  13.1 7.2 collective-permute-done
  20.4 5.5 collective-permute-start.1
  25.9 5.0 collective-permute-done.1
  31.0 4.3 collective-permute-start.2
  35.4 4.4 collective-permute-done.2
  39.9 6.1 collective-permute-start.3
  46.0 2.9 copy.12
  48.9 1.2 copy.13
  50.2 0.3 shift_right_arithmetic.90
  50.4 6.3 shift_right_arithmetic.87
  56.8 10.0 %shift_right_arithmetic.99 = s32[512,4096]{0,1:T(8,128)} reshape(s32[512,1024,4]{0,2,1:T(4,128)} %shift_right_arithmetic.87) | data formatting | bytes 16777216 | tf_op jit(solution)/shard_map/shift_right_arithmetic | solution.py:32
  66.8 0.8 fusion.10
  67.6 1.0 multiply_convert_fusion.2
  68.6 0.2 convert_element_type.67
  68.8 0.8 convolution_bitcast_fusion
  69.6 49.0 %all-gather.2.cloned.1.call-done = bf16[4096,128]{1,0:T(8,128)(2,1)} async-done(((bf16[256,128]{1,0:T(8,128)(2,1)}), bf16[4096,128]{1,0:T(8,128)(2,1)}) %all-gather.2.cloned.1.call-update) | async-done | bytes 1048592 | tf_op jit(solution)/shard_map/all_gather | solution.py:87
  118.6 9.4 %mul.124 = f32[4,128,4096]{1,0,2:T(4,128)S(1)} broadcast(f32[4,4096]{0,1:T(8,128)S(1)} %copy.13), dimensions={0,2} | broadcast | bytes 8454144 | tf_op jit(solution)/shard_map/mul | solution.py:39
  128.1 2.8 fusion.4
  130.9 143.1 %all-reduce.7.cloned.1.call-done = (f32[64,128]{1,0:T(8,128)}, f32[64,128]{1,0:T(8,128)}) async-done(((f32[64,128]{1,0:T(8,128)}, f32[64,128]{1,0:T(8,128)}), (f32[64,128]{1,0:T(8,128)}, f32[64,128]{1,0:T(8,128)})) %all-reduce.7.cloned.1.call-update) | async-done | bytes 65552 | tf_op jit(solution)/shard_map/psum | solution.py:64
  274.0 1.1 fusion.7
  275.1 0.1 reshape.99
  275.2 0.6 fusion.17
  275.9 4.7 collective-permute-start.4
  280.6 10.6 %shift_right_arithmetic.88 = s32[4,128,4096]{1,0,2:T(4,128)} reshape(s32[512,1024,4]{0,2,1:T(4,128)} %shift_right_arithmetic.87) | data formatting | bytes 16777216 | tf_op jit(solution)/shard_map/shift_right_arithmetic | solution.py:32
  291.2 1.0 add_select_fusion.2
  292.2 5.4 collective-permute-start.5
  297.7 16.6 %multiply_convert_fusion = bf16[4,128,4096]{1,0,2:T(4,128)(2,1)S(1)} fusion(s32[4,128,4096]{1,0,2:T(4,128)} %shift_right_arithmetic.88, f32[4,4096]{0,1:T(8,128)S(1)} %copy.13, s32[4096]{0:T(1024)S(1)} %shift_right_arithmetic.90), kind=kLoop, calls=%fused_computation.2 | loop fusion | flops 12582912 | bytes 12664832 | tf_op jit(solution)/shard_map/convert_element_type | solution.py:40
  314.4 1.9 collective-permute-start.6
  316.3 2.6 fusion.1
  319.0 5.4 collective-permute-done.6
  324.5 1.9 collective-permute-start.7
  326.4 0.8 convolution_multiply_fusion.3
  327.2 0.9 convolution_multiply_fusion.1
  328.2 7.2 collective-permute-done.7
  335.4 0.1 select_multiply_fusion
  335.5 0.2 reshape.100
  335.7 0.8 multiply_convert_fusion.1
  336.5 65.3 %reduce-scatter.2.cloned.1.call-done = f32[256,128]{1,0:T(8,128)} async-done(((f32[4096,128]{1,0:T(8,128)}), f32[256,128]{1,0:T(8,128)}) %reduce-scatter.2.cloned.1.call-update) | async-done | bytes 131088 | tf_op jit(solution)/shard_map/reduce_scatter | solution.py:67
  401.8 1.8 fusion.9
  403.6 336.8 %all-reduce.5.cloned.1.call-done = (f32[512,64]{0,1:T(8,128)}, f32[64,256]{1,0:T(8,128)}) async-done(((f32[512,64]{0,1:T(8,128)}, f32[64,256]{1,0:T(8,128)}), (f32[512,64]{0,1:T(8,128)}, f32[64,256]{1,0:T(8,128)})) %all-reduce.5.cloned.1.call-update) | async-done | bytes 196624 | tf_op jit(solution)/shard_map/psum | solution.py:109
  740.4 1.6 copy.28
  742.0 1.5 copy.29
  (44 shorter events, 0.7 us)
Async XLA Ops:
  7.2 59.6 %copy-start = (bf16[64,4096]{1,0:T(8,128)(2,1)S(1)}, bf16[64,4096]{1,0:T(8,128)(2,1)}, u32[]{:S(2)}) copy-start(bf16[64,4096]{1,0:T(8,128)(2,1)} %param.12) | copy-start | bytes 1572868
  7.2 111.4 %all-gather.2.cloned.1.call-start = ((), (), s32[]{:S(2)}) async-start(), calls=%async_computation.2 | async-start | bytes 1114112 | tf_op jit(solution)/shard_map/all_gather | solution.py:87
  7.2 5.9 copy-start.9
  7.2 5.9 copy-start.11
  8.0 0.6 copy-start.7
  10.4 9.9 %collective-permute-start = (f32[4,16384]{1,0:T(4,128)S(1)}, f32[4,16384]{1,0:T(4,128)S(1)}, u32[]{:S(2)}, u32[]{:S(2)}) collective-permute-start(f32[4,16384]{1,0:T(4,128)S(1)} %fusion.19), channel_id=1, source_target_pairs={{0,1},{1,0},{2,3},{3,2},{4,5},{5,4},{6,7},{7,6},{8,9},{9,8},{10,11... | collective-permute-start | bytes 786440 | tf_op jit(solution)/shard_map/ppermute | solution.py:19
  20.4 10.6 %collective-permute-start.1 = (f32[4,16384]{1,0:T(4,128)S(1)}, f32[4,16384]{1,0:T(4,128)S(1)}, u32[]{:S(2)}, u32[]{:S(2)}) collective-permute-start(f32[4,16384]{1,0:T(4,128)S(1)} %add_select_fusion.5), channel_id=1, source_target_pairs={{0,2},{1,3},{2,0},{3,1},{4,6},{5,7},{6,4},{7,5},{8,10},{9,11},{10,... | collective-permute-start | bytes 786440 | tf_op jit(solution)/shard_map/ppermute | solution.py:19
  31.0 8.8 %collective-permute-start.2 = (f32[4,16384]{1,0:T(4,128)S(1)}, f32[4,16384]{1,0:T(4,128)S(1)}, u32[]{:S(2)}, u32[]{:S(2)}) collective-permute-start(f32[4,16384]{1,0:T(4,128)S(1)} %add_select_fusion.4), channel_id=1, source_target_pairs={{0,4},{1,5},{2,6},{3,7},{4,0},{5,1},{6,2},{7,3},{8,12},{9,13},{10,... | collective-permute-start | bytes 786440 | tf_op jit(solution)/shard_map/ppermute | solution.py:19
  35.4 238.6 %all-reduce.7.cloned.1.call-start = ((), (), s32[]{:S(2)}) async-start(), calls=%async_computation.4 | async-start | bytes 131072 | tf_op jit(solution)/shard_map/psum | solution.py:64
  39.9 27.7 %collective-permute-start.3 = (f32[4,16384]{1,0:T(4,128)S(1)}, f32[4,16384]{1,0:T(4,128)}, u32[]{:S(2)}, u32[]{:S(2)}) collective-permute-start(f32[4,16384]{1,0:T(4,128)S(1)} %add_select_fusion.3), channel_id=1, source_target_pairs={{0,8},{1,9},{2,10},{3,11},{4,12},{5,13},{6,14},{7,15},{8,0},{9,1},... | collective-permute-start | bytes 786440 | tf_op jit(solution)/shard_map/ppermute | solution.py:19
  56.7 10.1 %copy-start.3 = (bf16[256,128]{1,0:T(8,128)(2,1)S(1)}, bf16[256,128]{1,0:T(8,128)(2,1)}, u32[]{:S(2)}) copy-start(bf16[256,128]{1,0:T(8,128)(2,1)} %param.13) | copy-start | bytes 196612
  56.7 12.0 %copy-start.4 = (bf16[512,64]{0,1:T(8,128)(2,1)S(1)}, bf16[512,64]{0,1:T(8,128)(2,1)}, u32[]{:S(2)}) copy-start(bf16[512,64]{0,1:T(8,128)(2,1)} %param.11) | copy-start | bytes 196612
  69.6 332.2 %reduce-scatter.2.cloned.1.call-start = ((), (), s32[]{:S(2)}) async-start(), calls=%async_computation.1 | async-start | bytes 2228224 | tf_op jit(solution)/shard_map/reduce_scatter | solution.py:67
  118.6 9.4 %copy-start.1 = (s32[512,4096]{0,1:T(8,128)S(1)}, s32[512,4096]{0,1:T(8,128)}, u32[]{:S(2)}) copy-start(s32[512,4096]{0,1:T(8,128)} %shift_right_arithmetic.99) | copy-start | bytes 25165828
  118.6 9.5 %copy-start.2 = (bf16[4096,128]{1,0:T(8,128)(2,1)S(1)}, bf16[4096,128]{1,0:T(8,128)(2,1)}, u32[]{:S(2)}) copy-start(bf16[4096,128]{1,0:T(8,128)(2,1)} %all-gather.2.cloned.1.call-done) | copy-start | bytes 3145732
  128.1 147.1 %copy-start.10 = (s32[4]{0:T(128)S(1)}, s32[4]{0:T(128)}, u32[]{:S(2)}) copy-start(s32[4]{0:T(128)} %copy-done.9) | copy-start | bytes 52
  128.1 147.1 %copy-start.12 = (s32[4]{0:T(128)S(1)}, s32[4]{0:T(128)}, u32[]{:S(2)}) copy-start(s32[4]{0:T(128)} %copy-done.11) | copy-start | bytes 52
  275.9 15.3 %collective-permute-start.4 = (f32[4,16384]{1,0:T(4,128)S(1)}, f32[4,16384]{1,0:T(4,128)}, u32[]{:S(2)}, u32[]{:S(2)}) collective-permute-start(f32[4,16384]{1,0:T(4,128)S(1)} %fusion.17), channel_id=1, source_target_pairs={{0,1},{1,0},{2,3},{3,2},{4,5},{5,4},{6,7},{7,6},{8,9},{9,8},{10,11... | collective-permute-start | bytes 786440 | tf_op jit(solution)/shard_map/ppermute | solution.py:19
  292.2 22.1 %collective-permute-start.5 = (f32[4,16384]{1,0:T(4,128)S(1)}, f32[4,16384]{1,0:T(4,128)S(1)}, u32[]{:S(2)}, u32[]{:S(2)}) collective-permute-start(f32[4,16384]{1,0:T(4,128)S(1)} %add_select_fusion.2), channel_id=1, source_target_pairs={{0,2},{1,3},{2,0},{3,1},{4,6},{5,7},{6,4},{7,5},{8,10},{9,11},{10,... | collective-permute-start | bytes 786440 | tf_op jit(solution)/shard_map/ppermute | solution.py:19
  314.3 12.1 %copy-start.6 = (f32[64,128]{1,0:T(8,128)S(1)}, f32[64,128]{1,0:T(8,128)}, u32[]{:S(2)}) copy-start(f32[64,128]{1,0:T(8,128)} %get-tuple-element.6) | copy-start | bytes 98308
  314.3 13.0 %copy-start.5 = (f32[64,128]{1,0:T(8,128)S(1)}, f32[64,128]{1,0:T(8,128)}, u32[]{:S(2)}) copy-start(f32[64,128]{1,0:T(8,128)} %get-tuple-element.7) | copy-start | bytes 98308
  314.3 21.4 %copy-start.8 = (f32[512]{0:T(512)S(1)}, f32[512]{0:T(512)}, u32[]{:S(2)}) copy-start(f32[512]{0:T(512)} %copy-done.7) | copy-start | bytes 6148
  314.4 10.0 %collective-permute-start.6 = (f32[4,16384]{1,0:T(4,128)S(1)}, f32[4,16384]{1,0:T(4,128)S(1)}, u32[]{:S(2)}, u32[]{:S(2)}) collective-permute-start(f32[4,16384]{1,0:T(4,128)S(1)} %add_select_fusion.1), channel_id=1, source_target_pairs={{0,4},{1,5},{2,6},{3,7},{4,0},{5,1},{6,2},{7,3},{8,12},{9,13},{10,... | collective-permute-start | bytes 786440 | tf_op jit(solution)/shard_map/ppermute | solution.py:19
  318.9 421.5 %all-reduce.5.cloned.1.call-start = ((), (), s32[]{:S(2)}) async-start(), calls=%async_computation.3 | async-start | bytes 393216 | tf_op jit(solution)/shard_map/psum | solution.py:109
  324.5 11.0 %collective-permute-start.7 = (f32[4,16384]{1,0:T(4,128)S(1)}, f32[4,16384]{1,0:T(4,128)S(1)}, u32[]{:S(2)}, u32[]{:S(2)}) collective-permute-start(f32[4,16384]{1,0:T(4,128)S(1)} %add_select_fusion), channel_id=1, source_target_pairs={{0,8},{1,9},{2,10},{3,11},{4,12},{5,13},{6,14},{7,15},{8,0},{9,1},... | collective-permute-start | bytes 786440 | tf_op jit(solution)/shard_map/ppermute | solution.py:19
Sparse Core Ops, SparseCore 0:
  35.5 83.0 all-gather.1
  122.1 151.7 all-reduce.6
  319.1 82.6 reduce-scatter.1
  405.5 334.8 all-reduce.4
where the time goes:
time: 751 us; the launch traced here: 750 us
  waiting for transfers between devices  623 us (83%)
  local copies, waits for them, and re-layouts  45 us (6%)
  starting transfers between devices  32.8 us (4%)
  other arithmetic  21.7 us (3%)
  between operations  14.1 us (2%)
  matrix products  12.9 us (2%)
    psum x1, waiting for transfers between devices, local(): lax.psum((down_gradient_piece, up_gradient_piece), 'dp')  337 us
    psum x1, waiting for transfers between devices, local(): down_product = lax.psum(down_product_piece, 'tensor')  143 us
    reduce_scatter x1, waiting for transfers between devices, local(): lax.psum_scatter(jnp.einsum('fo,ft->ot', w_cols, rotated_input, preferred...  65.3 us
    all_gather x1, waiting for transfers between devices, local(): lax.all_gather(cotangent, 'tensor', axis=0, tiled=True)  49 us
    ppermute x8, starting transfers between devices, partner_2(): return lax.ppermute(value, axis, pairs)  32.6 us
    ppermute x8, waiting for transfers between devices, partner_2(): return lax.ppermute(value, axis, pairs)  29.3 us
    shift_right_arithmetic x5, local copies, waits for them, and re-layouts, dequant(): nibbles = codes[:, :, None] >> offsets & 15  27.3 us
    convert_element_type x1, other arithmetic, dequant(): return values.reshape(in_count, output_feature_count).astype(jnp.bfloat16)  16.6 us
  transfers between devices with their start and end apart: 12, of which 9 were waited for; matrix products, arithmetic and copies ran while one was open for 9% of the time, Pallas kernels for 0%

commit v1 on v0

v1 whole, which is shorter than its diff:
```python
import jax
import jax.numpy as jnp
from jax import lax
from jax.experimental import pallas as pl
from jax.experimental.pallas import tpu as pltpu
from jax.sharding import PartitionSpec as P

HEADS = 64
GROUP = 128
RANK = 64
NT = 16
F = 512
O = 256
C = 1024
T = 128
ADAPTER_SCALE = 0.5
F32 = jnp.float32
BF16 = jnp.bfloat16
PARAMS = pltpu.CompilerParams(vmem_limit_bytes=40 * 1024 * 1024)
VMEM = pl.BlockSpec(memory_space=pltpu.VMEM)
SMEM = pl.BlockSpec(memory_space=pltpu.SMEM)


def dot(a, b):
    return jnp.dot(a, b, preferred_element_type=F32)


def dot_00(a, b):
    return lax.dot_general(a, b, (((0,), (0,)), ((), ())), preferred_element_type=F32)


def dot_11(a, b):
    return lax.dot_general(a, b, (((1,), (1,)), ((), ())), preferred_element_type=F32)


def split(a):
    high = a.astype(BF16)
    return high, (a - high.astype(F32)).astype(BF16)


def butterfly(v, bits):
    n = v.shape[0]
    rest = v.shape[1:]
    for bit in range(bits):
        w = v.reshape((n >> (bit + 1), 2, 1 << bit) + rest)
        low, high = w[:, 0], w[:, 1]
        v = jnp.stack([low + high, low - high], axis=1).reshape((n,) + rest)
    return v


def iota2(shape, dim):
    return lax.broadcasted_iota(jnp.int32, shape, dim)


def weights_kernel(codes, scales, up, weight, up_apart, scales_apart):
    group = pl.program_id(0)

    @pl.when(group == 0)
    def _():
        row, col = iota2((512, 512), 0), iota2((512, 512), 1)
        apart = jnp.where(row == 4 * (col & 127) + (col >> 7), 1.0, 0.0).astype(BF16)
        for block in range(8):
            lanes = slice(512 * block, 512 * (block + 1))
            s = dot(scales[:, lanes], apart)
            u = dot(up[:, lanes], apart).astype(BF16)
            for k in range(4):
                to = slice(128 * block, 128 * (block + 1))
                scales_apart[k, :, to] = s[:, 128 * k : 128 * (k + 1)]
                up_apart[k, :, to] = u[:, 128 * k : 128 * (k + 1)]

    for k in range(4):
        nibble = ((codes[...] >> (4 * k)) & 15) - 8
        scale = scales_apart[k, pl.ds(group, 1), :]
        weight[k] = (nibble.astype(F32) * scale).astype(BF16)


def make_weights(codes, scales, up):
    return pl.pallas_call(
        weights_kernel,
        grid=(F // GROUP,),
        in_specs=[
            pl.BlockSpec((GROUP, C), lambda g: (g, 0)),
            pl.BlockSpec((F // GROUP, 4 * C), lambda g: (0, 0)),
            pl.BlockSpec((RANK, 4 * C), lambda g: (0, 0)),
        ],
        out_specs=[
            pl.BlockSpec((4, GROUP, C), lambda g: (0, g, 0)),
            pl.BlockSpec((4, RANK, C), lambda g: (0, 0, 0)),
        ],
        out_shape=[
            jax.ShapeDtypeStruct((4, F, C), BF16),
            jax.ShapeDtypeStruct((4, RANK, C), BF16),
        ],
        scratch_shapes=[pltpu.VMEM((4, F // GROUP, C), F32)],
        compiler_params=PARAMS,
        cost_estimate=pl.CostEstimate(flops=20_000_000, bytes_accessed=7_000_000, transcendentals=0),
        name="weights",
    )(codes, scales, up)


def pack_kernel(activ, flags, down_map, cot, sent, cot_apart):
    eye = iota2((GROUP, GROUP), 0) == iota2((GROUP, GROUP), 1)
    parts = []
    for h in range(4):
        sign = (2 * flags[h : h + 1, :] - 1).astype(F32)
        diagonal = jnp.where(eye, sign, 0.0).astype(BF16)
        parts.append(dot(diagonal, activ[GROUP * h : GROUP * (h + 1), :]).reshape(NT, 8, T))
    lane, rank = iota2((RANK, 2 * RANK), 1), iota2((RANK, 2 * RANK), 0)
    left = jnp.where(lane == rank, 1.0, 0.0).astype(BF16)
    right = jnp.where(lane == rank + RANK, 1.0, 0.0).astype(BF16)
    for h in (0, 2):
        even = down_map[GROUP * h : GROUP * (h + 1), :]
        odd = down_map[GROUP * (h + 1) : GROUP * (h + 2), :]
        parts.append((dot(even, left) + dot(odd, right)).reshape(NT, 8, T))
    sent[...] = jnp.concatenate(parts, axis=1).astype(BF16)
    row, col = iota2((O, O), 0), iota2((O, O), 1)
    apart = jnp.where(col == 4 * (row & 63) + (row >> 6), 1.0, 0.0).astype(BF16)
    cot_apart[...] = dot(apart, cot[...]).astype(BF16)


def pack(activ, flags, down_map, cot):
    return pl.pallas_call(
        pack_kernel,
        in_specs=[VMEM] * 4,
        out_specs=[VMEM] * 2,
        out_shape=[
            jax.ShapeDtypeStruct((NT, 48, T), BF16),
            jax.ShapeDtypeStruct((O, T), BF16),
        ],
        compiler_params=PARAMS,
        cost_estimate=pl.CostEstimate(flops=60_000_000, bytes_accessed=600_000, transcendentals=0),
        name="pack",
    )(activ, flags, down_map, cot)


def mix_kernel(got, sent):
    v = got[:, 0:32, :].astype(F32).reshape(HEADS, 8, T)
    v = butterfly(v, 6) * 0.125
    mixed = v.reshape(NT, 32, T).astype(BF16)
    sent[:, 0:32, :] = mixed
    pairs = v.reshape(NT, 2, 2, 8, T)
    even = pairs[:, :, 0].reshape(256, T).astype(BF16)
    odd = pairs[:, :, 1].reshape(256, T).astype(BF16)
    maps = got[:, 32:48, :].reshape(256, 2 * RANK)
    down = dot_00(maps, even)[0:RANK] + dot_00(maps, odd)[RANK : 2 * RANK]
    sent[:, 32:96, :] = jnp.broadcast_to(down.astype(BF16)[None], (NT, RANK, T))


def mix(got):
    return pl.pallas_call(
        mix_kernel,
        in_specs=[VMEM],
        out_specs=VMEM,
        out_shape=jax.ShapeDtypeStruct((NT, 96, T), BF16),
        compiler_params=PARAMS,
        cost_estimate=pl.CostEstimate(flops=20_000_000, bytes_accessed=600_000, transcendentals=0),
        name="mix",
    )(got)


def project_kernel(got, weight, cot, shares, mixed, down, up_gradient):
    @pl.when(pl.program_id(0) == 0)
    def _():
        v = got[:, 0:32, :].astype(F32).reshape(NT, 4, 8, T)
        for h in range(4):
            mixed[GROUP * h : GROUP * (h + 1), :] = v[:, h].reshape(GROUP, T).astype(BF16)
        total = jnp.sum(got[:, 32:96, :].astype(F32), axis=0)
        down[...] = total
        high, low = split(total)
        for half in range(2):
            c = cot[GROUP * half : GROUP * (half + 1), :]
            up_gradient[RANK * half : RANK * (half + 1), :] = dot_11(high, c) + dot_11(low, c)

    share = dot_00(weight[0], mixed[...])
    shares[...] = share.reshape(NT, 64, T).astype(BF16)


def project(got, weight, cot):
    return pl.pallas_call(
        project_kernel,
        grid=(4,),
        in_specs=[
            pl.BlockSpec((NT, 96, T), lambda k: (0, 0, 0)),
            pl.BlockSpec((1, F, C), lambda k: (k, 0, 0)),
            pl.BlockSpec((O, T), lambda k: (0, 0)),
        ],
        out_specs=[
            pl.BlockSpec((NT, 64, T), lambda k: (0, k, 0)),
            pl.BlockSpec((F, T), lambda k: (0, 0)),
            pl.BlockSpec((RANK, T), lambda k: (0, 0)),
            pl.BlockSpec((2 * RANK, T), lambda k: (0, 0)),
        ],
        out_shape=[
            jax.ShapeDtypeStruct((NT, O, T), BF16),
            jax.ShapeDtypeStruct((F, T), BF16),
            jax.ShapeDtypeStruct((RANK, T), F32),
            jax.ShapeDtypeStruct((2 * RANK, T), F32),
        ],
        compiler_params=PARAMS,
        cost_estimate=pl.CostEstimate(flops=540_000_000, bytes_accessed=6_000_000, transcendentals=0),
        name="project",
    )(got, weight, cot)


def back_kernel(
    place, own, by1, by2, by3, weight, up_apart, down_map, mixed, up_gradient,
    current, narrow, keep, give, cot, total, back, sums,
):
    k = pl.program_id(0)

    @pl.when(k == 0)
    def _():
        for x, blocks in enumerate((own, by1, by2, by3)):
            for z in range(4):
                source = place[0] ^ (x + 4 * z)
                rows = pl.ds(pl.multiple_of(source * 64, 64), 64)
                for n in range(4):
                    cot[n, rows, :] = blocks[z, 64 * n : 64 * (n + 1), :]
        total[...] = jnp.zeros_like(total)
        back[...] = jnp.zeros_like(back)

    total[...] += dot(weight[0], cot[k])
    back[...] += dot(up_apart[0], cot[k])

    @pl.when(k == 3)
    def _():
        high, low = split(back[...])
        maps = down_map[...]
        g = total[...] + ADAPTER_SCALE * (dot(maps, high) + dot(maps, low))
        g = butterfly(g.reshape(4, GROUP, T), 2).reshape(F, T)
        current[...] = g
        narrow[...] = g.astype(BF16)
        zero = jnp.zeros((RANK, T), BF16)
        for half in range(2):
            m = mixed[256 * half : 256 * (half + 1), :]
            for n, part in enumerate((high, low)):
                side = jnp.concatenate([zero, part] if half else [part, zero], axis=0)
                product = dot_11(m, side)
                if half == 0 and n == 0:
                    gradient = product
                else:
                    gradient = gradient + product
        sums[0:256, :] = gradient
        sums[256:384, :] = up_gradient[...]
        keep[...] = sums[pl.ds(pl.multiple_of(place[1] * 192, 192), 192), :]
        give[...] = sums[pl.ds(pl.multiple_of(192 - place[1] * 192, 192), 192), :]


def backward(place, own, by1, by2, by3, weight, up_apart, down_map, mixed, up_gradient):
    whole2 = lambda k: (0, 0)
    whole3 = lambda k: (0, 0, 0)
    return pl.pallas_call(
        back_kernel,
        grid=(4,),
        in_specs=[SMEM]
        + [pl.BlockSpec((4, O, T), whole3)] * 4
        + [
            pl.BlockSpec((1, F, C), lambda k: (k, 0, 0)),
            pl.BlockSpec((1, RANK, C), lambda k: (k, 0, 0)),
            pl.BlockSpec((F, RANK), whole2),
            pl.BlockSpec((F, T), whole2),
            pl.BlockSpec((2 * RANK, T), whole2),
        ],
        out_specs=[
            pl.BlockSpec((F, T), whole2),
            pl.BlockSpec((F, T), whole2),
            pl.BlockSpec((192, T), whole2),
            pl.BlockSpec((192, T), whole2),
        ],
        out_shape=[
            jax.ShapeDtypeStruct((F, T), F32),
            jax.ShapeDtypeStruct((F, T), BF16),
            jax.ShapeDtypeStruct((192, T), F32),
            jax.ShapeDtypeStruct((192, T), F32),
        ],
        scratch_shapes=[
            pltpu.VMEM((4, C, T), BF16),
            pltpu.VMEM((F, T), F32),
            pltpu.VMEM((RANK, T), F32),
            pltpu.VMEM((384, T), F32),
        ],
        compiler_params=PARAMS,
        cost_estimate=pl.CostEstimate(flops=600_000_000, bytes_accessed=7_000_000, transcendentals=0),
        name="backward",
    )(place, own, by1, by2, by3, weight, up_apart, down_map, mixed, up_gradient)


def finish_kernel(place, shares, up, down, out):
    total = jnp.sum(shares[...].astype(F32), axis=0)
    row, col = iota2((O, O), 0), iota2((O, O), 1)
    together = jnp.where(row == 4 * (col & 63) + (col >> 6), 1.0, 0.0).astype(BF16)
    high, low = split(total)
    own = up[:, pl.ds(pl.multiple_of(place[0] * O, O), O)]
    down_high, down_low = split(down[...])
    adapter = dot_00(own, down_high) + dot_00(own, down_low)
    out[...] = (dot(together, high) + dot(together, low) + ADAPTER_SCALE * adapter).astype(BF16)


def finish(place, shares, up, down):
    return pl.pallas_call(
        finish_kernel,
        in_specs=[SMEM, VMEM, VMEM, VMEM],
        out_specs=VMEM,
        out_shape=jax.ShapeDtypeStruct((O, T), BF16),
        compiler_params=PARAMS,
        cost_estimate=pl.CostEstimate(flops=40_000_000, bytes_accessed=1_700_000, transcendentals=0),
        name="finish",
    )(place, shares, up, down)


def gradients_kernel(place, keep, other, down_gradient, up_gradient, sums):
    multiplier = ADAPTER_SCALE / 64.0
    sums[pl.ds(pl.multiple_of(place[1] * 192, 192), 192), :] = keep[...] * multiplier
    sums[pl.ds(pl.multiple_of(192 - place[1] * 192, 192), 192), :] = other[...] * multiplier
    down_gradient[0:256, :] = sums[0:256, 0:RANK]
    down_gradient[256:512, :] = sums[0:256, RANK : 2 * RANK]
    up_gradient[:, 0:128] = sums[256:320, :]
    up_gradient[:, 128:256] = sums[320:384, :]


def gradients(place, keep, other):
    return pl.pallas_call(
        gradients_kernel,
        in_specs=[SMEM, VMEM, VMEM],
        out_specs=[VMEM, VMEM],
        out_shape=[
            jax.ShapeDtypeStruct((F, RANK), F32),
            jax.ShapeDtypeStruct((RANK, O), F32),
        ],
        scratch_shapes=[pltpu.VMEM((384, T), F32)],
        compiler_params=PARAMS,
        cost_estimate=pl.CostEstimate(flops=100_000, bytes_accessed=500_000, transcendentals=0),
        name="gradients",
    )(place, keep, other)


def by(value, axis, mask):
    pairs = [(source, source ^ mask) for source in range(lax.axis_size(axis))]
    return lax.ppermute(value, axis, pairs)


def local(activ, flags, codes, scales, down_map, up, cot):
    me = lax.axis_index("tensor")
    replica = lax.axis_index("dp")
    place = jnp.stack([me, replica & 1]).astype(jnp.int32)
    sent, cot_apart = pack(activ, flags.reshape(4, GROUP), down_map, cot)
    got = lax.all_to_all(sent, "tensor", 0, 0, tiled=True)
    weight, up_apart = make_weights(codes, scales, up)

    along_z = [cot_apart] + [by(cot_apart, "tensor", 4 * z) for z in (1, 2, 3)]
    own = jnp.stack(along_z)
    by1, by2, by3 = (by(own, "tensor", x) for x in (1, 2, 3))

    got = lax.all_to_all(mix(got), "tensor", 0, 0, tiled=True)
    shares, mixed, down, up_part = project(got, weight, cot)
    shares = lax.all_to_all(shares, "tensor", 0, 0, tiled=True)

    current, narrow, keep, give = backward(
        place, own, by1, by2, by3, weight, up_apart, down_map, mixed, up_part
    )
    keep = keep + by(give, "dp", 1)
    for mask in (2, 4, 8, 16):
        keep = keep + by(keep, "dp", mask)
    down_gradient, up_gradient = gradients(place, keep, by(keep, "dp", 1))

    for bit in range(4):
        partner = by(narrow, "tensor", 1 << bit).astype(F32)
        current = jnp.where((me >> bit) & 1 == 1, partner - current, current + partner)
        narrow = current.astype(BF16)
    sign = (2 * flags - 1).astype(F32)[:, None]
    input_gradient = (sign * (current * 0.125)).astype(BF16)

    out = finish(place, shares, up, down)
    return out, input_gradient, down_gradient, up_gradient


def solution(mesh):
    in_specs = (
        P("tensor", "dp"),
        P("tensor"),
        P("tensor", None),
        P("tensor", None),
        P("tensor", None),
        P(),
        P("tensor", "dp"),
    )
    out_specs = (P("tensor", "dp"), P("tensor", "dp"), P("tensor", None), P(None, "tensor"))
    return jax.shard_map(local, mesh=mesh, in_specs=in_specs, out_specs=out_specs, check_vma=False)
```

time: 751 us -> 160 us (0.21)
  waiting for transfers between devices: 623 us -> 31.1 us
  starting transfers between devices: 32.8 us -> 75.1 us
  local copies, waits for them, and re-layouts: 45 us -> 18.2 us
  other arithmetic: 21.7 us -> 2.05 us
  blocking collectives: 0 us -> 16.8 us
  Pallas kernels: 0 us -> 14 us
  between operations: 14.1 us -> 0.98 us
  matrix products: 12.9 us -> 0 us
    psum x2 -> x0, waiting for transfers between devices: 480 us -> none  [the longest x1 337 us: local(): lax.psum((down_gradient_piece, up_gradient_piece), 'dp')]
    reduce_scatter x1 -> x0, waiting for transfers between devices: 65.3 us -> none  [local(): lax.psum_scatter(jnp.einsum('fo,ft->ot', w_cols, rotated_input, preferred...]
    all_gather x1 -> x0, waiting for transfers between devices: 49 us -> none  [local(): lax.all_gather(cotangent, 'tensor', axis=0, tiled=True)]
    ppermute x8 -> x16, starting transfers between devices: 32.6 us -> 61.2 us  [by(): return lax.ppermute(value, axis, pairs)]
    shift_right_arithmetic x5 -> x0, local copies, waits for them, and re-layouts: 27.3 us -> none  [dequant(): nibbles = codes[:, :, None] >> offsets & 15]
    convert_element_type x4, other arithmetic: 19.2 us -> 0.98 us  [the longest x1 0.79 us: local(): input_gradient = (sign * (current * 0.125)).astype(BF16)]
    all_to_all x0 -> x1, blocking collectives: none -> 16.8 us  [local(): got = lax.all_to_all(sent, 'tensor', 0, 0, tiled=True)]
    pallas_call x0 -> x7, Pallas kernels: none -> 14 us  [the longest x1 3.6 us: backward(): pl.pallas_call(back_kernel, grid=(4,), in_specs=[SMEM] + [pl.BlockSpec((4...]
  transfers between devices with their start and end apart: 12 -> 18, of which waited for: 9 -> 9; matrix products, arithmetic and copies ran while one was open for 9% -> 2% of each run, Pallas kernels for 0% -> 7%
where the time goes in v1:
time: 160 us; the launch traced here: 158 us
  starting transfers between devices  75.1 us (47%)
  waiting for transfers between devices  31.1 us (19%)
  local copies, waits for them, and re-layouts  18.2 us (11%)
  blocking collectives  16.8 us (10%)
  Pallas kernels  14 us (9%)
  other arithmetic  2.05 us (1%)
    ppermute x16, starting transfers between devices, by(): return lax.ppermute(value, axis, pairs)  61.2 us
    ppermute x16, waiting for transfers between devices, by(): return lax.ppermute(value, axis, pairs)  31.1 us
    unnamed x42, local copies, waits for them, and re-layouts  18.2 us
    all_to_all x1, blocking collectives, local(): got = lax.all_to_all(sent, 'tensor', 0, 0, tiled=True)  16.8 us
    all_to_all x1, starting transfers between devices, local(): shares = lax.all_to_all(shares, 'tensor', 0, 0, tiled=True)  7.58 us
    all_to_all x1, starting transfers between devices, local(): got = lax.all_to_all(mix(got), 'tensor', 0, 0, tiled=True)  6.29 us
    pallas_call x1, Pallas kernels, backward(): pl.pallas_call(back_kernel, grid=(4,), in_specs=[SMEM] + [pl.BlockSpec((4...  3.6 us
    pallas_call x1, Pallas kernels, project(): pl.pallas_call(project_kernel, grid=(4,), in_specs=[pl.BlockSpec((NT, 96,...  3.23 us
  transfers between devices with their start and end apart: 18, of which 9 were waited for; matrix products, arithmetic and copies ran while one was open for 2% of the time, Pallas kernels for 7%

profile of v1, /device:TPU:6, one launch (start us, length us, event | category | flops | bytes accessed | tf_op | source)
XLA Modules:
  0.0 158.3 jit_solution(9587605122012285984)
XLA Ops:
  0.6 1.0 copy.11.down_map
  1.6 0.8 copy-done.6
  2.5 0.9 copy-done.10
  3.4 0.7 copy-done.17
  4.3 16.8 %all_to_all.15.got = bf16[16,48,128]{2,1,0:T(8,128)(2,1)S(1)} all-to-all(bf16[16,48,128]{2,1,0:T(8,128)(2,1)S(1)} %get-tuple-element.18), channel_id=1, replica_groups=mesh['dp'=32,'tensor'=16] {'tensor'}, dimensions={0} | all-to-all | bytes 393216 | tf_op jit(solution)/shard_map/all_to_all | solution.py:347
  21.1 1.0 mix.1
  22.2 6.3 %all-to-all-start.1 = ((bf16[16,96,128]{2,1,0:T(8,128)(2,1)}), bf16[16,96,128]{2,1,0:T(8,128)(2,1)S(1)}, u32[]{:S(2)}, u32[]{:S(2)}) async-start(bf16[16,96,128]{2,1,0:T(8,128)(2,1)} %mix.1), calls=%async_computation.1 | async-start | bytes 786432 | tf_op jit(solution)/shard_map/all_to_all | solution.py:354
  28.5 5.2 %collective-permute-start.2 = (bf16[256,128]{1,0:T(8,128)(2,1)S(1)}, bf16[256,128]{1,0:T(8,128)(2,1)S(1)}, u32[]{:S(2)}, u32[]{:S(2)}) collective-permute-start(bf16[256,128]{1,0:T(8,128)(2,1)S(1)} %get-tuple-element.22), channel_id=1, source_target_pairs={{0,12},{1,13},{2,14},{3,15},{4,8},{5,9},{6,10},{7,11},{8,4},{9,5},... | collective-permute-start | bytes 196616 | tf_op jit(solution)/shard_map/ppermute | solution.py:339
  33.7 1.9 %collective-permute-start.1 = (bf16[256,128]{1,0:T(8,128)(2,1)S(1)}, bf16[256,128]{1,0:T(8,128)(2,1)S(1)}, u32[]{:S(2)}, u32[]{:S(2)}) collective-permute-start(bf16[256,128]{1,0:T(8,128)(2,1)S(1)} %get-tuple-element.22), channel_id=1, source_target_pairs={{0,8},{1,9},{2,10},{3,11},{4,12},{5,13},{6,14},{7,15},{8,0},{9,1},... | collective-permute-start | bytes 196616 | tf_op jit(solution)/shard_map/ppermute | solution.py:339
  35.6 3.0 %collective-permute-start = (bf16[256,128]{1,0:T(8,128)(2,1)S(1)}, bf16[256,128]{1,0:T(8,128)(2,1)S(1)}, u32[]{:S(2)}, u32[]{:S(2)}) collective-permute-start(bf16[256,128]{1,0:T(8,128)(2,1)S(1)} %get-tuple-element.22), channel_id=1, source_target_pairs={{0,4},{1,5},{2,6},{3,7},{4,0},{5,1},{6,2},{7,3},{8,12},{9,13},{10,... | collective-permute-start | bytes 196616 | tf_op jit(solution)/shard_map/ppermute | solution.py:339
  38.6 1.6 copy-done.3
  40.2 1.0 copy-done.4
  41.2 0.8 copy-done.16
  42.0 3.2 %weights.1 = (bf16[4,512,1024]{2,1,0:T(8,128)(2,1)S(1)}, bf16[4,64,1024]{2,1,0:T(8,128)(2,1)S(1)}) custom-call(s32[512,1024]{1,0:T(8,128)S(1)} %copy-done.3, bf16[4,4096]{1,0:T(4,128)(2,1)S(1)} %copy-done.16, bf16[64,4096]{1,0:T(8,128)(2,1)S(1)} %copy-done.4), custom_call_target="tpu_custom_call" | custom-call | flops 20000000 | bytes 7000000 | tf_op jit(solution)/shard_map/weights/pallas_call | solution.py:78
  45.2 2.0 %copy-done = bf16[4,512,1024]{2,1,0:T(8,128)(2,1)} copy-done((bf16[4,512,1024]{2,1,0:T(8,128)(2,1)}, bf16[4,512,1024]{2,1,0:T(8,128)(2,1)S(1)}, u32[]{:S(2)}) %copy-start) | copy-done | bytes 4194328
  47.1 2.2 %copy-done.1 = bf16[4,512,1024]{2,1,0:T(8,128)(2,1)S(1)} copy-done((bf16[4,512,1024]{2,1,0:T(8,128)(2,1)S(1)}, bf16[4,512,1024]{2,1,0:T(8,128)(2,1)}, u32[]{:S(2)}) %copy-start.1) | copy-done | bytes 4194328
  49.3 3.2 %project.1 = (bf16[16,256,128]{2,1,0:T(8,128)(2,1)}, bf16[512,128]{1,0:T(8,128)(2,1)S(1)}, f32[64,128]{1,0:T(8,128)S(1)}, f32[128,128]{1,0:T(8,128)S(1)}) custom-call(bf16[16,96,128]{2,1,0:T(8,128)(2,1)S(1)} %all-to-all-done.1.got, bf16[4,512,1024]{2,1,0:T(8,128)(2,1)S(1)} %copy-done.1, bf16[256,128]{1,0:T(8,128)(2,1)S(1)} %copy-done.7), custom_call_target="tpu_custom_call" | custom-call | flops 540000000 | bytes 6000000 | tf_op jit(solution)/shard_map/project/pallas_call | solution.py:179
  53.8 7.6 %all-to-all-start.2 = ((bf16[16,256,128]{2,1,0:T(8,128)(2,1)}), bf16[16,256,128]{2,1,0:T(8,128)(2,1)S(1)}, u32[]{:S(2)}, u32[]{:S(2)}) async-start(bf16[16,256,128]{2,1,0:T(8,128)(2,1)} %get-tuple-element.20), calls=%async_computation.2 | async-start | bytes 2097152 | tf_op jit(solution)/shard_map/all_to_all | solution.py:356
  61.5 2.8 %collective-permute-start.3 = (bf16[4,256,128]{2,1,0:T(8,128)(2,1)S(1)}, bf16[4,256,128]{2,1,0:T(8,128)(2,1)S(1)}, u32[]{:S(2)}, u32[]{:S(2)}) collective-permute-start(bf16[4,256,128]{2,1,0:T(8,128)(2,1)S(1)} %pad_maximum_fusion.own), channel_id=1, source_target_pairs={{0,1},{1,0},{2,3},{3,2},{4,5},{5,4},{6,7},{7,6},{8,9},{9,8},{10,11... | collective-permute-start | bytes 786440 | tf_op jit(solution)/shard_map/ppermute | solution.py:339
  64.3 2.6 %collective-permute-start.4 = (bf16[4,256,128]{2,1,0:T(8,128)(2,1)S(1)}, bf16[4,256,128]{2,1,0:T(8,128)(2,1)S(1)}, u32[]{:S(2)}, u32[]{:S(2)}) collective-permute-start(bf16[4,256,128]{2,1,0:T(8,128)(2,1)S(1)} %pad_maximum_fusion.own), channel_id=1, source_target_pairs={{0,2},{1,3},{2,0},{3,1},{4,6},{5,7},{6,4},{7,5},{8,10},{9,11},{10,... | collective-permute-start | bytes 786440 | tf_op jit(solution)/shard_map/ppermute | solution.py:339
  66.9 5.0 %collective-permute-start.5 = (bf16[4,256,128]{2,1,0:T(8,128)(2,1)S(1)}, bf16[4,256,128]{2,1,0:T(8,128)(2,1)S(1)}, u32[]{:S(2)}, u32[]{:S(2)}) collective-permute-start(bf16[4,256,128]{2,1,0:T(8,128)(2,1)S(1)} %pad_maximum_fusion.own), channel_id=1, source_target_pairs={{0,3},{1,2},{2,1},{3,0},{4,7},{5,6},{6,5},{7,4},{8,11},{9,10},{10,... | collective-permute-start | bytes 786440 | tf_op jit(solution)/shard_map/ppermute | solution.py:339
  72.0 5.3 %collective-permute-done.3.by1 = bf16[4,256,128]{2,1,0:T(8,128)(2,1)S(1)} collective-permute-done((bf16[4,256,128]{2,1,0:T(8,128)(2,1)S(1)}, bf16[4,256,128]{2,1,0:T(8,128)(2,1)S(1)}, u32[]{:S(2)}, u32[]{:S(2)}) %collective-permute-start.3) | collective-permute-done | bytes 262176 | tf_op jit(solution)/shard_map/ppermute | solution.py:339
  77.3 7.1 %collective-permute-done.4.by2 = bf16[4,256,128]{2,1,0:T(8,128)(2,1)S(1)} collective-permute-done((bf16[4,256,128]{2,1,0:T(8,128)(2,1)S(1)}, bf16[4,256,128]{2,1,0:T(8,128)(2,1)S(1)}, u32[]{:S(2)}, u32[]{:S(2)}) %collective-permute-start.4) | collective-permute-done | bytes 262176 | tf_op jit(solution)/shard_map/ppermute | solution.py:339
  84.4 2.5 %collective-permute-done.5.by3 = bf16[4,256,128]{2,1,0:T(8,128)(2,1)S(1)} collective-permute-done((bf16[4,256,128]{2,1,0:T(8,128)(2,1)S(1)}, bf16[4,256,128]{2,1,0:T(8,128)(2,1)S(1)}, u32[]{:S(2)}, u32[]{:S(2)}) %collective-permute-start.5) | collective-permute-done | bytes 262176 | tf_op jit(solution)/shard_map/ppermute | solution.py:339
  86.9 2.2 %copy-done.2 = bf16[4,512,1024]{2,1,0:T(8,128)(2,1)S(1)} copy-done((bf16[4,512,1024]{2,1,0:T(8,128)(2,1)S(1)}, bf16[4,512,1024]{2,1,0:T(8,128)(2,1)}, u32[]{:S(2)}) %copy-start.2) | copy-done | bytes 4194328
  89.1 0.9 copy-done.9
  90.0 0.8 copy-done.13
  90.9 3.6 %backward.1 = (f32[512,128]{1,0:T(8,128)S(1)}, bf16[512,128]{1,0:T(8,128)(2,1)}, f32[192,128]{1,0:T(8,128)S(1)}, f32[192,128]{1,0:T(8,128)S(1)}) custom-call(s32[2]{0:T(128)S(1)} %pad_add_fusion.place, bf16[4,256,128]{2,1,0:T(8,128)(2,1)S(1)} %pad_maximum_fusion.own, bf16[4,256,128]{2,1,0:T(8,128)(2,1)S(1)} %collective-permute-done.3.by1, ...), custom_call_target="tpu_custom_call" | custom-call | flops 600000000 | bytes 7000000 | tf_op jit(solution)/shard_map/backward/pallas_call | solution.py:252
  95.8 2.0 %collective-permute-start.6 = (bf16[512,128]{1,0:T(8,128)(2,1)}, bf16[512,128]{1,0:T(8,128)(2,1)S(1)}, u32[]{:S(2)}, u32[]{:S(2)}) collective-permute-start(bf16[512,128]{1,0:T(8,128)(2,1)} %get-tuple-element.26), channel_id=1, source_target_pairs={{0,1},{1,0},{2,3},{3,2},{4,5},{5,4},{6,7},{7,6},{8,9},{9,8},{10,11... | collective-permute-start | bytes 393224 | tf_op jit(solution)/shard_map/ppermute | solution.py:339
  97.8 5.1 %collective-permute-done.6 = bf16[512,128]{1,0:T(8,128)(2,1)S(1)} collective-permute-done((bf16[512,128]{1,0:T(8,128)(2,1)}, bf16[512,128]{1,0:T(8,128)(2,1)S(1)}, u32[]{:S(2)}, u32[]{:S(2)}) %collective-permute-start.6) | collective-permute-done | bytes 131104 | tf_op jit(solution)/shard_map/ppermute | solution.py:339
  103.0 2.6 %collective-permute-start.7 = (bf16[512,128]{1,0:T(8,128)(2,1)S(1)}, bf16[512,128]{1,0:T(8,128)(2,1)S(1)}, u32[]{:S(2)}, u32[]{:S(2)}) collective-permute-start(bf16[512,128]{1,0:T(8,128)(2,1)S(1)} %fusion.7), channel_id=1, source_target_pairs={{0,2},{1,3},{2,0},{3,1},{4,6},{5,7},{6,4},{7,5},{8,10},{9,11},{10,... | collective-permute-start | bytes 393224 | tf_op jit(solution)/shard_map/ppermute | solution.py:339
  105.6 1.9 %collective-permute-start.10 = (f32[192,128]{1,0:T(8,128)}, f32[192,128]{1,0:T(8,128)S(1)}, u32[]{:S(2)}, u32[]{:S(2)}) collective-permute-start(f32[192,128]{1,0:T(8,128)} %copy-done.19), channel_id=1, source_target_pairs={{0,16},{16,0},{32,48},{48,32},{64,80},{80,64},{96,112},{112,96},{1... | collective-permute-start | bytes 294920 | tf_op jit(solution)/shard_map/ppermute | solution.py:339
  107.5 1.5 collective-permute-done.10
  109.0 0.9 add.32
  109.9 3.5 %collective-permute-start.11 = (f32[192,128]{1,0:T(8,128)S(1)}, f32[192,128]{1,0:T(8,128)S(1)}, u32[]{:S(2)}, u32[]{:S(2)}) collective-permute-start(f32[192,128]{1,0:T(8,128)S(1)} %add.32), channel_id=1, source_target_pairs={{0,32},{16,48},{32,0},{48,16},{64,96},{80,112},{96,64},{112,80},{1... | collective-permute-start | bytes 294920 | tf_op jit(solution)/shard_map/ppermute | solution.py:339
  113.5 4.7 %collective-permute-start.8 = (bf16[512,128]{1,0:T(8,128)(2,1)S(1)}, bf16[512,128]{1,0:T(8,128)(2,1)S(1)}, u32[]{:S(2)}, u32[]{:S(2)}) collective-permute-start(bf16[512,128]{1,0:T(8,128)(2,1)S(1)} %get-tuple-element.36), channel_id=1, source_target_pairs={{0,4},{1,5},{2,6},{3,7},{4,0},{5,1},{6,2},{7,3},{8,12},{9,13},{10,... | collective-permute-start | bytes 393224 | tf_op jit(solution)/shard_map/ppermute | solution.py:339
  118.2 4.5 %collective-permute-start.12 = (f32[192,128]{1,0:T(8,128)S(1)}, f32[192,128]{1,0:T(8,128)S(1)}, u32[]{:S(2)}, u32[]{:S(2)}) collective-permute-start(f32[192,128]{1,0:T(8,128)S(1)} %add.33), channel_id=1, source_target_pairs={{0,64},{16,80},{32,96},{48,112},{64,0},{80,16},{96,32},{112,48},{1... | collective-permute-start | bytes 294920 | tf_op jit(solution)/shard_map/ppermute | solution.py:339
  122.7 4.6 %collective-permute-done.12 = f32[192,128]{1,0:T(8,128)S(1)} collective-permute-done((f32[192,128]{1,0:T(8,128)S(1)}, f32[192,128]{1,0:T(8,128)S(1)}, u32[]{:S(2)}, u32[]{:S(2)}) %collective-permute-start.12) | collective-permute-done | bytes 98336 | tf_op jit(solution)/shard_map/ppermute | solution.py:339
  127.3 6.9 %collective-permute-start.13 = (f32[192,128]{1,0:T(8,128)S(1)}, f32[192,128]{1,0:T(8,128)S(1)}, u32[]{:S(2)}, u32[]{:S(2)}) collective-permute-start(f32[192,128]{1,0:T(8,128)S(1)} %add.34), channel_id=1, source_target_pairs={{0,128},{16,144},{32,160},{48,176},{64,192},{80,208},{96,224},{112... | collective-permute-start | bytes 294920 | tf_op jit(solution)/shard_map/ppermute | solution.py:339
  134.3 4.4 %collective-permute-start.9 = (bf16[512,128]{1,0:T(8,128)(2,1)S(1)}, bf16[512,128]{1,0:T(8,128)(2,1)S(1)}, u32[]{:S(2)}, u32[]{:S(2)}) collective-permute-start(bf16[512,128]{1,0:T(8,128)(2,1)S(1)} %fusion.6), channel_id=1, source_target_pairs={{0,8},{1,9},{2,10},{3,11},{4,12},{5,13},{6,14},{7,15},{8,0},{9,1},... | collective-permute-start | bytes 393224 | tf_op jit(solution)/shard_map/ppermute | solution.py:339
  138.7 0.8 collective-permute-done.13
  139.6 8.2 %collective-permute-start.14 = (f32[192,128]{1,0:T(8,128)S(1)}, f32[192,128]{1,0:T(8,128)S(1)}, u32[]{:S(2)}, u32[]{:S(2)}) collective-permute-start(f32[192,128]{1,0:T(8,128)S(1)} %add.35), channel_id=1, source_target_pairs={{0,256},{16,272},{32,288},{48,304},{64,320},{80,336},{96,352},{112... | collective-permute-start | bytes 294920 | tf_op jit(solution)/shard_map/ppermute | solution.py:339
  147.8 3.7 %collective-permute-done.14 = f32[192,128]{1,0:T(8,128)S(1)} collective-permute-done((f32[192,128]{1,0:T(8,128)S(1)}, f32[192,128]{1,0:T(8,128)S(1)}, u32[]{:S(2)}, u32[]{:S(2)}) %collective-permute-start.14) | collective-permute-done | bytes 98336 | tf_op jit(solution)/shard_map/ppermute | solution.py:339
  151.5 1.9 %collective-permute-start.15 = (f32[192,128]{1,0:T(8,128)S(1)}, f32[192,128]{1,0:T(8,128)S(1)}, u32[]{:S(2)}, u32[]{:S(2)}) collective-permute-start(f32[192,128]{1,0:T(8,128)S(1)} %add.36.keep), channel_id=1, source_target_pairs={{0,16},{16,0},{32,48},{48,32},{64,80},{80,64},{96,112},{112,96},{1... | collective-permute-start | bytes 294920 | tf_op jit(solution)/shard_map/ppermute | solution.py:339
  153.4 0.8 fusion.5
  154.7 1.2 gradients.1
  155.9 0.8 copy.13
  156.7 1.6 finish.1
  (50 shorter events, 3.7 us)
Async XLA Ops:
  0.6 46.5 %copy-start.7 = (bf16[256,128]{1,0:T(8,128)(2,1)S(1)}, bf16[256,128]{1,0:T(8,128)(2,1)}, u32[]{:S(2)}) copy-start(bf16[256,128]{1,0:T(8,128)(2,1)} %cot.3) | copy-start | bytes 196612
  1.6 0.8 copy-start.6
  2.5 0.9 copy-start.10
  3.4 0.7 copy-start.17
  22.2 24.9 %all-to-all-start.1 = ((bf16[16,96,128]{2,1,0:T(8,128)(2,1)}), bf16[16,96,128]{2,1,0:T(8,128)(2,1)S(1)}, u32[]{:S(2)}, u32[]{:S(2)}) async-start(bf16[16,96,128]{2,1,0:T(8,128)(2,1)} %mix.1), calls=%async_computation.1 | async-start | bytes 786432 | tf_op jit(solution)/shard_map/all_to_all | solution.py:354
  28.5 32.9 %collective-permute-start.2 = (bf16[256,128]{1,0:T(8,128)(2,1)S(1)}, bf16[256,128]{1,0:T(8,128)(2,1)S(1)}, u32[]{:S(2)}, u32[]{:S(2)}) collective-permute-start(bf16[256,128]{1,0:T(8,128)(2,1)S(1)} %get-tuple-element.22), channel_id=1, source_target_pairs={{0,12},{1,13},{2,14},{3,15},{4,8},{5,9},{6,10},{7,11},{8,4},{9,5},... | collective-permute-start | bytes 196616 | tf_op jit(solution)/shard_map/ppermute | solution.py:339
  33.7 27.7 %collective-permute-start.1 = (bf16[256,128]{1,0:T(8,128)(2,1)S(1)}, bf16[256,128]{1,0:T(8,128)(2,1)S(1)}, u32[]{:S(2)}, u32[]{:S(2)}) collective-permute-start(bf16[256,128]{1,0:T(8,128)(2,1)S(1)} %get-tuple-element.22), channel_id=1, source_target_pairs={{0,8},{1,9},{2,10},{3,11},{4,12},{5,13},{6,14},{7,15},{8,0},{9,1},... | collective-permute-start | bytes 196616 | tf_op jit(solution)/shard_map/ppermute | solution.py:339
  35.6 25.8 %collective-permute-start = (bf16[256,128]{1,0:T(8,128)(2,1)S(1)}, bf16[256,128]{1,0:T(8,128)(2,1)S(1)}, u32[]{:S(2)}, u32[]{:S(2)}) collective-permute-start(bf16[256,128]{1,0:T(8,128)(2,1)S(1)} %get-tuple-element.22), channel_id=1, source_target_pairs={{0,4},{1,5},{2,6},{3,7},{4,0},{5,1},{6,2},{7,3},{8,12},{9,13},{10,... | collective-permute-start | bytes 196616 | tf_op jit(solution)/shard_map/ppermute | solution.py:339
  38.6 1.6 %copy-start.3 = (s32[512,1024]{1,0:T(8,128)S(1)}, s32[512,1024]{1,0:T(8,128)}, u32[]{:S(2)}) copy-start(s32[512,1024]{1,0:T(8,128)} %codes.1) | copy-start | bytes 6291460
  40.2 1.0 copy-start.4
  41.2 0.8 copy-start.16
  45.1 2.0 %copy-start = (bf16[4,512,1024]{2,1,0:T(8,128)(2,1)}, bf16[4,512,1024]{2,1,0:T(8,128)(2,1)S(1)}, u32[]{:S(2)}) copy-start(bf16[4,512,1024]{2,1,0:T(8,128)(2,1)S(1)} %get-tuple-element.19.weight) | copy-start | bytes 12582916
  47.1 2.2 %copy-start.1 = (bf16[4,512,1024]{2,1,0:T(8,128)(2,1)S(1)}, bf16[4,512,1024]{2,1,0:T(8,128)(2,1)}, u32[]{:S(2)}) copy-start(bf16[4,512,1024]{2,1,0:T(8,128)(2,1)} %copy-done) | copy-start | bytes 12582916
  52.5 0.7 copy-start.8
  53.2 0.6 copy-start.12
  53.8 7.6 %copy-start.14 = (f32[64,128]{1,0:T(8,128)}, f32[64,128]{1,0:T(8,128)S(1)}, u32[]{:S(2)}) copy-start(f32[64,128]{1,0:T(8,128)S(1)} %get-tuple-element.21.down) | copy-start | bytes 98308
  53.8 102.9 %all-to-all-start.2 = ((bf16[16,256,128]{2,1,0:T(8,128)(2,1)}), bf16[16,256,128]{2,1,0:T(8,128)(2,1)S(1)}, u32[]{:S(2)}, u32[]{:S(2)}) async-start(bf16[16,256,128]{2,1,0:T(8,128)(2,1)} %get-tuple-element.20), calls=%async_computation.2 | async-start | bytes 2097152 | tf_op jit(solution)/shard_map/all_to_all | solution.py:356
  61.5 15.8 %collective-permute-start.3 = (bf16[4,256,128]{2,1,0:T(8,128)(2,1)S(1)}, bf16[4,256,128]{2,1,0:T(8,128)(2,1)S(1)}, u32[]{:S(2)}, u32[]{:S(2)}) collective-permute-start(bf16[4,256,128]{2,1,0:T(8,128)(2,1)S(1)} %pad_maximum_fusion.own), channel_id=1, source_target_pairs={{0,1},{1,0},{2,3},{3,2},{4,5},{5,4},{6,7},{7,6},{8,9},{9,8},{10,11... | collective-permute-start | bytes 786440 | tf_op jit(solution)/shard_map/ppermute | solution.py:339
  64.3 20.2 %collective-permute-start.4 = (bf16[4,256,128]{2,1,0:T(8,128)(2,1)S(1)}, bf16[4,256,128]{2,1,0:T(8,128)(2,1)S(1)}, u32[]{:S(2)}, u32[]{:S(2)}) collective-permute-start(bf16[4,256,128]{2,1,0:T(8,128)(2,1)S(1)} %pad_maximum_fusion.own), channel_id=1, source_target_pairs={{0,2},{1,3},{2,0},{3,1},{4,6},{5,7},{6,4},{7,5},{8,10},{9,11},{10,... | collective-permute-start | bytes 786440 | tf_op jit(solution)/shard_map/ppermute | solution.py:339
  66.9 20.1 %collective-permute-start.5 = (bf16[4,256,128]{2,1,0:T(8,128)(2,1)S(1)}, bf16[4,256,128]{2,1,0:T(8,128)(2,1)S(1)}, u32[]{:S(2)}, u32[]{:S(2)}) collective-permute-start(bf16[4,256,128]{2,1,0:T(8,128)(2,1)S(1)} %pad_maximum_fusion.own), channel_id=1, source_target_pairs={{0,3},{1,2},{2,1},{3,0},{4,7},{5,6},{6,5},{7,4},{8,11},{9,10},{10,... | collective-permute-start | bytes 786440 | tf_op jit(solution)/shard_map/ppermute | solution.py:339
  86.9 2.2 %copy-start.2 = (bf16[4,512,1024]{2,1,0:T(8,128)(2,1)S(1)}, bf16[4,512,1024]{2,1,0:T(8,128)(2,1)}, u32[]{:S(2)}) copy-start(bf16[4,512,1024]{2,1,0:T(8,128)(2,1)} %copy-done) | copy-start | bytes 12582916
  89.1 0.9 copy-start.9
  90.0 0.8 copy-start.13
  90.9 56.9 %copy-start.18 = (s32[512]{0:T(512)S(1)}, s32[512]{0:T(512)}, u32[]{:S(2)}) copy-start(s32[512]{0:T(512)} %param.8) | copy-start | bytes 6148
  90.9 65.8 %copy-start.5 = (bf16[64,4096]{1,0:T(8,128)(2,1)S(1)}, bf16[64,4096]{1,0:T(8,128)(2,1)}, u32[]{:S(2)}) copy-start(bf16[64,4096]{1,0:T(8,128)(2,1)} %up.3) | copy-start | bytes 1572868
  94.5 0.6 copy-start.11
  95.1 0.6 copy-start.19
  95.8 60.9 %copy-start.15 = (f32[64,128]{1,0:T(8,128)S(1)}, f32[64,128]{1,0:T(8,128)}, u32[]{:S(2)}) copy-start(f32[64,128]{1,0:T(8,128)} %copy-done.14) | copy-start | bytes 98308
  95.8 7.2 %collective-permute-start.6 = (bf16[512,128]{1,0:T(8,128)(2,1)}, bf16[512,128]{1,0:T(8,128)(2,1)S(1)}, u32[]{:S(2)}, u32[]{:S(2)}) collective-permute-start(bf16[512,128]{1,0:T(8,128)(2,1)} %get-tuple-element.26), channel_id=1, source_target_pairs={{0,1},{1,0},{2,3},{3,2},{4,5},{5,4},{6,7},{7,6},{8,9},{9,8},{10,11... | collective-permute-start | bytes 393224 | tf_op jit(solution)/shard_map/ppermute | solution.py:339
  103.0 10.4 %collective-permute-start.7 = (bf16[512,128]{1,0:T(8,128)(2,1)S(1)}, bf16[512,128]{1,0:T(8,128)(2,1)S(1)}, u32[]{:S(2)}, u32[]{:S(2)}) collective-permute-start(bf16[512,128]{1,0:T(8,128)(2,1)S(1)} %fusion.7), channel_id=1, source_target_pairs={{0,2},{1,3},{2,0},{3,1},{4,6},{5,7},{6,4},{7,5},{8,10},{9,11},{10,... | collective-permute-start | bytes 393224 | tf_op jit(solution)/shard_map/ppermute | solution.py:339
  105.6 3.4 %collective-permute-start.10 = (f32[192,128]{1,0:T(8,128)}, f32[192,128]{1,0:T(8,128)S(1)}, u32[]{:S(2)}, u32[]{:S(2)}) collective-permute-start(f32[192,128]{1,0:T(8,128)} %copy-done.19), channel_id=1, source_target_pairs={{0,16},{16,0},{32,48},{48,32},{64,80},{80,64},{96,112},{112,96},{1... | collective-permute-start | bytes 294920 | tf_op jit(solution)/shard_map/ppermute | solution.py:339
  109.9 8.3 %collective-permute-start.11 = (f32[192,128]{1,0:T(8,128)S(1)}, f32[192,128]{1,0:T(8,128)S(1)}, u32[]{:S(2)}, u32[]{:S(2)}) collective-permute-start(f32[192,128]{1,0:T(8,128)S(1)} %add.32), channel_id=1, source_target_pairs={{0,32},{16,48},{32,0},{48,16},{64,96},{80,112},{96,64},{112,80},{1... | collective-permute-start | bytes 294920 | tf_op jit(solution)/shard_map/ppermute | solution.py:339
  113.5 20.8 %collective-permute-start.8 = (bf16[512,128]{1,0:T(8,128)(2,1)S(1)}, bf16[512,128]{1,0:T(8,128)(2,1)S(1)}, u32[]{:S(2)}, u32[]{:S(2)}) collective-permute-start(bf16[512,128]{1,0:T(8,128)(2,1)S(1)} %get-tuple-element.36), channel_id=1, source_target_pairs={{0,4},{1,5},{2,6},{3,7},{4,0},{5,1},{6,2},{7,3},{8,12},{9,13},{10,... | collective-permute-start | bytes 393224 | tf_op jit(solution)/shard_map/ppermute | solution.py:339
  118.2 9.1 %collective-permute-start.12 = (f32[192,128]{1,0:T(8,128)S(1)}, f32[192,128]{1,0:T(8,128)S(1)}, u32[]{:S(2)}, u32[]{:S(2)}) collective-permute-start(f32[192,128]{1,0:T(8,128)S(1)} %add.33), channel_id=1, source_target_pairs={{0,64},{16,80},{32,96},{48,112},{64,0},{80,16},{96,32},{112,48},{1... | collective-permute-start | bytes 294920 | tf_op jit(solution)/shard_map/ppermute | solution.py:339
  127.3 12.3 %collective-permute-start.13 = (f32[192,128]{1,0:T(8,128)S(1)}, f32[192,128]{1,0:T(8,128)S(1)}, u32[]{:S(2)}, u32[]{:S(2)}) collective-permute-start(f32[192,128]{1,0:T(8,128)S(1)} %add.34), channel_id=1, source_target_pairs={{0,128},{16,144},{32,160},{48,176},{64,192},{80,208},{96,224},{112... | collective-permute-start | bytes 294920 | tf_op jit(solution)/shard_map/ppermute | solution.py:339
  134.3 19.1 %collective-permute-start.9 = (bf16[512,128]{1,0:T(8,128)(2,1)S(1)}, bf16[512,128]{1,0:T(8,128)(2,1)S(1)}, u32[]{:S(2)}, u32[]{:S(2)}) collective-permute-start(bf16[512,128]{1,0:T(8,128)(2,1)S(1)} %fusion.6), channel_id=1, source_target_pairs={{0,8},{1,9},{2,10},{3,11},{4,12},{5,13},{6,14},{7,15},{8,0},{9,1},... | collective-permute-start | bytes 393224 | tf_op jit(solution)/shard_map/ppermute | solution.py:339
  139.6 11.9 %collective-permute-start.14 = (f32[192,128]{1,0:T(8,128)S(1)}, f32[192,128]{1,0:T(8,128)S(1)}, u32[]{:S(2)}, u32[]{:S(2)}) collective-permute-start(f32[192,128]{1,0:T(8,128)S(1)} %add.35), channel_id=1, source_target_pairs={{0,256},{16,272},{32,288},{48,304},{64,320},{80,336},{96,352},{112... | collective-permute-start | bytes 294920 | tf_op jit(solution)/shard_map/ppermute | solution.py:339
  151.5 3.2 %collective-permute-start.15 = (f32[192,128]{1,0:T(8,128)S(1)}, f32[192,128]{1,0:T(8,128)S(1)}, u32[]{:S(2)}, u32[]{:S(2)}) collective-permute-start(f32[192,128]{1,0:T(8,128)S(1)} %add.36.keep), channel_id=1, source_target_pairs={{0,16},{16,0},{32,48},{48,32},{64,80},{80,64},{96,112},{112,96},{1... | collective-permute-start | bytes 294920 | tf_op jit(solution)/shard_map/ppermute | solution.py:339

commit v2 on v0

v2 whole, which is shorter than its diff:
```python
import jax
import jax.numpy as jnp
from jax import lax
from jax.experimental import pallas as pl
from jax.experimental.pallas import tpu as pltpu
from jax.sharding import PartitionSpec as P

HEADS = 64
GROUP = 128
RANK = 64
NT = 16
F = 512
O = 256
C = 1024
T = 128
ADAPTER_SCALE = 0.5
F32 = jnp.float32
BF16 = jnp.bfloat16
PARAMS = pltpu.CompilerParams(vmem_limit_bytes=24 * 1024 * 1024)
VMEM = pl.BlockSpec(memory_space=pltpu.VMEM)
SMEM = pl.BlockSpec(memory_space=pltpu.SMEM)
HBM = pl.BlockSpec(memory_space=pltpu.HBM)
DMA = pltpu.SemaphoreType.DMA


def in_hbm(*arrays):
    return [pltpu.with_memory_space_constraint(a, pltpu.HBM) for a in arrays]


def dot(a, b):
    return jnp.dot(a, b, preferred_element_type=F32)


def dot_00(a, b):
    return lax.dot_general(a, b, (((0,), (0,)), ((), ())), preferred_element_type=F32)


def dot_11(a, b):
    return lax.dot_general(a, b, (((1,), (1,)), ((), ())), preferred_element_type=F32)


def split(a):
    high = a.astype(BF16)
    return high, (a - high.astype(F32)).astype(BF16)


def butterfly(v, bits):
    n = v.shape[0]
    rest = v.shape[1:]
    for bit in range(bits):
        w = v.reshape((n >> (bit + 1), 2, 1 << bit) + rest)
        low, high = w[:, 0], w[:, 1]
        v = jnp.stack([low + high, low - high], axis=1).reshape((n,) + rest)
    return v


def iota2(shape, dim):
    return lax.broadcasted_iota(jnp.int32, shape, dim)


def weights_kernel(
    codes_hbm, scales_hbm, up_hbm, weight_out, weight_t_out, up_out,
    codes, scales, up, scales_apart, weight, weight_t, up_apart, sems, out_sems,
):
    copy_scales = pltpu.make_async_copy(scales_hbm, scales, sems.at[4])
    copy_up = pltpu.make_async_copy(up_hbm, up, sems.at[5])
    copies = []
    for g in range(4):
        rows = slice(GROUP * g, GROUP * (g + 1))
        copies.append(pltpu.make_async_copy(codes_hbm.at[rows], codes.at[rows], sems.at[g]))
    copy_scales.start()
    copy_up.start()
    for copy in copies:
        copy.start()
    row, col = iota2((512, 512), 0), iota2((512, 512), 1)
    apart = jnp.where(row == 4 * (col & 127) + (col >> 7), 1.0, 0.0).astype(BF16)
    copy_scales.wait()
    copy_up.wait()
    for block in range(8):
        lanes = slice(512 * block, 512 * (block + 1))
        s = dot(scales[:, lanes], apart)
        u = dot(up[:, lanes], apart).astype(BF16)
        for k in range(4):
            to = slice(128 * block, 128 * (block + 1))
            scales_apart[k, :, to] = s[:, 128 * k : 128 * (k + 1)]
            up_apart[k, :, to] = u[:, 128 * k : 128 * (k + 1)]
    sends = [pltpu.make_async_copy(up_apart, up_out, out_sems.at[5])]
    sends[0].start()
    for g in range(4):
        copies[g].wait()
        rows = slice(GROUP * g, GROUP * (g + 1))
        for k in range(4):
            nibble = ((codes[rows, :] >> (4 * k)) & 15) - 8
            part = nibble.astype(F32) * scales_apart[k, g : g + 1, :]
            weight[k, rows, :] = part.astype(BF16)
            weight_t[k, :, rows] = part.T.astype(BF16)
        sends.append(
            pltpu.make_async_copy(weight.at[:, rows], weight_out.at[:, rows], out_sems.at[g])
        )
        sends[g + 1].start()
    sends.append(pltpu.make_async_copy(weight_t, weight_t_out, out_sems.at[4]))
    sends[5].start()
    for send in sends:
        send.wait()


def make_weights(codes, scales, up):
    return pl.pallas_call(
        weights_kernel,
        in_specs=[HBM] * 3,
        out_specs=[HBM] * 3,
        out_shape=[
            pltpu.HBM((4, F, C), BF16),
            pltpu.HBM((4, C, F), BF16),
            pltpu.HBM((4, RANK, C), BF16),
        ],
        scratch_shapes=[
            pltpu.VMEM((F, C), jnp.int32),
            pltpu.VMEM((F // GROUP, 4 * C), BF16),
            pltpu.VMEM((RANK, 4 * C), BF16),
            pltpu.VMEM((4, F // GROUP, C), F32),
            pltpu.VMEM((4, F, C), BF16),
            pltpu.VMEM((4, C, F), BF16),
            pltpu.VMEM((4, RANK, C), BF16),
            DMA((6,)),
            DMA((6,)),
        ],
        compiler_params=PARAMS,
        cost_estimate=pl.CostEstimate(flops=20_000_000, bytes_accessed=20_000_000, transcendentals=0),
        name="weights",
    )(*in_hbm(codes, scales, up))


def pack_kernel(
    activ_hbm, flags_hbm, down_hbm, cot_hbm, sent,
    activ, flags, down_map, cot, first, own, sems, out_sems,
):
    pairs = ((activ_hbm, activ), (flags_hbm, flags), (down_hbm, down_map), (cot_hbm, cot))
    copies = [pltpu.make_async_copy(a, b, sems.at[n]) for n, (a, b) in enumerate(pairs)]
    for copy in copies:
        copy.start()
    row, col = iota2((O, O), 0), iota2((O, O), 1)
    apart = jnp.where(col == 4 * (row & 63) + (row >> 6), 1.0, 0.0).astype(BF16)
    eye = iota2((GROUP, GROUP), 0) == iota2((GROUP, GROUP), 1)
    lane, rank = iota2((RANK, 2 * RANK), 1), iota2((RANK, 2 * RANK), 0)
    left = jnp.where(lane == rank, 1.0, 0.0).astype(BF16)
    right = jnp.where(lane == rank + RANK, 1.0, 0.0).astype(BF16)
    copies[3].wait()
    own[...] = dot(apart, cot[...]).astype(BF16)
    sends = []
    for q in range(NT):
        sends.append(pltpu.make_async_copy(own, sent.at[q, 48:304], out_sems.at[q]))
        sends[q].start()
    for copy in copies[:3]:
        copy.wait()
    parts = []
    for h in range(4):
        sign = (2 * flags[h : h + 1, :] - 1).astype(F32)
        diagonal = jnp.where(eye, sign, 0.0).astype(BF16)
        parts.append(dot(diagonal, activ[GROUP * h : GROUP * (h + 1), :]).reshape(NT, 8, T))
    for h in (0, 2):
        even = down_map[:, GROUP * h : GROUP * (h + 1)]
        odd = down_map[:, GROUP * (h + 1) : GROUP * (h + 2)]
        parts.append((dot_00(even, left) + dot_00(odd, right)).reshape(NT, 8, T))
    first[...] = jnp.concatenate(parts, axis=1).astype(BF16)
    sends.append(pltpu.make_async_copy(first, sent.at[:, 0:48], out_sems.at[NT]))
    sends[NT].start()
    for send in sends:
        send.wait()


def pack(activ, flags, down_t, cot):
    return pl.pallas_call(
        pack_kernel,
        in_specs=[HBM] * 4,
        out_specs=HBM,
        out_shape=pltpu.HBM((NT, 304, T), BF16),
        scratch_shapes=[
            pltpu.VMEM((F, T), BF16),
            pltpu.VMEM((4, GROUP), jnp.int32),
            pltpu.VMEM((RANK, F), BF16),
            pltpu.VMEM((O, T), BF16),
            pltpu.VMEM((NT, 48, T), BF16),
            pltpu.VMEM((O, T), BF16),
            DMA((4,)),
            DMA((NT + 1,)),
        ],
        compiler_params=PARAMS,
        cost_estimate=pl.CostEstimate(flops=60_000_000, bytes_accessed=2_000_000, transcendentals=0),
        name="pack",
    )(*in_hbm(activ, flags, down_t, cot))


def turn_kernel(
    got, weight_hbm, up_hbm, down_hbm, sent, back_out, cot, weight, up_apart, down_t, sems
):
    copy_up = pltpu.make_async_copy(up_hbm, up_apart, sems.at[4])
    copy_down = pltpu.make_async_copy(down_hbm, down_t, sems.at[5])
    copies = []
    for h in range(4):
        rows = slice(GROUP * h, GROUP * (h + 1))
        copies.append(
            pltpu.make_async_copy(weight_hbm.at[:, rows], weight.at[:, rows], sems.at[h])
        )
    copy_up.start()
    copy_down.start()
    for copy in copies:
        copy.start()
    v = got[:, 0:32, :].astype(F32).reshape(HEADS, 8, T)
    v = butterfly(v, 6) * 0.125
    sent[:, 0:32, :] = v.reshape(NT, 32, T).astype(BF16)
    pairs = v.reshape(NT, 2, 2, 8, T)
    even = pairs[:, :, 0].reshape(256, T).astype(BF16)
    odd = pairs[:, :, 1].reshape(256, T).astype(BF16)
    maps = got[:, 32:48, :].reshape(256, 2 * RANK)
    down = dot_00(maps, even)[0:RANK] + dot_00(maps, odd)[RANK : 2 * RANK]
    down = down.astype(BF16)
    for q in range(NT):
        sent[q, 64:128, :] = down
        for k in range(4):
            cot[k, 64 * q : 64 * (q + 1), :] = got[q, 48 + 64 * k : 112 + 64 * k, :]
    copy_up.wait()
    copy_down.wait()
    back = jnp.zeros((RANK, T), F32)
    for k in range(4):
        back = back + dot(up_apart[k], cot[k])
    back_out[...] = back
    high, low = split(back)
    for h in range(4):
        rows = slice(GROUP * h, GROUP * (h + 1))
        copies[h].wait()
        maps = down_t[:, rows]
        g = ADAPTER_SCALE * (dot_00(maps, high) + dot_00(maps, low))
        for k in range(4):
            g = g + dot(weight[k, rows, :], cot[k])
        cot_rows = g.reshape(NT, 8, T)
        if h % 2 == 0:
            first = cot_rows
        else:
            both = jnp.concatenate([first, cot_rows], axis=1)
            sent[:, 24 + 8 * h : 40 + 8 * h, :] = both.astype(BF16)


def turn(got, weight, up_apart, down_t):
    return pl.pallas_call(
        turn_kernel,
        in_specs=[VMEM] + [HBM] * 3,
        out_specs=[VMEM] * 2,
        out_shape=[
            jax.ShapeDtypeStruct((NT, 128, T), BF16),
            jax.ShapeDtypeStruct((RANK, T), F32),
        ],
        scratch_shapes=[
            pltpu.VMEM((4, C, T), BF16),
            pltpu.VMEM((4, F, C), BF16),
            pltpu.VMEM((4, RANK, C), BF16),
            pltpu.VMEM((RANK, F), BF16),
            DMA((6,)),
        ],
        compiler_params=PARAMS,
        cost_estimate=pl.CostEstimate(flops=600_000_000, bytes_accessed=7_000_000, transcendentals=0),
        name="turn",
    )(got, *in_hbm(weight, up_apart, down_t))


def project_kernel(
    got, weight_hbm, back, cot, sent, down, sums, mixed, weight_t, sems
):
    copies = [pltpu.make_async_copy(weight_hbm.at[k], weight_t.at[k], sems.at[k]) for k in range(4)]
    for copy in copies:
        copy.start()
    v = got[:, 0:32, :].astype(F32).reshape(NT, 4, 8, T)
    for h in range(4):
        mixed[GROUP * h : GROUP * (h + 1), :] = v[:, h].reshape(GROUP, T).astype(BF16)
    g = got[:, 32:64, :].astype(F32).reshape(HEADS, 8, T)
    g = butterfly(g, 6) * 0.125
    sent[:, 256:288, :] = g.reshape(NT, 32, T).astype(BF16)
    total = jnp.sum(got[:, 64:128, :].astype(F32), axis=0)
    down[...] = total
    high, low = split(total)
    back_high, back_low = split(back[...])
    for h in range(4):
        rows = slice(GROUP * h, GROUP * (h + 1))
        product = dot_11(back_high, mixed[rows, :]) + dot_11(back_low, mixed[rows, :])
        sums[RANK * h : RANK * (h + 1), :] = product
    for half in range(2):
        c = cot[GROUP * half : GROUP * (half + 1), :]
        sums[256 + RANK * half : 320 + RANK * half, :] = dot_11(high, c) + dot_11(low, c)
    for k in range(4):
        copies[k].wait()
        share = dot(weight_t[k], mixed[...])
        sent[:, 64 * k : 64 * (k + 1), :] = share.reshape(NT, 64, T).astype(BF16)


def project(got, weight_t, back, cot):
    return pl.pallas_call(
        project_kernel,
        in_specs=[VMEM, HBM, VMEM, VMEM],
        out_specs=[VMEM] * 3,
        out_shape=[
            jax.ShapeDtypeStruct((NT, 288, T), BF16),
            jax.ShapeDtypeStruct((RANK, T), F32),
            jax.ShapeDtypeStruct((384, T), F32),
        ],
        scratch_shapes=[
            pltpu.VMEM((F, T), BF16),
            pltpu.VMEM((4, C, F), BF16),
            DMA((4,)),
        ],
        compiler_params=PARAMS,
        cost_estimate=pl.CostEstimate(flops=540_000_000, bytes_accessed=6_000_000, transcendentals=0),
        name="project",
    )(got, *in_hbm(weight_t), back, cot)


def finish_kernel(place, got, up, down, flags, out, input_gradient, own, sem):
    lanes = pl.ds(pl.multiple_of(place[0] * O, O), O)
    copy = pltpu.make_async_copy(up.at[:, lanes], own, sem)
    copy.start()
    total = jnp.sum(got[:, 0:256, :].astype(F32), axis=0)
    row, col = iota2((O, O), 0), iota2((O, O), 1)
    together = jnp.where(row == 4 * (col & 63) + (col >> 6), 1.0, 0.0).astype(BF16)
    high, low = split(total)
    down_high, down_low = split(down[...])
    copy.wait()
    adapter = dot_00(own[...], down_high) + dot_00(own[...], down_low)
    out[...] = (dot(together, high) + dot(together, low) + ADAPTER_SCALE * adapter).astype(BF16)
    eye = iota2((GROUP, GROUP), 0) == iota2((GROUP, GROUP), 1)
    g = got[:, 256:288, :].astype(F32).reshape(NT, 4, 8, T)
    for h in range(4):
        sign = (2 * flags[h : h + 1, :] - 1).astype(F32)
        diagonal = jnp.where(eye, sign, 0.0).astype(BF16)
        part = g[:, h].reshape(GROUP, T).astype(BF16)
        input_gradient[GROUP * h : GROUP * (h + 1), :] = dot(diagonal, part).astype(BF16)


def finish(place, got, up, down, flags):
    return pl.pallas_call(
        finish_kernel,
        in_specs=[SMEM, VMEM, HBM, VMEM, VMEM],
        out_specs=[VMEM] * 2,
        out_shape=[
            jax.ShapeDtypeStruct((O, T), BF16),
            jax.ShapeDtypeStruct((F, T), BF16),
        ],
        scratch_shapes=[pltpu.VMEM((RANK, O), BF16), DMA(())],
        compiler_params=PARAMS,
        cost_estimate=pl.CostEstimate(flops=40_000_000, bytes_accessed=1_700_000, transcendentals=0),
        name="finish",
    )(place, got, *in_hbm(up), down, flags)


def gradients_kernel(sums, down_gradient, up_gradient):
    multiplier = ADAPTER_SCALE / 64.0
    for h in range(4):
        lanes = slice(GROUP * h, GROUP * (h + 1))
        down_gradient[:, lanes] = sums[RANK * h : RANK * (h + 1), :] * multiplier
    for half in range(2):
        lanes = slice(GROUP * half, GROUP * (half + 1))
        up_gradient[:, lanes] = sums[256 + RANK * half : 320 + RANK * half, :] * multiplier


def gradients(sums):
    return pl.pallas_call(
        gradients_kernel,
        in_specs=[VMEM],
        out_specs=[VMEM, VMEM],
        out_shape=[
            jax.ShapeDtypeStruct((RANK, F), F32),
            jax.ShapeDtypeStruct((RANK, O), F32),
        ],
        compiler_params=PARAMS,
        cost_estimate=pl.CostEstimate(flops=100_000, bytes_accessed=500_000, transcendentals=0),
        name="gradients",
    )(sums)


def by(value, axis, mask):
    pairs = [(source, source ^ mask) for source in range(lax.axis_size(axis))]
    return lax.ppermute(value, axis, pairs)


def exchange(value):
    return lax.all_to_all(value, "tensor", 0, 0, tiled=True)


def both_cores(value):
    groups = [[device, device + 1] for device in range(0, lax.axis_size("dp"), 2)]
    return lax.all_gather(value, "dp", axis=0, tiled=True, axis_index_groups=groups)


def add_partner(value, mask):
    value = value.astype(BF16)
    return value.astype(F32) + by(value, "dp", mask).astype(F32)


def local(activ, flags, codes, scales, down_map, up, cot):
    core = lax.axis_index("dp") & 1
    place = jnp.stack([lax.axis_index("tensor")]).astype(jnp.int32)
    flags = flags.reshape(4, GROUP)
    down_t = down_map.T
    got = exchange(pack(activ, flags, down_t, cot))
    weight, weight_t, up_apart = make_weights(codes, scales, up)
    sent, back = turn(got, weight, up_apart, down_t)
    sent, down, sums = project(exchange(sent), weight_t, back, cot)
    got = exchange(sent)
    two = both_cores(sums)
    half = lax.dynamic_slice_in_dim(two[:384] + two[384:], core * 192, 192)
    for mask in (2, 4, 12, 16):
        half = add_partner(half, mask)
    out, input_gradient = finish(place, got, up, down, flags)
    half, out, input_gradient = lax.optimization_barrier((half, out, input_gradient))
    down_gradient, up_gradient = gradients(both_cores(half))
    return out, input_gradient, down_gradient.T, up_gradient


def solution(mesh):
    in_specs = (
        P("tensor", "dp"),
        P("tensor"),
        P("tensor", None),
        P("tensor", None),
        P("tensor", None),
        P(),
        P("tensor", "dp"),
    )
    out_specs = (P("tensor", "dp"), P("tensor", "dp"), P("tensor", None), P(None, "tensor"))
    return jax.shard_map(local, mesh=mesh, in_specs=in_specs, out_specs=out_specs, check_vma=False)
```

time: 751 us -> 115 us (0.15)
  waiting for transfers between devices: 623 us -> 29.6 us
  local copies, waits for them, and re-layouts: 45 us -> 0.03 us
  blocking collectives: 0 us -> 24 us
  other arithmetic: 21.7 us -> 0.08 us
  Pallas kernels: 0 us -> 20.6 us
  between operations: 14.1 us -> 0.76 us
  matrix products: 12.9 us -> 0 us
    psum x2 -> x0, waiting for transfers between devices: 480 us -> none  [the longest x1 337 us: local(): lax.psum((down_gradient_piece, up_gradient_piece), 'dp')]
    reduce_scatter x1 -> x0, waiting for transfers between devices: 65.3 us -> none  [local(): lax.psum_scatter(jnp.einsum('fo,ft->ot', w_cols, rotated_input, preferred...]
    all_gather x1 -> x0, waiting for transfers between devices: 49 us -> none  [local(): lax.all_gather(cotangent, 'tensor', axis=0, tiled=True)]
    shift_right_arithmetic x5 -> x0, local copies, waits for them, and re-layouts: 27.3 us -> none  [dequant(): nibbles = codes[:, :, None] >> offsets & 15]
    pallas_call x0 -> x6, Pallas kernels: none -> 20.6 us  [the longest x1 7.01 us: make_weights(): pl.pallas_call(weights_kernel, in_specs=[HBM] * 3, out_specs=[HBM] * 3, o...]
    all_to_all x0 -> x2, waiting for transfers between devices: none -> 20.4 us  [exchange(): return lax.all_to_all(value, 'tensor', 0, 0, tiled=True)]
    ppermute x8 -> x4, waiting for transfers between devices: 29.3 us -> 9.15 us  [by(): return lax.ppermute(value, axis, pairs)]
    all_to_all x0 -> x1, blocking collectives: none -> 20 us  [exchange(): return lax.all_to_all(value, 'tensor', 0, 0, tiled=True)]
  transfers between devices with their start and end apart: 12 -> 6, of which waited for: 9 -> 5; matrix products, arithmetic and copies ran while one was open for 9% -> 0% of each run, Pallas kernels for 0% -> 6%
where the time goes in v2:
time: 115 us; the launch traced here: 114 us
  starting transfers between devices  39 us (34%)
  waiting for transfers between devices  29.6 us (26%)
  blocking collectives  24 us (21%)
  Pallas kernels  20.6 us (18%)
    ppermute x4, starting transfers between devices, by(): return lax.ppermute(value, axis, pairs)  22.3 us
    all_to_all x2, waiting for transfers between devices, exchange(): return lax.all_to_all(value, 'tensor', 0, 0, tiled=True)  20.4 us
    all_to_all x1, blocking collectives, exchange(): return lax.all_to_all(value, 'tensor', 0, 0, tiled=True)  20 us
    all_to_all x2, starting transfers between devices, exchange(): return lax.all_to_all(value, 'tensor', 0, 0, tiled=True)  16.6 us
    ppermute x4, waiting for transfers between devices, by(): return lax.ppermute(value, axis, pairs)  9.15 us
    pallas_call x1, Pallas kernels, make_weights(): pl.pallas_call(weights_kernel, in_specs=[HBM] * 3, out_specs=[HBM] * 3, o...  7.01 us
    pallas_call x1, Pallas kernels, project(): pl.pallas_call(project_kernel, in_specs=[VMEM, HBM, VMEM, VMEM], out_spec...  5.29 us
    all_gather x2, blocking collectives, both_cores(): lax.all_gather(value, 'dp', axis=0, tiled=True, axis_index_groups=groups)  4.04 us
  transfers between devices with their start and end apart: 6, of which 5 were waited for; matrix products, arithmetic and copies ran while one was open for 0% of the time, Pallas kernels for 6%

profile of v2, /device:TPU:6, one launch (start us, length us, event | category | flops | bytes accessed | tf_op | source)
XLA Modules:
  0.0 114.1 jit_solution(1147192852029957276)
XLA Ops:
  0.6 2.5 %pack.1 = bf16[16,304,128]{2,1,0:T(8,128)(2,1)} custom-call(bf16[512,128]{1,0:T(8,128)(2,1)} %activ_hbm.1, s32[4,128]{1,0:T(4,128)} %bitcast.4, bf16[64,512]{1,0:T(8,128)(2,1)} %bitcast.6, bf16[256,128]{1,0:T(8,128)(2,1)} %cot.1), custom_call_target="tpu_custom_call" | custom-call | flops 60000000 | bytes 2000000 | tf_op jit(solution)/shard_map/pack/pallas_call | solution.py:173
  3.1 10.2 %all-to-all-start = ((bf16[16,304,128]{2,1,0:T(8,128)(2,1)}), bf16[16,304,128]{2,1,0:T(8,128)(2,1)S(1)}, u32[]{:S(2)}, u32[]{:S(2)}) async-start(bf16[16,304,128]{2,1,0:T(8,128)(2,1)} %pack.1), calls=%async_computation | async-start | bytes 2490368 | tf_op jit(solution)/shard_map/all_to_all | solution.py:384
  13.3 7.0 %weights.1 = (bf16[4,512,1024]{2,1,0:T(8,128)(2,1)}, bf16[4,1024,512]{2,1,0:T(8,128)(2,1)}, bf16[4,64,1024]{2,1,0:T(8,128)(2,1)}) custom-call(s32[512,1024]{1,0:T(8,128)} %codes_hbm.1, bf16[4,4096]{1,0:T(4,128)(2,1)} %scales_hbm.1, bf16[64,4096]{1,0:T(8,128)(2,1)} %up.1), custom_call_target="tpu_custom_call" | custom-call | flops 20000000 | bytes 20000000 | tf_op jit(solution)/shard_map/weights/pallas_call | solution.py:108
  20.3 20.4 %all-to-all-done.got = bf16[16,304,128]{2,1,0:T(8,128)(2,1)S(1)} async-done(((bf16[16,304,128]{2,1,0:T(8,128)(2,1)}), bf16[16,304,128]{2,1,0:T(8,128)(2,1)S(1)}, u32[]{:S(2)}, u32[]{:S(2)}) %all-to-all-start) | async-done | bytes 1245216 | tf_op jit(solution)/shard_map/all_to_all | solution.py:384
  40.8 0.0 copy-start
  40.8 3.4 %turn.1 = (bf16[16,128,128]{2,1,0:T(8,128)(2,1)S(1)}, f32[64,128]{1,0:T(8,128)S(1)}) custom-call(bf16[16,304,128]{2,1,0:T(8,128)(2,1)S(1)} %all-to-all-done.got, bf16[4,512,1024]{2,1,0:T(8,128)(2,1)} %get-tuple-element.19.weight_hbm, bf16[4,64,1024]{2,1,0:T(8,128)(2,1)} %get-tuple-element.20.up_hbm, bf16[64,512]{1,0:T(8,128)(2,1)} %bitcast.7), custom_call_target="tpu_custom_call" | custom-call | flops 600000000 | bytes 7000000 | tf_op jit(solution)/shard_map/turn/pallas_call | solution.py:245
  44.2 20.0 %all_to_all.15.got = bf16[16,128,128]{2,1,0:T(8,128)(2,1)S(1)} all-to-all(bf16[16,128,128]{2,1,0:T(8,128)(2,1)S(1)} %get-tuple-element.21), channel_id=1, replica_groups=mesh['dp'=32,'tensor'=16] {'tensor'}, dimensions={0} | all-to-all | bytes 1048576 | tf_op jit(solution)/shard_map/all_to_all | solution.py:384
  64.2 0.0 copy-done
  64.2 5.3 %project.1 = (bf16[16,288,128]{2,1,0:T(8,128)(2,1)}, f32[64,128]{1,0:T(8,128)S(1)}, f32[384,128]{1,0:T(8,128)S(1)}) custom-call(bf16[16,128,128]{2,1,0:T(8,128)(2,1)S(1)} %all_to_all.15.got, bf16[4,1024,512]{2,1,0:T(8,128)(2,1)} %get-tuple-element.22.weight_hbm, f32[64,128]{1,0:T(8,128)S(1)} %get-tuple-element.23.back, bf16[256,128]{1,0:T(8,128)(2,1)S(1)} %copy-done), custom_call_target="tpu_custom_call" | custom-call | flops 540000000 | bytes 6000000 | tf_op jit(solution)/shard_map/project/pallas_call | solution.py:296
  69.5 6.4 %all-to-all-start.2 = ((bf16[16,288,128]{2,1,0:T(8,128)(2,1)}), bf16[16,288,128]{2,1,0:T(8,128)(2,1)S(1)}, u32[]{:S(2)}, u32[]{:S(2)}) async-start(bf16[16,288,128]{2,1,0:T(8,128)(2,1)} %get-tuple-element.25), calls=%async_computation.2 | async-start | bytes 2359296 | tf_op jit(solution)/shard_map/all_to_all | solution.py:384
  75.9 0.0 copy-start.1
  75.9 2.1 %all_gather.6 = f32[768,128]{1,0:T(8,128)S(1)} all-gather(f32[384,128]{1,0:T(8,128)S(1)} %get-tuple-element.24), channel_id=1, replica_groups={{0,16},{32,48},{64,80},{96,112},{128,144},{160,176},{192,208},{224,240}..., dimensions={0}, use_global_device_ids=true | all-gather | bytes 589824 | tf_op jit(solution)/shard_map/all_gather | solution.py:389
  78.1 3.5 %collective-permute-start = (bf16[192,128]{1,0:T(8,128)(2,1)S(1)}, bf16[192,128]{1,0:T(8,128)(2,1)S(1)}, u32[]{:S(2)}, u32[]{:S(2)}) collective-permute-start(bf16[192,128]{1,0:T(8,128)(2,1)S(1)} %fusion), channel_id=1, source_target_pairs={{0,32},{16,48},{32,0},{48,16},{64,96},{80,112},{96,64},{112,80},{1... | collective-permute-start | bytes 147464 | tf_op jit(solution)/shard_map/ppermute | solution.py:380
  81.5 2.5 %collective-permute-done = bf16[192,128]{1,0:T(8,128)(2,1)S(1)} collective-permute-done((bf16[192,128]{1,0:T(8,128)(2,1)S(1)}, bf16[192,128]{1,0:T(8,128)(2,1)S(1)}, u32[]{:S(2)}, u32[]{:S(2)}) %collective-permute-start) | collective-permute-done | bytes 49184 | tf_op jit(solution)/shard_map/ppermute | solution.py:380
  84.1 4.5 %collective-permute-start.1 = (bf16[192,128]{1,0:T(8,128)(2,1)S(1)}, bf16[192,128]{1,0:T(8,128)(2,1)S(1)}, u32[]{:S(2)}, u32[]{:S(2)}) collective-permute-start(bf16[192,128]{1,0:T(8,128)(2,1)S(1)} %add_convert_fusion.2), channel_id=1, source_target_pairs={{0,64},{16,80},{32,96},{48,112},{64,0},{80,16},{96,32},{112,48},{1... | collective-permute-start | bytes 147464 | tf_op jit(solution)/shard_map/ppermute | solution.py:380
  88.6 2.4 %collective-permute-done.1 = bf16[192,128]{1,0:T(8,128)(2,1)S(1)} collective-permute-done((bf16[192,128]{1,0:T(8,128)(2,1)S(1)}, bf16[192,128]{1,0:T(8,128)(2,1)S(1)}, u32[]{:S(2)}, u32[]{:S(2)}) %collective-permute-start.1) | collective-permute-done | bytes 49184 | tf_op jit(solution)/shard_map/ppermute | solution.py:380
  91.0 6.2 %collective-permute-start.2 = (bf16[192,128]{1,0:T(8,128)(2,1)S(1)}, bf16[192,128]{1,0:T(8,128)(2,1)S(1)}, u32[]{:S(2)}, u32[]{:S(2)}) collective-permute-start(bf16[192,128]{1,0:T(8,128)(2,1)S(1)} %add_convert_fusion.1), channel_id=1, source_target_pairs={{0,192},{16,208},{32,224},{48,240},{64,128},{80,144},{96,160},{112... | collective-permute-start | bytes 147464 | tf_op jit(solution)/shard_map/ppermute | solution.py:380
  97.1 2.2 %collective-permute-done.2 = bf16[192,128]{1,0:T(8,128)(2,1)S(1)} collective-permute-done((bf16[192,128]{1,0:T(8,128)(2,1)S(1)}, bf16[192,128]{1,0:T(8,128)(2,1)S(1)}, u32[]{:S(2)}, u32[]{:S(2)}) %collective-permute-start.2) | collective-permute-done | bytes 49184 | tf_op jit(solution)/shard_map/ppermute | solution.py:380
  99.3 8.2 %collective-permute-start.3 = (bf16[192,128]{1,0:T(8,128)(2,1)S(1)}, bf16[192,128]{1,0:T(8,128)(2,1)S(1)}, u32[]{:S(2)}, u32[]{:S(2)}) collective-permute-start(bf16[192,128]{1,0:T(8,128)(2,1)S(1)} %add_convert_fusion), channel_id=1, source_target_pairs={{0,256},{16,272},{32,288},{48,304},{64,320},{80,336},{96,352},{112... | collective-permute-start | bytes 147464 | tf_op jit(solution)/shard_map/ppermute | solution.py:380
  107.5 2.1 %collective-permute-done.3 = bf16[192,128]{1,0:T(8,128)(2,1)S(1)} collective-permute-done((bf16[192,128]{1,0:T(8,128)(2,1)S(1)}, bf16[192,128]{1,0:T(8,128)(2,1)S(1)}, u32[]{:S(2)}, u32[]{:S(2)}) %collective-permute-start.3) | collective-permute-done | bytes 49184 | tf_op jit(solution)/shard_map/ppermute | solution.py:380
  109.7 0.0 all-to-all-done.2.got
  109.7 0.0 copy-done.1
  109.7 1.8 %finish.1 = (bf16[256,128]{1,0:T(8,128)(2,1)}, bf16[512,128]{1,0:T(8,128)(2,1)}) custom-call(s32[1]{0:T(128)} %bitcast.2.place, bf16[16,288,128]{2,1,0:T(8,128)(2,1)S(1)} %all-to-all-done.2.got, bf16[64,4096]{1,0:T(8,128)(2,1)} %up.1, f32[64,128]{1,0:T(8,128)S(1)} %get-tuple-element.26.down, s32[4,128]{1,0:T(4,128)S(1)} %bitcast.5), custom_call_target="tpu_custom_call" | custom-call | flops 40000000 | bytes 1700000 | tf_op jit(solution)/shard_map/finish/pallas_call | solution.py:338
  111.5 1.9 %all_gather.7.sums = f32[384,128]{1,0:T(8,128)S(1)} all-gather(f32[192,128]{1,0:T(8,128)S(1)} %convert_add_fusion), channel_id=1, replica_groups={{0,16},{32,48},{64,80},{96,112},{128,144},{160,176},{192,208},{224,240}..., dimensions={0}, use_global_device_ids=true | all-gather | bytes 294912 | tf_op jit(solution)/shard_map/all_gather | solution.py:389
  113.4 0.7 gradients.1
  (6 shorter events, 0.1 us)
Async XLA Ops:
  3.1 37.7 %all-to-all-start = ((bf16[16,304,128]{2,1,0:T(8,128)(2,1)}), bf16[16,304,128]{2,1,0:T(8,128)(2,1)S(1)}, u32[]{:S(2)}, u32[]{:S(2)}) async-start(bf16[16,304,128]{2,1,0:T(8,128)(2,1)} %pack.1), calls=%async_computation | async-start | bytes 2490368 | tf_op jit(solution)/shard_map/all_to_all | solution.py:384
  40.8 23.4 %copy-start = (bf16[256,128]{1,0:T(8,128)(2,1)S(1)}, bf16[256,128]{1,0:T(8,128)(2,1)}, u32[]{:S(2)}) copy-start(bf16[256,128]{1,0:T(8,128)(2,1)} %cot.1) | copy-start | bytes 196612
  69.5 40.2 %all-to-all-start.2 = ((bf16[16,288,128]{2,1,0:T(8,128)(2,1)}), bf16[16,288,128]{2,1,0:T(8,128)(2,1)S(1)}, u32[]{:S(2)}, u32[]{:S(2)}) async-start(bf16[16,288,128]{2,1,0:T(8,128)(2,1)} %get-tuple-element.25), calls=%async_computation.2 | async-start | bytes 2359296 | tf_op jit(solution)/shard_map/all_to_all | solution.py:384
  75.9 33.8 %copy-start.1 = (s32[512]{0:T(512)S(1)}, s32[512]{0:T(512)}, u32[]{:S(2)}) copy-start(s32[512]{0:T(512)} %param.8) | copy-start | bytes 6148
  78.1 6.0 %collective-permute-start = (bf16[192,128]{1,0:T(8,128)(2,1)S(1)}, bf16[192,128]{1,0:T(8,128)(2,1)S(1)}, u32[]{:S(2)}, u32[]{:S(2)}) collective-permute-start(bf16[192,128]{1,0:T(8,128)(2,1)S(1)} %fusion), channel_id=1, source_target_pairs={{0,32},{16,48},{32,0},{48,16},{64,96},{80,112},{96,64},{112,80},{1... | collective-permute-start | bytes 147464 | tf_op jit(solution)/shard_map/ppermute | solution.py:380
  84.1 6.9 %collective-permute-start.1 = (bf16[192,128]{1,0:T(8,128)(2,1)S(1)}, bf16[192,128]{1,0:T(8,128)(2,1)S(1)}, u32[]{:S(2)}, u32[]{:S(2)}) collective-permute-start(bf16[192,128]{1,0:T(8,128)(2,1)S(1)} %add_convert_fusion.2), channel_id=1, source_target_pairs={{0,64},{16,80},{32,96},{48,112},{64,0},{80,16},{96,32},{112,48},{1... | collective-permute-start | bytes 147464 | tf_op jit(solution)/shard_map/ppermute | solution.py:380
  91.0 8.3 %collective-permute-start.2 = (bf16[192,128]{1,0:T(8,128)(2,1)S(1)}, bf16[192,128]{1,0:T(8,128)(2,1)S(1)}, u32[]{:S(2)}, u32[]{:S(2)}) collective-permute-start(bf16[192,128]{1,0:T(8,128)(2,1)S(1)} %add_convert_fusion.1), channel_id=1, source_target_pairs={{0,192},{16,208},{32,224},{48,240},{64,128},{80,144},{96,160},{112... | collective-permute-start | bytes 147464 | tf_op jit(solution)/shard_map/ppermute | solution.py:380
  99.3 10.3 %collective-permute-start.3 = (bf16[192,128]{1,0:T(8,128)(2,1)S(1)}, bf16[192,128]{1,0:T(8,128)(2,1)S(1)}, u32[]{:S(2)}, u32[]{:S(2)}) collective-permute-start(bf16[192,128]{1,0:T(8,128)(2,1)S(1)} %add_convert_fusion), channel_id=1, source_target_pairs={{0,256},{16,272},{32,288},{48,304},{64,320},{80,336},{96,352},{112... | collective-permute-start | bytes 147464 | tf_op jit(solution)/shard_map/ppermute | solution.py:380

commit v3 on v2

--- a/solution.py
+++ b/solution.py
@@ -25,6 +25,10 @@
 
 def in_hbm(*arrays):
     return [pltpu.with_memory_space_constraint(a, pltpu.HBM) for a in arrays]
+
+
+def in_vmem(*arrays):
+    return [pltpu.with_memory_space_constraint(a, pltpu.VMEM) for a in arrays]
 
 
 def dot(a, b):
@@ -263,18 +267,10 @@
     )(got, *in_hbm(weight, up_apart, down_t))
 
 
-def project_kernel(
-    got, weight_hbm, back, cot, sent, down, sums, mixed, weight_t, sems
-):
-    copies = [pltpu.make_async_copy(weight_hbm.at[k], weight_t.at[k], sems.at[k]) for k in range(4)]
-    for copy in copies:
-        copy.start()
+def adapter_kernel(got, back, cot, mixed, down, sums):
     v = got[:, 0:32, :].astype(F32).reshape(NT, 4, 8, T)
     for h in range(4):
         mixed[GROUP * h : GROUP * (h + 1), :] = v[:, h].reshape(GROUP, T).astype(BF16)
-    g = got[:, 32:64, :].astype(F32).reshape(HEADS, 8, T)
-    g = butterfly(g, 6) * 0.125
-    sent[:, 256:288, :] = g.reshape(NT, 32, T).astype(BF16)
     total = jnp.sum(got[:, 64:128, :].astype(F32), axis=0)
     down[...] = total
     high, low = split(total)
@@ -286,31 +282,43 @@
     for half in range(2):
         c = cot[GROUP * half : GROUP * (half + 1), :]
         sums[256 + RANK * half : 320 + RANK * half, :] = dot_11(high, c) + dot_11(low, c)
+
+
+def adapter(got, back, cot):
+    return pl.pallas_call(
+        adapter_kernel,
+        in_specs=[VMEM] * 3,
+        out_specs=[VMEM] * 3,
+        out_shape=[
+            jax.ShapeDtypeStruct((F, T), BF16),
+            jax.ShapeDtypeStruct((RANK, T), F32),
+            jax.ShapeDtypeStruct((384, T), F32),
+        ],
+        compiler_params=PARAMS,
+        cost_estimate=pl.CostEstimate(flops=30_000_000, bytes_accessed=1_000_000, transcendentals=0),
+        name="adapter",
+    )(got, back, cot)
+
+
+def project_kernel(got, mixed, weight_t, sent):
+    g = got[:, 32:64, :].astype(F32).reshape(HEADS, 8, T)
+    g = butterfly(g, 6) * 0.125
+    sent[:, 256:288, :] = g.reshape(NT, 32, T).astype(BF16)
     for k in range(4):
-        copies[k].wait()
         share = dot(weight_t[k], mixed[...])
         sent[:, 64 * k : 64 * (k + 1), :] = share.reshape(NT, 64, T).astype(BF16)
 
 
-def project(got, weight_t, back, cot):
+def project(got, mixed, weight_t):
     return pl.pallas_call(
         project_kernel,
-        in_specs=[VMEM, HBM, VMEM, VMEM],
-        out_specs=[VMEM] * 3,
-        out_shape=[
-            jax.ShapeDtypeStruct((NT, 288, T), BF16),
-            jax.ShapeDtypeStruct((RANK, T), F32),
-            jax.ShapeDtypeStruct((384, T), F32),
-        ],
-        scratch_shapes=[
-            pltpu.VMEM((F, T), BF16),
-            pltpu.VMEM((4, C, F), BF16),
-            DMA((4,)),
-        ],
+        in_specs=[VMEM] * 3,
+        out_specs=VMEM,
+        out_shape=jax.ShapeDtypeStruct((NT, 288, T), BF16),
         compiler_params=PARAMS,
         cost_estimate=pl.CostEstimate(flops=540_000_000, bytes_accessed=6_000_000, transcendentals=0),
         name="project",
-    )(got, *in_hbm(weight_t), back, cot)
+    )(got, mixed, *in_vmem(weight_t))
 
 
 def finish_kernel(place, got, up, down, flags, out, input_gradient, own, sem):
@@ -350,17 +358,18 @@
     )(place, got, *in_hbm(up), down, flags)
 
 
-def gradients_kernel(sums, down_gradient, up_gradient):
+def gradients_kernel(terms, down_gradient, up_gradient):
     multiplier = ADAPTER_SCALE / 64.0
+    sums = (terms[0].astype(F32) + terms[1].astype(F32)) * multiplier
     for h in range(4):
         lanes = slice(GROUP * h, GROUP * (h + 1))
-        down_gradient[:, lanes] = sums[RANK * h : RANK * (h + 1), :] * multiplier
+        down_gradient[:, lanes] = sums[RANK * h : RANK * (h + 1), :]
     for half in range(2):
         lanes = slice(GROUP * half, GROUP * (half + 1))
-        up_gradient[:, lanes] = sums[256 + RANK * half : 320 + RANK * half, :] * multiplier
-
-
-def gradients(sums):
+        up_gradient[:, lanes] = sums[256 + RANK * half : 320 + RANK * half, :]
+
+
+def gradients(terms):
     return pl.pallas_call(
         gradients_kernel,
         in_specs=[VMEM],
@@ -372,45 +381,49 @@
         compiler_params=PARAMS,
         cost_estimate=pl.CostEstimate(flops=100_000, bytes_accessed=500_000, transcendentals=0),
         name="gradients",
-    )(sums)
-
-
-def by(value, axis, mask):
-    pairs = [(source, source ^ mask) for source in range(lax.axis_size(axis))]
-    return lax.ppermute(value, axis, pairs)
+    )(terms)
 
 
 def exchange(value):
     return lax.all_to_all(value, "tensor", 0, 0, tiled=True)
 
 
-def both_cores(value):
-    groups = [[device, device + 1] for device in range(0, lax.axis_size("dp"), 2)]
-    return lax.all_gather(value, "dp", axis=0, tiled=True, axis_index_groups=groups)
-
-
-def add_partner(value, mask):
-    value = value.astype(BF16)
-    return value.astype(F32) + by(value, "dp", mask).astype(F32)
+def terms_of(value, masks):
+    devices = range(lax.axis_size("dp"))
+    groups = {}
+    for device in devices:
+        members = [device]
+        for mask in masks:
+            members += [member ^ mask for member in members]
+        groups[min(members)] = sorted(members)
+    return lax.all_gather(
+        value.astype(BF16), "dp", axis=0, axis_index_groups=list(groups.values())
+    )
+
+
+def sum_of(terms):
+    terms = [terms[n].astype(F32) for n in range(terms.shape[0])]
+    while len(terms) > 1:
+        terms = [terms[n] + terms[n + 1] for n in range(0, len(terms), 2)]
+    return terms[0]
 
 
 def local(activ, flags, codes, scales, down_map, up, cot):
-    core = lax.axis_index("dp") & 1
     place = jnp.stack([lax.axis_index("tensor")]).astype(jnp.int32)
     flags = flags.reshape(4, GROUP)
     down_t = down_map.T
     got = exchange(pack(activ, flags, down_t, cot))
     weight, weight_t, up_apart = make_weights(codes, scales, up)
     sent, back = turn(got, weight, up_apart, down_t)
-    sent, down, sums = project(exchange(sent), weight_t, back, cot)
     got = exchange(sent)
-    two = both_cores(sums)
-    half = lax.dynamic_slice_in_dim(two[:384] + two[384:], core * 192, 192)
-    for mask in (2, 4, 12, 16):
-        half = add_partner(half, mask)
+    mixed, down, sums = adapter(got, back, cot)
+    got = exchange(project(got, mixed, weight_t))
+    sums = sum_of(terms_of(sums, (1, 2)))
+    sums = sum_of(terms_of(sums, (4,)))
+    sums = sum_of(terms_of(sums, (12,)))
+    terms = terms_of(sums, (16,))
+    down_gradient, up_gradient = gradients(terms)
     out, input_gradient = finish(place, got, up, down, flags)
-    half, out, input_gradient = lax.optimization_barrier((half, out, input_gradient))
-    down_gradient, up_gradient = gradients(both_cores(half))
     return out, input_gradient, down_gradient.T, up_gradient
 
 

time: 115 us -> 111 us (0.965)
  blocking collectives: 24 us -> 53.1 us
  starting transfers between devices: 39 us -> 16.6 us
  waiting for transfers between devices: 29.6 us -> 20.4 us
  Pallas kernels: 20.6 us -> 18.2 us
    all_gather x2 -> x4, blocking collectives: 4.04 us -> 33.1 us  [terms_of(): lax.all_gather(value.astype(BF16), 'dp', axis=0, axis_index_groups=list(g...]
    ppermute x4 -> x0, starting transfers between devices: 22.3 us -> none  [by(): return lax.ppermute(value, axis, pairs)]
    ppermute x4 -> x0, waiting for transfers between devices: 9.15 us -> none  [by(): return lax.ppermute(value, axis, pairs)]
    pallas_call x1 -> x2, Pallas kernels: 5.29 us -> 2.7 us  [the longest x1 2.33 us: project(): pl.pallas_call(project_kernel, in_specs=[VMEM] * 3, out_specs=VMEM, out_s...]
  transfers between devices with their start and end apart: 6 -> 2, of which waited for: 5 -> 1; matrix products, arithmetic and copies ran while one was open for 0% -> 0% of each run, Pallas kernels for 6% -> 7%
where the time goes in v3:
time: 111 us; the launch traced here: 109 us
  blocking collectives  53.1 us (48%)
  waiting for transfers between devices  20.4 us (18%)
  Pallas kernels  18.2 us (16%)
  starting transfers between devices  16.6 us (15%)
    all_gather x4, blocking collectives, terms_of(): lax.all_gather(value.astype(BF16), 'dp', axis=0, axis_index_groups=list(g...  33.1 us
    all_to_all x2, waiting for transfers between devices, exchange(): return lax.all_to_all(value, 'tensor', 0, 0, tiled=True)  20.4 us
    all_to_all x1, blocking collectives, exchange(): return lax.all_to_all(value, 'tensor', 0, 0, tiled=True)  20 us
    all_to_all x2, starting transfers between devices, exchange(): return lax.all_to_all(value, 'tensor', 0, 0, tiled=True)  16.6 us
    pallas_call x1, Pallas kernels, make_weights(): pl.pallas_call(weights_kernel, in_specs=[HBM] * 3, out_specs=[HBM] * 3, o...  7.02 us
    pallas_call x1, Pallas kernels, turn(): pl.pallas_call(turn_kernel, in_specs=[VMEM] + [HBM] * 3, out_specs=[VMEM]...  3.56 us
    pallas_call x1, Pallas kernels, pack(): pl.pallas_call(pack_kernel, in_specs=[HBM] * 4, out_specs=HBM, out_shape=...  2.44 us
    pallas_call x1, Pallas kernels, project(): pl.pallas_call(project_kernel, in_specs=[VMEM] * 3, out_specs=VMEM, out_s...  2.33 us
  transfers between devices with their start and end apart: 2, of which 1 were waited for; matrix products, arithmetic and copies ran while one was open for 0% of the time, Pallas kernels for 7%

profile of v3, /device:TPU:6, one launch (start us, length us, event | category | flops | bytes accessed | tf_op | source)
XLA Modules:
  0.0 109.1 jit_solution(13427142395563308)
XLA Ops:
  0.6 2.4 %pack.1 = bf16[16,304,128]{2,1,0:T(8,128)(2,1)} custom-call(bf16[512,128]{1,0:T(8,128)(2,1)} %activ_hbm.1, s32[4,128]{1,0:T(4,128)} %bitcast.6, bf16[64,512]{1,0:T(8,128)(2,1)} %bitcast.8, bf16[256,128]{1,0:T(8,128)(2,1)} %cot.1), custom_call_target="tpu_custom_call" | custom-call | flops 60000000 | bytes 2000000 | tf_op jit(solution)/shard_map/pack/pallas_call | solution.py:177
  3.1 10.2 %all-to-all-start = ((bf16[16,304,128]{2,1,0:T(8,128)(2,1)}), bf16[16,304,128]{2,1,0:T(8,128)(2,1)S(1)}, u32[]{:S(2)}, u32[]{:S(2)}) async-start(bf16[16,304,128]{2,1,0:T(8,128)(2,1)} %pack.1), calls=%async_computation | async-start | bytes 2490368 | tf_op jit(solution)/shard_map/all_to_all | solution.py:388
  13.3 7.0 %weights.1 = (bf16[4,512,1024]{2,1,0:T(8,128)(2,1)}, bf16[4,1024,512]{2,1,0:T(8,128)(2,1)}, bf16[4,64,1024]{2,1,0:T(8,128)(2,1)}) custom-call(s32[512,1024]{1,0:T(8,128)} %codes_hbm.1, bf16[4,4096]{1,0:T(4,128)(2,1)} %scales_hbm.1, bf16[64,4096]{1,0:T(8,128)(2,1)} %up.1), custom_call_target="tpu_custom_call" | custom-call | flops 20000000 | bytes 20000000 | tf_op jit(solution)/shard_map/weights/pallas_call | solution.py:112
  20.3 20.4 %all-to-all-done.got = bf16[16,304,128]{2,1,0:T(8,128)(2,1)S(1)} async-done(((bf16[16,304,128]{2,1,0:T(8,128)(2,1)}), bf16[16,304,128]{2,1,0:T(8,128)(2,1)S(1)}, u32[]{:S(2)}, u32[]{:S(2)}) %all-to-all-start) | async-done | bytes 1245216 | tf_op jit(solution)/shard_map/all_to_all | solution.py:388
  40.7 0.0 copy-start.1
  40.7 0.0 copy-start
  40.7 3.6 %turn.1 = (bf16[16,128,128]{2,1,0:T(8,128)(2,1)S(1)}, f32[64,128]{1,0:T(8,128)S(1)}) custom-call(bf16[16,304,128]{2,1,0:T(8,128)(2,1)S(1)} %all-to-all-done.got, bf16[4,512,1024]{2,1,0:T(8,128)(2,1)} %get-tuple-element.16.weight_hbm, bf16[4,64,1024]{2,1,0:T(8,128)(2,1)} %get-tuple-element.17.up_hbm, bf16[64,512]{1,0:T(8,128)(2,1)} %bitcast.9), custom_call_target="tpu_custom_call" | custom-call | flops 600000000 | bytes 7000000 | tf_op jit(solution)/shard_map/turn/pallas_call | solution.py:249
  44.3 20.0 %all_to_all.15.got = bf16[16,128,128]{2,1,0:T(8,128)(2,1)S(1)} all-to-all(bf16[16,128,128]{2,1,0:T(8,128)(2,1)S(1)} %get-tuple-element.18), channel_id=1, replica_groups=mesh['dp'=32,'tensor'=16] {'tensor'}, dimensions={0} | all-to-all | bytes 1048576 | tf_op jit(solution)/shard_map/all_to_all | solution.py:388
  64.3 0.0 copy-done.1
  64.3 0.4 adapter.1
  64.7 0.0 copy-done
  64.7 2.3 %project.1 = bf16[16,288,128]{2,1,0:T(8,128)(2,1)} custom-call(bf16[16,128,128]{2,1,0:T(8,128)(2,1)S(1)} %all_to_all.15.got, bf16[512,128]{1,0:T(8,128)(2,1)S(1)} %get-tuple-element.20.mixed, bf16[4,1024,512]{2,1,0:T(8,128)(2,1)S(1)} %copy-done), custom_call_target="tpu_custom_call" | custom-call | flops 540000000 | bytes 6000000 | tf_op jit(solution)/shard_map/project/pallas_call | solution.py:313
  67.0 6.4 %all-to-all-start.2 = ((bf16[16,288,128]{2,1,0:T(8,128)(2,1)}), bf16[16,288,128]{2,1,0:T(8,128)(2,1)S(1)}, u32[]{:S(2)}, u32[]{:S(2)}) async-start(bf16[16,288,128]{2,1,0:T(8,128)(2,1)} %project.1), calls=%async_computation.2 | async-start | bytes 2359296 | tf_op jit(solution)/shard_map/all_to_all | solution.py:388
  73.4 0.0 copy-start.2
  73.4 6.5 %all-gather = bf16[1536,128]{1,0:T(8,128)(2,1)S(1)} all-gather(bf16[384,128]{1,0:T(8,128)(2,1)S(1)} %convert_element_type.47), channel_id=2, replica_groups={{0,16,32,48},{64,80,96,112},{128,144,160,176},{192,208,224,240},{256,27..., dimensions={0}, use_global_device_ids=true | all-gather | bytes 491520 | tf_op jit(solution)/shard_map/all_gather | solution.py:399
  80.0 0.1 fusion
  80.0 8.7 %all_gather.20 = bf16[2,384,128]{2,1,0:T(8,128)(2,1)S(1)} all-gather(bf16[1,384,128]{2,1,0:T(8,128)(2,1)S(1)} %fusion), channel_id=1, replica_groups={{0,64},{16,80},{32,96},{48,112},{128,192},{144,208},{160,224},{176,240}..., dimensions={0}, use_global_device_ids=true | all-gather | bytes 294912 | tf_op jit(solution)/shard_map/all_gather | solution.py:399
  88.8 7.6 %all_gather.21 = bf16[2,384,128]{2,1,0:T(8,128)(2,1)S(1)} all-gather(bf16[1,384,128]{2,1,0:T(8,128)(2,1)S(1)} %add_convert_fusion.2), channel_id=1, replica_groups={{0,192},{16,208},{32,224},{48,240},{64,128},{80,144},{96,160},{112,176}..., dimensions={0}, use_global_device_ids=true | all-gather | bytes 294912 | tf_op jit(solution)/shard_map/all_gather | solution.py:399
  96.4 10.2 %all_gather.22.terms = bf16[2,384,128]{2,1,0:T(8,128)(2,1)S(1)} all-gather(bf16[1,384,128]{2,1,0:T(8,128)(2,1)S(1)} %add_convert_fusion.1), channel_id=1, replica_groups={{0,256},{16,272},{32,288},{48,304},{64,320},{80,336},{96,352},{112,368}..., dimensions={0}, use_global_device_ids=true | all-gather | bytes 294912 | tf_op jit(solution)/shard_map/all_gather | solution.py:399
  106.6 0.7 gradients.1
  107.3 0.0 all-to-all-done.2.got
  107.3 0.0 copy-done.2
  107.3 1.8 %finish.1 = (bf16[256,128]{1,0:T(8,128)(2,1)}, bf16[512,128]{1,0:T(8,128)(2,1)}) custom-call(s32[1]{0:T(128)} %bitcast.place, bf16[16,288,128]{2,1,0:T(8,128)(2,1)S(1)} %all-to-all-done.2.got, bf16[64,4096]{1,0:T(8,128)(2,1)} %up.1, f32[64,128]{1,0:T(8,128)S(1)} %get-tuple-element.22.down, s32[4,128]{1,0:T(4,128)S(1)} %bitcast.7), custom_call_target="tpu_custom_call" | custom-call | flops 40000000 | bytes 1700000 | tf_op jit(solution)/shard_map/finish/pallas_call | solution.py:346
  (3 shorter events, 0.1 us)
Async XLA Ops:
  3.1 37.7 %all-to-all-start = ((bf16[16,304,128]{2,1,0:T(8,128)(2,1)}), bf16[16,304,128]{2,1,0:T(8,128)(2,1)S(1)}, u32[]{:S(2)}, u32[]{:S(2)}) async-start(bf16[16,304,128]{2,1,0:T(8,128)(2,1)} %pack.1), calls=%async_computation | async-start | bytes 2490368 | tf_op jit(solution)/shard_map/all_to_all | solution.py:388
  40.7 23.6 %copy-start.1 = (bf16[256,128]{1,0:T(8,128)(2,1)S(1)}, bf16[256,128]{1,0:T(8,128)(2,1)}, u32[]{:S(2)}) copy-start(bf16[256,128]{1,0:T(8,128)(2,1)} %cot.1) | copy-start | bytes 196612
  40.7 23.9 %copy-start = (bf16[4,1024,512]{2,1,0:T(8,128)(2,1)S(1)}, bf16[4,1024,512]{2,1,0:T(8,128)(2,1)}, u32[]{:S(2)}) copy-start(bf16[4,1024,512]{2,1,0:T(8,128)(2,1)} %get-tuple-element.21.weight_t) | copy-start | bytes 12582916
  67.0 40.3 %all-to-all-start.2 = ((bf16[16,288,128]{2,1,0:T(8,128)(2,1)}), bf16[16,288,128]{2,1,0:T(8,128)(2,1)S(1)}, u32[]{:S(2)}, u32[]{:S(2)}) async-start(bf16[16,288,128]{2,1,0:T(8,128)(2,1)} %project.1), calls=%async_computation.2 | async-start | bytes 2359296 | tf_op jit(solution)/shard_map/all_to_all | solution.py:388
  73.4 33.9 %copy-start.2 = (s32[512]{0:T(512)S(1)}, s32[512]{0:T(512)}, u32[]{:S(2)}) copy-start(s32[512]{0:T(512)} %param.8) | copy-start | bytes 6148

commit v4 on v3

--- a/solution.py
+++ b/solution.py
@@ -358,18 +358,17 @@
     )(place, got, *in_hbm(up), down, flags)
 
 
-def gradients_kernel(terms, down_gradient, up_gradient):
+def gradients_kernel(sums, down_gradient, up_gradient):
     multiplier = ADAPTER_SCALE / 64.0
-    sums = (terms[0].astype(F32) + terms[1].astype(F32)) * multiplier
     for h in range(4):
         lanes = slice(GROUP * h, GROUP * (h + 1))
-        down_gradient[:, lanes] = sums[RANK * h : RANK * (h + 1), :]
+        down_gradient[:, lanes] = sums[RANK * h : RANK * (h + 1), :] * multiplier
     for half in range(2):
         lanes = slice(GROUP * half, GROUP * (half + 1))
-        up_gradient[:, lanes] = sums[256 + RANK * half : 320 + RANK * half, :]
-
-
-def gradients(terms):
+        up_gradient[:, lanes] = sums[256 + RANK * half : 320 + RANK * half, :] * multiplier
+
+
+def gradients(sums):
     return pl.pallas_call(
         gradients_kernel,
         in_specs=[VMEM],
@@ -381,27 +380,25 @@
         compiler_params=PARAMS,
         cost_estimate=pl.CostEstimate(flops=100_000, bytes_accessed=500_000, transcendentals=0),
         name="gradients",
-    )(terms)
+    )(sums)
 
 
 def exchange(value):
     return lax.all_to_all(value, "tensor", 0, 0, tiled=True)
 
 
-def terms_of(value, masks):
-    devices = range(lax.axis_size("dp"))
+def gather(value, masks):
     groups = {}
-    for device in devices:
+    for device in range(lax.axis_size("dp")):
         members = [device]
         for mask in masks:
             members += [member ^ mask for member in members]
         groups[min(members)] = sorted(members)
-    return lax.all_gather(
-        value.astype(BF16), "dp", axis=0, axis_index_groups=list(groups.values())
-    )
-
-
-def sum_of(terms):
+    return lax.all_gather(value, "dp", axis=0, axis_index_groups=list(groups.values()))
+
+
+def sum_over(value, masks):
+    terms = gather(value.astype(BF16), masks)
     terms = [terms[n].astype(F32) for n in range(terms.shape[0])]
     while len(terms) > 1:
         terms = [terms[n] + terms[n + 1] for n in range(0, len(terms), 2)]
@@ -409,6 +406,7 @@
 
 
 def local(activ, flags, codes, scales, down_map, up, cot):
+    replica = lax.axis_index("dp")
     place = jnp.stack([lax.axis_index("tensor")]).astype(jnp.int32)
     flags = flags.reshape(4, GROUP)
     down_t = down_map.T
@@ -418,12 +416,15 @@
     got = exchange(sent)
     mixed, down, sums = adapter(got, back, cot)
     got = exchange(project(got, mixed, weight_t))
-    sums = sum_of(terms_of(sums, (1, 2)))
-    sums = sum_of(terms_of(sums, (4,)))
-    sums = sum_of(terms_of(sums, (12,)))
-    terms = terms_of(sums, (16,))
-    down_gradient, up_gradient = gradients(terms)
+    half = lax.dynamic_slice_in_dim(sum_over(sums, (1, 2)), 192 * (replica & 1), 192)
+    half = sum_over(half, (4,))
+    half = sum_over(half, (12,)).astype(BF16)
+    pairs = [(source, source ^ 16) for source in range(lax.axis_size("dp"))]
+    other = lax.ppermute(half, "dp", pairs)
     out, input_gradient = finish(place, got, up, down, flags)
+    other, out, input_gradient = lax.optimization_barrier((other, out, input_gradient))
+    half = half.astype(F32) + other.astype(F32)
+    down_gradient, up_gradient = gradients(gather(half, (1,)).reshape(384, T))
     return out, input_gradient, down_gradient.T, up_gradient
 
 

time: 111 us -> 108 us (0.973)
  blocking collectives: 53.1 us -> 42.1 us
  starting transfers between devices: 16.6 us -> 24.8 us
    all_gather x4, blocking collectives: 33.1 us -> 22.1 us  [gather(): lax.all_gather(value, 'dp', axis=0, axis_index_groups=list(groups.values()))]
    ppermute x0 -> x1, starting transfers between devices: none -> 8.23 us  [local(): other = lax.ppermute(half, 'dp', pairs)]
  transfers between devices with their start and end apart: 2 -> 3, of which waited for: 1 -> 2; matrix products, arithmetic and copies ran while one was open for 0% -> 0% of each run, Pallas kernels for 7% -> 8%
where the time goes in v4:
time: 108 us; the launch traced here: 107 us
  blocking collectives  42.1 us (39%)
  starting transfers between devices  24.8 us (23%)
  waiting for transfers between devices  20.8 us (19%)
  Pallas kernels  18.2 us (17%)
    all_gather x4, blocking collectives, gather(): lax.all_gather(value, 'dp', axis=0, axis_index_groups=list(groups.values()))  22.1 us
    all_to_all x2, waiting for transfers between devices, exchange(): return lax.all_to_all(value, 'tensor', 0, 0, tiled=True)  20.4 us
    all_to_all x1, blocking collectives, exchange(): return lax.all_to_all(value, 'tensor', 0, 0, tiled=True)  20 us
    all_to_all x2, starting transfers between devices, exchange(): return lax.all_to_all(value, 'tensor', 0, 0, tiled=True)  16.6 us
    ppermute x1, starting transfers between devices, local(): other = lax.ppermute(half, 'dp', pairs)  8.23 us
    pallas_call x1, Pallas kernels, make_weights(): pl.pallas_call(weights_kernel, in_specs=[HBM] * 3, out_specs=[HBM] * 3, o...  7.03 us
    pallas_call x1, Pallas kernels, turn(): pl.pallas_call(turn_kernel, in_specs=[VMEM] + [HBM] * 3, out_specs=[VMEM]...  3.56 us
    pallas_call x1, Pallas kernels, pack(): pl.pallas_call(pack_kernel, in_specs=[HBM] * 4, out_specs=HBM, out_shape=...  2.47 us
  transfers between devices with their start and end apart: 3, of which 2 were waited for; matrix products, arithmetic and copies ran while one was open for 0% of the time, Pallas kernels for 8%

profile of v4, /device:TPU:6, one launch (start us, length us, event | category | flops | bytes accessed | tf_op | source)
XLA Modules:
  0.0 106.8 jit_solution(17322067310564301022)
XLA Ops:
  0.6 2.5 %pack.1 = bf16[16,304,128]{2,1,0:T(8,128)(2,1)} custom-call(bf16[512,128]{1,0:T(8,128)(2,1)} %activ_hbm.1, s32[4,128]{1,0:T(4,128)} %bitcast.10, bf16[64,512]{1,0:T(8,128)(2,1)} %bitcast.12, bf16[256,128]{1,0:T(8,128)(2,1)} %cot.1), custom_call_target="tpu_custom_call" | custom-call | flops 60000000 | bytes 2000000 | tf_op jit(solution)/shard_map/pack/pallas_call | solution.py:177
  3.1 10.2 %all-to-all-start = ((bf16[16,304,128]{2,1,0:T(8,128)(2,1)}), bf16[16,304,128]{2,1,0:T(8,128)(2,1)S(1)}, u32[]{:S(2)}, u32[]{:S(2)}) async-start(bf16[16,304,128]{2,1,0:T(8,128)(2,1)} %pack.1), calls=%async_computation | async-start | bytes 2490368 | tf_op jit(solution)/shard_map/all_to_all | solution.py:387
  13.3 7.0 %weights.1 = (bf16[4,512,1024]{2,1,0:T(8,128)(2,1)}, bf16[4,1024,512]{2,1,0:T(8,128)(2,1)}, bf16[4,64,1024]{2,1,0:T(8,128)(2,1)}) custom-call(s32[512,1024]{1,0:T(8,128)} %codes_hbm.1, bf16[4,4096]{1,0:T(4,128)(2,1)} %scales_hbm.1, bf16[64,4096]{1,0:T(8,128)(2,1)} %up.1), custom_call_target="tpu_custom_call" | custom-call | flops 20000000 | bytes 20000000 | tf_op jit(solution)/shard_map/weights/pallas_call | solution.py:112
  20.4 20.4 %all-to-all-done.got = bf16[16,304,128]{2,1,0:T(8,128)(2,1)S(1)} async-done(((bf16[16,304,128]{2,1,0:T(8,128)(2,1)}), bf16[16,304,128]{2,1,0:T(8,128)(2,1)S(1)}, u32[]{:S(2)}, u32[]{:S(2)}) %all-to-all-start) | async-done | bytes 1245216 | tf_op jit(solution)/shard_map/all_to_all | solution.py:387
  40.8 0.0 copy-start.1
  40.8 0.0 copy-start
  40.8 3.6 %turn.1 = (bf16[16,128,128]{2,1,0:T(8,128)(2,1)S(1)}, f32[64,128]{1,0:T(8,128)S(1)}) custom-call(bf16[16,304,128]{2,1,0:T(8,128)(2,1)S(1)} %all-to-all-done.got, bf16[4,512,1024]{2,1,0:T(8,128)(2,1)} %get-tuple-element.19.weight_hbm, bf16[4,64,1024]{2,1,0:T(8,128)(2,1)} %get-tuple-element.20.up_hbm, bf16[64,512]{1,0:T(8,128)(2,1)} %bitcast.13), custom_call_target="tpu_custom_call" | custom-call | flops 600000000 | bytes 7000000 | tf_op jit(solution)/shard_map/turn/pallas_call | solution.py:249
  44.3 20.0 %all_to_all.15.got = bf16[16,128,128]{2,1,0:T(8,128)(2,1)S(1)} all-to-all(bf16[16,128,128]{2,1,0:T(8,128)(2,1)S(1)} %get-tuple-element.21), channel_id=1, replica_groups=mesh['dp'=32,'tensor'=16] {'tensor'}, dimensions={0} | all-to-all | bytes 1048576 | tf_op jit(solution)/shard_map/all_to_all | solution.py:387
  64.3 0.0 copy-done.1
  64.3 0.4 adapter.1
  64.7 0.0 copy-done
  64.7 2.3 %project.1 = bf16[16,288,128]{2,1,0:T(8,128)(2,1)} custom-call(bf16[16,128,128]{2,1,0:T(8,128)(2,1)S(1)} %all_to_all.15.got, bf16[512,128]{1,0:T(8,128)(2,1)S(1)} %get-tuple-element.24.mixed, bf16[4,1024,512]{2,1,0:T(8,128)(2,1)S(1)} %copy-done), custom_call_target="tpu_custom_call" | custom-call | flops 540000000 | bytes 6000000 | tf_op jit(solution)/shard_map/project/pallas_call | solution.py:313
  67.1 6.4 %all-to-all-start.2 = ((bf16[16,288,128]{2,1,0:T(8,128)(2,1)}), bf16[16,288,128]{2,1,0:T(8,128)(2,1)S(1)}, u32[]{:S(2)}, u32[]{:S(2)}) async-start(bf16[16,288,128]{2,1,0:T(8,128)(2,1)} %project.1), calls=%async_computation.2 | async-start | bytes 2359296 | tf_op jit(solution)/shard_map/all_to_all | solution.py:387
  73.4 0.0 copy-start.2
  73.5 6.5 %all-gather = bf16[1536,128]{1,0:T(8,128)(2,1)S(1)} all-gather(bf16[384,128]{1,0:T(8,128)(2,1)S(1)} %convert_element_type.55), channel_id=2, replica_groups={{0,16,32,48},{64,80,96,112},{128,144,160,176},{192,208,224,240},{256,27..., dimensions={0}, use_global_device_ids=true | all-gather | bytes 491520 | tf_op jit(solution)/shard_map/all_gather | solution.py:397
  80.1 6.7 %all_gather.22 = bf16[2,192,128]{2,1,0:T(8,128)(2,1)S(1)} all-gather(bf16[1,192,128]{2,1,0:T(8,128)(2,1)S(1)} %fusion.1), channel_id=1, replica_groups={{0,64},{16,80},{32,96},{48,112},{128,192},{144,208},{160,224},{176,240}..., dimensions={0}, use_global_device_ids=true | all-gather | bytes 147456 | tf_op jit(solution)/shard_map/all_gather | solution.py:397
  86.8 6.9 %all_gather.23 = bf16[2,192,128]{2,1,0:T(8,128)(2,1)S(1)} all-gather(bf16[1,192,128]{2,1,0:T(8,128)(2,1)S(1)} %add_convert_fusion.2), channel_id=1, replica_groups={{0,192},{16,208},{32,224},{48,240},{64,128},{80,144},{96,160},{112,176}..., dimensions={0}, use_global_device_ids=true | all-gather | bytes 147456 | tf_op jit(solution)/shard_map/all_gather | solution.py:397
  93.7 8.2 %collective-permute-start = (bf16[192,128]{1,0:T(8,128)(2,1)S(1)}, bf16[192,128]{1,0:T(8,128)(2,1)S(1)}, u32[]{:S(2)}, u32[]{:S(2)}) collective-permute-start(bf16[192,128]{1,0:T(8,128)(2,1)S(1)} %fusion), channel_id=1, source_target_pairs={{0,256},{16,272},{32,288},{48,304},{64,320},{80,336},{96,352},{112... | collective-permute-start | bytes 147464 | tf_op jit(solution)/shard_map/ppermute | solution.py:423
  101.9 0.0 all-to-all-done.2.got
  102.0 0.0 copy-done.2
  102.0 1.8 %finish.1 = (bf16[256,128]{1,0:T(8,128)(2,1)}, bf16[512,128]{1,0:T(8,128)(2,1)}) custom-call(s32[1]{0:T(128)} %bitcast.4.place, bf16[16,288,128]{2,1,0:T(8,128)(2,1)S(1)} %all-to-all-done.2.got, bf16[64,4096]{1,0:T(8,128)(2,1)} %up.1, f32[64,128]{1,0:T(8,128)S(1)} %get-tuple-element.26.down, s32[4,128]{1,0:T(4,128)S(1)} %bitcast.11), custom_call_target="tpu_custom_call" | custom-call | flops 40000000 | bytes 1700000 | tf_op jit(solution)/shard_map/finish/pallas_call | solution.py:346
  103.7 0.4 collective-permute-done
  104.1 1.9 %all-gather.1.sums = f32[384,128]{1,0:T(8,128)S(1)} all-gather(f32[192,128]{1,0:T(8,128)S(1)} %convert_add_fusion), channel_id=3, replica_groups={{0,16},{32,48},{64,80},{96,112},{128,144},{160,176},{192,208},{224,240}..., dimensions={0}, use_global_device_ids=true | all-gather | bytes 294912 | tf_op jit(solution)/shard_map/all_gather | solution.py:397
  106.1 0.7 gradients.1
  (6 shorter events, 0.1 us)
Async XLA Ops:
  3.1 37.7 %all-to-all-start = ((bf16[16,304,128]{2,1,0:T(8,128)(2,1)}), bf16[16,304,128]{2,1,0:T(8,128)(2,1)S(1)}, u32[]{:S(2)}, u32[]{:S(2)}) async-start(bf16[16,304,128]{2,1,0:T(8,128)(2,1)} %pack.1), calls=%async_computation | async-start | bytes 2490368 | tf_op jit(solution)/shard_map/all_to_all | solution.py:387
  40.8 23.6 %copy-start.1 = (bf16[256,128]{1,0:T(8,128)(2,1)S(1)}, bf16[256,128]{1,0:T(8,128)(2,1)}, u32[]{:S(2)}) copy-start(bf16[256,128]{1,0:T(8,128)(2,1)} %cot.1) | copy-start | bytes 196612
  40.8 23.9 %copy-start = (bf16[4,1024,512]{2,1,0:T(8,128)(2,1)S(1)}, bf16[4,1024,512]{2,1,0:T(8,128)(2,1)}, u32[]{:S(2)}) copy-start(bf16[4,1024,512]{2,1,0:T(8,128)(2,1)} %get-tuple-element.25.weight_t) | copy-start | bytes 12582916
  67.1 34.9 %all-to-all-start.2 = ((bf16[16,288,128]{2,1,0:T(8,128)(2,1)}), bf16[16,288,128]{2,1,0:T(8,128)(2,1)S(1)}, u32[]{:S(2)}, u32[]{:S(2)}) async-start(bf16[16,288,128]{2,1,0:T(8,128)(2,1)} %project.1), calls=%async_computation.2 | async-start | bytes 2359296 | tf_op jit(solution)/shard_map/all_to_all | solution.py:387
  73.4 28.5 %copy-start.2 = (s32[512]{0:T(512)S(1)}, s32[512]{0:T(512)}, u32[]{:S(2)}) copy-start(s32[512]{0:T(512)} %param.8) | copy-start | bytes 6148
  93.7 10.4 %collective-permute-start = (bf16[192,128]{1,0:T(8,128)(2,1)S(1)}, bf16[192,128]{1,0:T(8,128)(2,1)S(1)}, u32[]{:S(2)}, u32[]{:S(2)}) collective-permute-start(bf16[192,128]{1,0:T(8,128)(2,1)S(1)} %fusion), channel_id=1, source_target_pairs={{0,256},{16,272},{32,288},{48,304},{64,320},{80,336},{96,352},{112... | collective-permute-start | bytes 147464 | tf_op jit(solution)/shard_map/ppermute | solution.py:423

commit v5 on v4

--- a/solution.py
+++ b/solution.py
@@ -63,8 +63,8 @@
 
 
 def weights_kernel(
-    codes_hbm, scales_hbm, up_hbm, weight_out, weight_t_out, up_out,
-    codes, scales, up, scales_apart, weight, weight_t, up_apart, sems, out_sems,
+    codes_hbm, scales_hbm, up_hbm, weight_out, up_out,
+    codes, scales, up, scales_apart, weight, up_apart, sems, out_sems,
 ):
     copy_scales = pltpu.make_async_copy(scales_hbm, scales, sems.at[4])
     copy_up = pltpu.make_async_copy(up_hbm, up, sems.at[5])
@@ -97,13 +97,10 @@
             nibble = ((codes[rows, :] >> (4 * k)) & 15) - 8
             part = nibble.astype(F32) * scales_apart[k, g : g + 1, :]
             weight[k, rows, :] = part.astype(BF16)
-            weight_t[k, :, rows] = part.T.astype(BF16)
         sends.append(
             pltpu.make_async_copy(weight.at[:, rows], weight_out.at[:, rows], out_sems.at[g])
         )
         sends[g + 1].start()
-    sends.append(pltpu.make_async_copy(weight_t, weight_t_out, out_sems.at[4]))
-    sends[5].start()
     for send in sends:
         send.wait()
 
@@ -112,10 +109,9 @@
     return pl.pallas_call(
         weights_kernel,
         in_specs=[HBM] * 3,
-        out_specs=[HBM] * 3,
+        out_specs=[HBM] * 2,
         out_shape=[
             pltpu.HBM((4, F, C), BF16),
-            pltpu.HBM((4, C, F), BF16),
             pltpu.HBM((4, RANK, C), BF16),
         ],
         scratch_shapes=[
@@ -124,7 +120,6 @@
             pltpu.VMEM((RANK, 4 * C), BF16),
             pltpu.VMEM((4, F // GROUP, C), F32),
             pltpu.VMEM((4, F, C), BF16),
-            pltpu.VMEM((4, C, F), BF16),
             pltpu.VMEM((4, RANK, C), BF16),
             DMA((6,)),
             DMA((6,)),
@@ -135,9 +130,18 @@
     )(*in_hbm(codes, scales, up))
 
 
-def pack_kernel(
-    activ_hbm, flags_hbm, down_hbm, cot_hbm, sent,
-    activ, flags, down_map, cot, first, own, sems, out_sems,
+def lanes_in_order(value):
+    halves = value.reshape(2, 8, 8, T)
+    return jnp.stack([halves[0], halves[1]], axis=1).reshape(GROUP, T)
+
+
+def lanes_by_device(value):
+    value = value.reshape(8, 2, 8, T)
+    return jnp.concatenate([value[:, 0], value[:, 1]], axis=0)
+
+
+def sign_kernel(
+    place, activ_hbm, flags_hbm, down_hbm, cot_hbm, keep, give, activ, flags, down_map, cot, sems
 ):
     pairs = ((activ_hbm, activ), (flags_hbm, flags), (down_hbm, down_map), (cot_hbm, cot))
     copies = [pltpu.make_async_copy(a, b, sems.at[n]) for n, (a, b) in enumerate(pairs)]
@@ -149,54 +153,70 @@
     lane, rank = iota2((RANK, 2 * RANK), 1), iota2((RANK, 2 * RANK), 0)
     left = jnp.where(lane == rank, 1.0, 0.0).astype(BF16)
     right = jnp.where(lane == rank + RANK, 1.0, 0.0).astype(BF16)
-    copies[3].wait()
-    own[...] = dot(apart, cot[...]).astype(BF16)
-    sends = []
-    for q in range(NT):
-        sends.append(pltpu.make_async_copy(own, sent.at[q, 48:304], out_sems.at[q]))
-        sends[q].start()
-    for copy in copies[:3]:
+    for copy in copies:
         copy.wait()
     parts = []
     for h in range(4):
         sign = (2 * flags[h : h + 1, :] - 1).astype(F32)
         diagonal = jnp.where(eye, sign, 0.0).astype(BF16)
-        parts.append(dot(diagonal, activ[GROUP * h : GROUP * (h + 1), :]).reshape(NT, 8, T))
+        parts.append(dot(diagonal, activ[GROUP * h : GROUP * (h + 1), :]))
     for h in (0, 2):
         even = down_map[:, GROUP * h : GROUP * (h + 1)]
         odd = down_map[:, GROUP * (h + 1) : GROUP * (h + 2)]
-        parts.append((dot_00(even, left) + dot_00(odd, right)).reshape(NT, 8, T))
-    first[...] = jnp.concatenate(parts, axis=1).astype(BF16)
-    sends.append(pltpu.make_async_copy(first, sent.at[:, 0:48], out_sems.at[NT]))
-    sends[NT].start()
-    for send in sends:
-        send.wait()
-
-
-def pack(activ, flags, down_t, cot):
-    return pl.pallas_call(
-        pack_kernel,
-        in_specs=[HBM] * 4,
-        out_specs=HBM,
-        out_shape=pltpu.HBM((NT, 304, T), BF16),
+        parts.append(dot_00(even, left) + dot_00(odd, right))
+    parts = [part.reshape(8, 2, 8, T) for part in parts]
+    low, high = (
+        jnp.concatenate([part[:, n] for part in parts], axis=1).reshape(384, T) for n in range(2)
+    )
+    keep[0:384, :] = jnp.where(place[1] == 0, low, high).astype(BF16)
+    give[0:384, :] = jnp.where(place[1] == 0, high, low).astype(BF16)
+    own = dot(apart, cot[...]).astype(BF16)
+    keep[384:640, :] = own
+    give[384:640, :] = own
+
+
+def sign(place, activ, flags, down_t, cot):
+    return pl.pallas_call(
+        sign_kernel,
+        in_specs=[SMEM] + [HBM] * 4,
+        out_specs=[VMEM] * 2,
+        out_shape=[jax.ShapeDtypeStruct((640, T), BF16)] * 2,
         scratch_shapes=[
             pltpu.VMEM((F, T), BF16),
             pltpu.VMEM((4, GROUP), jnp.int32),
             pltpu.VMEM((RANK, F), BF16),
             pltpu.VMEM((O, T), BF16),
-            pltpu.VMEM((NT, 48, T), BF16),
-            pltpu.VMEM((O, T), BF16),
             DMA((4,)),
-            DMA((NT + 1,)),
-        ],
-        compiler_params=PARAMS,
-        cost_estimate=pl.CostEstimate(flops=60_000_000, bytes_accessed=2_000_000, transcendentals=0),
+        ],
+        compiler_params=PARAMS,
+        cost_estimate=pl.CostEstimate(flops=60_000_000, bytes_accessed=600_000, transcendentals=0),
+        name="sign",
+    )(place, *in_hbm(activ, flags, down_t, cot))
+
+
+def pack_kernel(own, other, sent):
+    for n, part in enumerate((own, other)):
+        cot = part[384:640, :]
+        for j in range(8):
+            sent[j, 48 * n : 48 * (n + 1), :] = part[48 * j : 48 * (j + 1), :]
+            sent[j, 96 + 256 * n : 352 + 256 * n, :] = cot
+
+
+def pack(own, other):
+    return pl.pallas_call(
+        pack_kernel,
+        in_specs=[VMEM] * 2,
+        out_specs=VMEM,
+        out_shape=pltpu.VMEM((8, 608, T), BF16),
+        compiler_params=PARAMS,
+        cost_estimate=pl.CostEstimate(flops=0, bytes_accessed=2_000_000, transcendentals=0),
         name="pack",
-    )(*in_hbm(activ, flags, down_t, cot))
+    )(own, other)
 
 
 def turn_kernel(
-    got, weight_hbm, up_hbm, down_hbm, sent, back_out, cot, weight, up_apart, down_t, sems
+    place, got, weight_hbm, up_hbm, down_hbm, sent, back_out,
+    cot, weight, up_apart, down_t, sems,
 ):
     copy_up = pltpu.make_async_copy(up_hbm, up_apart, sems.at[4])
     copy_down = pltpu.make_async_copy(down_hbm, down_t, sems.at[5])
@@ -210,19 +230,27 @@
     copy_down.start()
     for copy in copies:
         copy.start()
-    v = got[:, 0:32, :].astype(F32).reshape(HEADS, 8, T)
-    v = butterfly(v, 6) * 0.125
+    one, two = got[:, 0:48, :].astype(F32), got[:, 48:96, :].astype(F32)
+    low = jnp.where(place[1] == 0, one, two)
+    high = jnp.where(place[1] == 0, two, one)
+    both = jnp.concatenate([low, high], axis=0)
+    v = butterfly(both[:, 0:32].reshape(HEADS, 8, T), 6) * 0.125
     sent[:, 0:32, :] = v.reshape(NT, 32, T).astype(BF16)
     pairs = v.reshape(NT, 2, 2, 8, T)
     even = pairs[:, :, 0].reshape(256, T).astype(BF16)
     odd = pairs[:, :, 1].reshape(256, T).astype(BF16)
-    maps = got[:, 32:48, :].reshape(256, 2 * RANK)
+    maps = both[:, 32:48].reshape(256, 2 * RANK).astype(BF16)
     down = dot_00(maps, even)[0:RANK] + dot_00(maps, odd)[RANK : 2 * RANK]
     down = down.astype(BF16)
     for q in range(NT):
         sent[q, 64:128, :] = down
-        for k in range(4):
-            cot[k, 64 * q : 64 * (q + 1), :] = got[q, 48 + 64 * k : 112 + 64 * k, :]
+    for n in range(2):
+        start = 512 * (place[1] ^ n)
+        for j in range(8):
+            rows = pl.ds(pl.multiple_of(start + 64 * j, 64), 64)
+            for k in range(4):
+                at = 96 + 256 * n + 64 * k
+                cot[k, rows, :] = got[j, at : at + 64, :]
     copy_up.wait()
     copy_down.wait()
     back = jnp.zeros((RANK, T), F32)
@@ -237,18 +265,18 @@
         g = ADAPTER_SCALE * (dot_00(maps, high) + dot_00(maps, low))
         for k in range(4):
             g = g + dot(weight[k, rows, :], cot[k])
-        cot_rows = g.reshape(NT, 8, T)
+        g = lanes_by_device(g)
         if h % 2 == 0:
-            first = cot_rows
+            first = g
         else:
-            both = jnp.concatenate([first, cot_rows], axis=1)
+            both = jnp.concatenate([first, g], axis=1)
             sent[:, 24 + 8 * h : 40 + 8 * h, :] = both.astype(BF16)
 
 
-def turn(got, weight, up_apart, down_t):
+def turn(place, got, weight, up_apart, down_t):
     return pl.pallas_call(
         turn_kernel,
-        in_specs=[VMEM] + [HBM] * 3,
+        in_specs=[SMEM, VMEM] + [HBM] * 3,
         out_specs=[VMEM] * 2,
         out_shape=[
             jax.ShapeDtypeStruct((NT, 128, T), BF16),
@@ -264,13 +292,10 @@
         compiler_params=PARAMS,
         cost_estimate=pl.CostEstimate(flops=600_000_000, bytes_accessed=7_000_000, transcendentals=0),
         name="turn",
-    )(got, *in_hbm(weight, up_apart, down_t))
-
-
-def adapter_kernel(got, back, cot, mixed, down, sums):
-    v = got[:, 0:32, :].astype(F32).reshape(NT, 4, 8, T)
-    for h in range(4):
-        mixed[GROUP * h : GROUP * (h + 1), :] = v[:, h].reshape(GROUP, T).astype(BF16)
+    )(place, got, *in_hbm(weight, up_apart, down_t))
+
+
+def adapter_kernel(got, mixed, back, cot, down, sums):
     total = jnp.sum(got[:, 64:128, :].astype(F32), axis=0)
     down[...] = total
     high, low = split(total)
@@ -284,41 +309,46 @@
         sums[256 + RANK * half : 320 + RANK * half, :] = dot_11(high, c) + dot_11(low, c)
 
 
-def adapter(got, back, cot):
+def adapter(got, mixed, back, cot):
     return pl.pallas_call(
         adapter_kernel,
-        in_specs=[VMEM] * 3,
-        out_specs=[VMEM] * 3,
-        out_shape=[
-            jax.ShapeDtypeStruct((F, T), BF16),
+        in_specs=[VMEM] * 4,
+        out_specs=[VMEM] * 2,
+        out_shape=[
             jax.ShapeDtypeStruct((RANK, T), F32),
             jax.ShapeDtypeStruct((384, T), F32),
         ],
         compiler_params=PARAMS,
         cost_estimate=pl.CostEstimate(flops=30_000_000, bytes_accessed=1_000_000, transcendentals=0),
         name="adapter",
-    )(got, back, cot)
-
-
-def project_kernel(got, mixed, weight_t, sent):
+    )(got, mixed, back, cot)
+
+
+def project_kernel(got, weight, sent, mixed):
+    v = got[:, 0:32, :].astype(F32).reshape(NT, 4, 8, T)
+    for h in range(4):
+        mixed[GROUP * h : GROUP * (h + 1), :] = lanes_in_order(v[:, h]).astype(BF16)
     g = got[:, 32:64, :].astype(F32).reshape(HEADS, 8, T)
     g = butterfly(g, 6) * 0.125
     sent[:, 256:288, :] = g.reshape(NT, 32, T).astype(BF16)
     for k in range(4):
-        share = dot(weight_t[k], mixed[...])
+        share = dot_00(weight[k], mixed[...])
         sent[:, 64 * k : 64 * (k + 1), :] = share.reshape(NT, 64, T).astype(BF16)
 
 
-def project(got, mixed, weight_t):
+def project(got, weight):
     return pl.pallas_call(
         project_kernel,
-        in_specs=[VMEM] * 3,
-        out_specs=VMEM,
-        out_shape=jax.ShapeDtypeStruct((NT, 288, T), BF16),
+        in_specs=[VMEM] * 2,
+        out_specs=[VMEM] * 2,
+        out_shape=[
+            jax.ShapeDtypeStruct((NT, 288, T), BF16),
+            jax.ShapeDtypeStruct((F, T), BF16),
+        ],
         compiler_params=PARAMS,
         cost_estimate=pl.CostEstimate(flops=540_000_000, bytes_accessed=6_000_000, transcendentals=0),
         name="project",
-    )(got, mixed, *in_vmem(weight_t))
+    )(got, *in_vmem(weight))
 
 
 def finish_kernel(place, got, up, down, flags, out, input_gradient, own, sem):
@@ -338,7 +368,7 @@
     for h in range(4):
         sign = (2 * flags[h : h + 1, :] - 1).astype(F32)
         diagonal = jnp.where(eye, sign, 0.0).astype(BF16)
-        part = g[:, h].reshape(GROUP, T).astype(BF16)
+        part = lanes_in_order(g[:, h]).astype(BF16)
         input_gradient[GROUP * h : GROUP * (h + 1), :] = dot(diagonal, part).astype(BF16)
 
 
@@ -407,15 +437,23 @@
 
 def local(activ, flags, codes, scales, down_map, up, cot):
     replica = lax.axis_index("dp")
-    place = jnp.stack([lax.axis_index("tensor")]).astype(jnp.int32)
+    me = lax.axis_index("tensor")
+    place = jnp.stack([me, me >> 3]).astype(jnp.int32)
     flags = flags.reshape(4, GROUP)
     down_t = down_map.T
-    got = exchange(pack(activ, flags, down_t, cot))
-    weight, weight_t, up_apart = make_weights(codes, scales, up)
-    sent, back = turn(got, weight, up_apart, down_t)
+    own, give = sign(place, activ, flags, down_t, cot)
+    other = lax.ppermute(give, "tensor", [(source, source ^ 8) for source in range(NT)])
+    weight, up_apart = make_weights(codes, scales, up)
+    other, weight = lax.optimization_barrier((other, weight))
+    halves = [list(range(8)), list(range(8, NT))]
+    got = lax.all_to_all(
+        pack(own, other), "tensor", 0, 0, tiled=True, axis_index_groups=halves
+    )
+    sent, back = turn(place, got, weight, up_apart, down_t)
     got = exchange(sent)
-    mixed, down, sums = adapter(got, back, cot)
-    got = exchange(project(got, mixed, weight_t))
+    sent, mixed = project(got, weight)
+    down, sums = adapter(got, mixed, back, cot)
+    got = exchange(sent)
     half = lax.dynamic_slice_in_dim(sum_over(sums, (1, 2)), 192 * (replica & 1), 192)
     half = sum_over(half, (4,))
     half = sum_over(half, (12,)).astype(BF16)

time: 108 us -> 107 us (level)
  blocking collectives: 42.1 us -> 62.9 us
  waiting for transfers between devices: 20.8 us -> 2.7 us
  starting transfers between devices: 24.8 us -> 21.7 us
  Pallas kernels: 18.2 us -> 16.9 us
    all_to_all x0 -> x1, blocking collectives: none -> 20.6 us  [local(): lax.all_to_all(pack(own, other), 'tensor', 0, 0, tiled=True, axis_index_g...]
    all_to_all x2 -> x1, waiting for transfers between devices: 20.4 us -> 0.01 us  [exchange(): return lax.all_to_all(value, 'tensor', 0, 0, tiled=True)]
    all_to_all x2 -> x1, starting transfers between devices: 16.6 us -> 6.51 us  [exchange(): return lax.all_to_all(value, 'tensor', 0, 0, tiled=True)]
    ppermute x0 -> x1, starting transfers between devices: none -> 6.09 us  [local(): lax.ppermute(give, 'tensor', [(source, source ^ 8) for source in range(NT)])]
    ppermute x0 -> x1, waiting for transfers between devices: none -> 2.69 us  [local(): lax.ppermute(give, 'tensor', [(source, source ^ 8) for source in range(NT)])]
    pallas_call x5 -> x6, Pallas kernels: 15.8 us -> 13.9 us  [the longest x1 5 us: make_weights(): pl.pallas_call(weights_kernel, in_specs=[HBM] * 3, out_specs=[HBM] * 2, o...]
  transfers between devices with their start and end apart: 3 -> 3, of which waited for: 2 -> 1; matrix products, arithmetic and copies ran while one was open for 0% -> 0% of each run, Pallas kernels for 8% -> 7%
where the time goes in v5:
time: 107 us; the launch traced here: 105 us
  blocking collectives  62.9 us (59%)
  starting transfers between devices  21.7 us (20%)
  Pallas kernels  16.9 us (16%)
  waiting for transfers between devices  2.7 us (3%)
    all_gather x4, blocking collectives, gather(): lax.all_gather(value, 'dp', axis=0, axis_index_groups=list(groups.values()))  22.1 us
    all_to_all x1, blocking collectives, local(): lax.all_to_all(pack(own, other), 'tensor', 0, 0, tiled=True, axis_index_g...  20.6 us
    all_to_all x1, blocking collectives, exchange(): return lax.all_to_all(value, 'tensor', 0, 0, tiled=True)  20.2 us
    ppermute x1, starting transfers between devices, local(): other = lax.ppermute(half, 'dp', pairs)  9.12 us
    all_to_all x1, starting transfers between devices, exchange(): return lax.all_to_all(value, 'tensor', 0, 0, tiled=True)  6.51 us
    ppermute x1, starting transfers between devices, local(): lax.ppermute(give, 'tensor', [(source, source ^ 8) for source in range(NT)])  6.09 us
    pallas_call x1, Pallas kernels, make_weights(): pl.pallas_call(weights_kernel, in_specs=[HBM] * 3, out_specs=[HBM] * 2, o...  5 us
    pallas_call x1, Pallas kernels, turn(): pl.pallas_call(turn_kernel, in_specs=[SMEM, VMEM] + [HBM] * 3, out_specs=...  4.2 us
  transfers between devices with their start and end apart: 3, of which 1 were waited for; matrix products, arithmetic and copies ran while one was open for 0% of the time, Pallas kernels for 7%

profile of v5, /device:TPU:6, one launch (start us, length us, event | category | flops | bytes accessed | tf_op | source)
XLA Modules:
  0.0 105.2 jit_solution(12443888991954679111)
XLA Ops:
  0.6 0.1 pad_add_fusion.place
  0.7 1.8 %sign.1 = (bf16[640,128]{1,0:T(8,128)(2,1)S(1)}, bf16[640,128]{1,0:T(8,128)(2,1)S(1)}) custom-call(s32[2]{0:T(128)S(1)} %pad_add_fusion.place, bf16[512,128]{1,0:T(8,128)(2,1)} %activ_hbm.1, s32[4,128]{1,0:T(4,128)} %bitcast.11, bf16[64,512]{1,0:T(8,128)(2,1)} %bitcast.13, bf16[256,128]{1,0:T(8,128)(2,1)} %cot.1), custom_call_target="tpu_custom_call" | custom-call | flops 60000000 | bytes 600000 | tf_op jit(solution)/shard_map/sign/pallas_call | solution.py:179
  2.5 6.1 %collective-permute-start = (bf16[640,128]{1,0:T(8,128)(2,1)S(1)}, bf16[640,128]{1,0:T(8,128)(2,1)S(1)}, u32[]{:S(2)}, u32[]{:S(2)}) collective-permute-start(bf16[640,128]{1,0:T(8,128)(2,1)S(1)} %get-tuple-element.24), channel_id=1, source_target_pairs={{0,8},{1,9},{2,10},{3,11},{4,12},{5,13},{6,14},{7,15},{8,0},{9,1},... | collective-permute-start | bytes 491528 | tf_op jit(solution)/shard_map/ppermute | solution.py:445
  8.6 5.0 %weights.1 = (bf16[4,512,1024]{2,1,0:T(8,128)(2,1)}, bf16[4,64,1024]{2,1,0:T(8,128)(2,1)}) custom-call(s32[512,1024]{1,0:T(8,128)} %codes_hbm.1, bf16[4,4096]{1,0:T(4,128)(2,1)} %scales_hbm.1, bf16[64,4096]{1,0:T(8,128)(2,1)} %up.1), custom_call_target="tpu_custom_call" | custom-call | flops 20000000 | bytes 20000000 | tf_op jit(solution)/shard_map/weights/pallas_call | solution.py:109
  13.6 2.7 %collective-permute-done.other = bf16[640,128]{1,0:T(8,128)(2,1)S(1)} collective-permute-done((bf16[640,128]{1,0:T(8,128)(2,1)S(1)}, bf16[640,128]{1,0:T(8,128)(2,1)S(1)}, u32[]{:S(2)}, u32[]{:S(2)}) %collective-permute-start) | collective-permute-done | bytes 163872 | tf_op jit(solution)/shard_map/ppermute | solution.py:445
  16.3 0.1 pack.1
  16.5 20.6 %all_to_all.15.got = bf16[8,608,128]{2,1,0:T(8,128)(2,1)S(1)} all-to-all(bf16[8,608,128]{2,1,0:T(8,128)(2,1)S(1)} %pack.1), channel_id=1, replica_groups={{0,1,2,3,4,5,6,7},{8,9,10,11,12,13,14,15},{16,17,18,19,20,21,22,23},{24..., dimensions={0} | all-to-all | bytes 2490368 | tf_op jit(solution)/shard_map/all_to_all | solution.py:449
  37.0 0.0 copy-start
  37.0 4.2 %turn.1 = (bf16[16,128,128]{2,1,0:T(8,128)(2,1)S(1)}, f32[64,128]{1,0:T(8,128)S(1)}) custom-call(s32[2]{0:T(128)S(1)} %pad_add_fusion.place, bf16[8,608,128]{2,1,0:T(8,128)(2,1)S(1)} %all_to_all.15.got, bf16[4,512,1024]{2,1,0:T(8,128)(2,1)} %get-tuple-element.27.weight_hbm.weight, bf16[4,64,1024]{2,1,0:T(8,128)(2,1)} %get-tuple-element.28.up_hbm, ...), custom_call_target="tpu_custom_call" | custom-call | flops 600000000 | bytes 7000000 | tf_op jit(solution)/shard_map/turn/pallas_call | solution.py:277
  41.3 20.2 %all_to_all.16.got = bf16[16,128,128]{2,1,0:T(8,128)(2,1)S(1)} all-to-all(bf16[16,128,128]{2,1,0:T(8,128)(2,1)S(1)} %get-tuple-element.29), channel_id=1, replica_groups=mesh['dp'=32,'tensor'=16] {'tensor'}, dimensions={0} | all-to-all | bytes 1048576 | tf_op jit(solution)/shard_map/all_to_all | solution.py:417
  61.5 0.0 copy-done
  61.5 2.5 %project.1 = (bf16[16,288,128]{2,1,0:T(8,128)(2,1)}, bf16[512,128]{1,0:T(8,128)(2,1)S(1)}) custom-call(bf16[16,128,128]{2,1,0:T(8,128)(2,1)S(1)} %all_to_all.16.got, bf16[4,512,1024]{2,1,0:T(8,128)(2,1)S(1)} %copy-done), custom_call_target="tpu_custom_call" | custom-call | flops 540000000 | bytes 6000000 | tf_op jit(solution)/shard_map/project/pallas_call | solution.py:340
  63.9 0.0 copy-start.1
  63.9 6.5 %all-to-all-start.2 = ((bf16[16,288,128]{2,1,0:T(8,128)(2,1)}), bf16[16,288,128]{2,1,0:T(8,128)(2,1)S(1)}, u32[]{:S(2)}, u32[]{:S(2)}) async-start(bf16[16,288,128]{2,1,0:T(8,128)(2,1)} %get-tuple-element.33), calls=%async_computation.2 | async-start | bytes 2359296 | tf_op jit(solution)/shard_map/all_to_all | solution.py:417
  70.4 0.0 copy-done.1
  70.5 0.4 adapter.1
  70.8 0.0 copy-start.2
  70.8 6.5 %all-gather = bf16[1536,128]{1,0:T(8,128)(2,1)S(1)} all-gather(bf16[384,128]{1,0:T(8,128)(2,1)S(1)} %convert_element_type.55), channel_id=2, replica_groups={{0,16,32,48},{64,80,96,112},{128,144,160,176},{192,208,224,240},{256,27..., dimensions={0}, use_global_device_ids=true | all-gather | bytes 491520 | tf_op jit(solution)/shard_map/all_gather | solution.py:427
  77.5 6.7 %all_gather.22 = bf16[2,192,128]{2,1,0:T(8,128)(2,1)S(1)} all-gather(bf16[1,192,128]{2,1,0:T(8,128)(2,1)S(1)} %fusion.1), channel_id=1, replica_groups={{0,64},{16,80},{32,96},{48,112},{128,192},{144,208},{160,224},{176,240}..., dimensions={0}, use_global_device_ids=true | all-gather | bytes 147456 | tf_op jit(solution)/shard_map/all_gather | solution.py:427
  84.2 6.9 %all_gather.23 = bf16[2,192,128]{2,1,0:T(8,128)(2,1)S(1)} all-gather(bf16[1,192,128]{2,1,0:T(8,128)(2,1)S(1)} %add_convert_fusion.2), channel_id=1, replica_groups={{0,192},{16,208},{32,224},{48,240},{64,128},{80,144},{96,160},{112,176}..., dimensions={0}, use_global_device_ids=true | all-gather | bytes 147456 | tf_op jit(solution)/shard_map/all_gather | solution.py:427
  91.1 9.1 %collective-permute-start.1 = (bf16[192,128]{1,0:T(8,128)(2,1)S(1)}, bf16[192,128]{1,0:T(8,128)(2,1)S(1)}, u32[]{:S(2)}, u32[]{:S(2)}) collective-permute-start(bf16[192,128]{1,0:T(8,128)(2,1)S(1)} %fusion), channel_id=1, source_target_pairs={{0,256},{16,272},{32,288},{48,304},{64,320},{80,336},{96,352},{112... | collective-permute-start | bytes 147464 | tf_op jit(solution)/shard_map/ppermute | solution.py:461
  100.2 0.0 all-to-all-done.2.got
  100.2 0.0 copy-done.2
  100.2 2.3 %finish.1 = (bf16[256,128]{1,0:T(8,128)(2,1)}, bf16[512,128]{1,0:T(8,128)(2,1)}) custom-call(s32[2]{0:T(128)S(1)} %pad_add_fusion.place, bf16[16,288,128]{2,1,0:T(8,128)(2,1)S(1)} %all-to-all-done.2.got, bf16[64,4096]{1,0:T(8,128)(2,1)} %up.1, f32[64,128]{1,0:T(8,128)S(1)} %get-tuple-element.34.down, s32[4,128]{1,0:T(4,128)S(1)} %bitcast.12), custom_call_target="tpu_custom_call" | custom-call | flops 40000000 | bytes 1700000 | tf_op jit(solution)/shard_map/finish/pallas_call | solution.py:376
  102.6 0.0 collective-permute-done.1
  102.6 1.9 %all-gather.1.sums = f32[384,128]{1,0:T(8,128)S(1)} all-gather(f32[192,128]{1,0:T(8,128)S(1)} %convert_add_fusion), channel_id=3, replica_groups={{0,16},{32,48},{64,80},{96,112},{128,144},{160,176},{192,208},{224,240}..., dimensions={0}, use_global_device_ids=true | all-gather | bytes 294912 | tf_op jit(solution)/shard_map/all_gather | solution.py:427
  104.5 0.7 gradients.1
  (6 shorter events, 0.1 us)
Async XLA Ops:
  2.5 13.8 %collective-permute-start = (bf16[640,128]{1,0:T(8,128)(2,1)S(1)}, bf16[640,128]{1,0:T(8,128)(2,1)S(1)}, u32[]{:S(2)}, u32[]{:S(2)}) collective-permute-start(bf16[640,128]{1,0:T(8,128)(2,1)S(1)} %get-tuple-element.24), channel_id=1, source_target_pairs={{0,8},{1,9},{2,10},{3,11},{4,12},{5,13},{6,14},{7,15},{8,0},{9,1},... | collective-permute-start | bytes 491528 | tf_op jit(solution)/shard_map/ppermute | solution.py:445
  37.0 24.4 %copy-start = (bf16[4,512,1024]{2,1,0:T(8,128)(2,1)S(1)}, bf16[4,512,1024]{2,1,0:T(8,128)(2,1)}, u32[]{:S(2)}) copy-start(bf16[4,512,1024]{2,1,0:T(8,128)(2,1)} %get-tuple-element.27.weight_hbm.weight) | copy-start | bytes 12582916
  63.9 6.5 %copy-start.1 = (bf16[256,128]{1,0:T(8,128)(2,1)S(1)}, bf16[256,128]{1,0:T(8,128)(2,1)}, u32[]{:S(2)}) copy-start(bf16[256,128]{1,0:T(8,128)(2,1)} %cot.1) | copy-start | bytes 196612
  63.9 36.3 %all-to-all-start.2 = ((bf16[16,288,128]{2,1,0:T(8,128)(2,1)}), bf16[16,288,128]{2,1,0:T(8,128)(2,1)S(1)}, u32[]{:S(2)}, u32[]{:S(2)}) async-start(bf16[16,288,128]{2,1,0:T(8,128)(2,1)} %get-tuple-element.33), calls=%async_computation.2 | async-start | bytes 2359296 | tf_op jit(solution)/shard_map/all_to_all | solution.py:417
  70.8 29.4 %copy-start.2 = (s32[512]{0:T(512)S(1)}, s32[512]{0:T(512)}, u32[]{:S(2)}) copy-start(s32[512]{0:T(512)} %param.8) | copy-start | bytes 6148
  91.1 11.5 %collective-permute-start.1 = (bf16[192,128]{1,0:T(8,128)(2,1)S(1)}, bf16[192,128]{1,0:T(8,128)(2,1)S(1)}, u32[]{:S(2)}, u32[]{:S(2)}) collective-permute-start(bf16[192,128]{1,0:T(8,128)(2,1)S(1)} %fusion), channel_id=1, source_target_pairs={{0,256},{16,272},{32,288},{48,304},{64,320},{80,336},{96,352},{112... | collective-permute-start | bytes 147464 | tf_op jit(solution)/shard_map/ppermute | solution.py:461

commit v6 on v5

--- a/solution.py
+++ b/solution.py
@@ -63,8 +63,8 @@
 
 
 def weights_kernel(
-    codes_hbm, scales_hbm, up_hbm, weight_out, up_out,
-    codes, scales, up, scales_apart, weight, up_apart, sems, out_sems,
+    codes_hbm, scales_hbm, up_hbm, weight, up_apart,
+    codes, scales, up, scales_apart, sems,
 ):
     copy_scales = pltpu.make_async_copy(scales_hbm, scales, sems.at[4])
     copy_up = pltpu.make_async_copy(up_hbm, up, sems.at[5])
@@ -88,8 +88,6 @@
             to = slice(128 * block, 128 * (block + 1))
             scales_apart[k, :, to] = s[:, 128 * k : 128 * (k + 1)]
             up_apart[k, :, to] = u[:, 128 * k : 128 * (k + 1)]
-    sends = [pltpu.make_async_copy(up_apart, up_out, out_sems.at[5])]
-    sends[0].start()
     for g in range(4):
         copies[g].wait()
         rows = slice(GROUP * g, GROUP * (g + 1))
@@ -97,31 +95,22 @@
             nibble = ((codes[rows, :] >> (4 * k)) & 15) - 8
             part = nibble.astype(F32) * scales_apart[k, g : g + 1, :]
             weight[k, rows, :] = part.astype(BF16)
-        sends.append(
-            pltpu.make_async_copy(weight.at[:, rows], weight_out.at[:, rows], out_sems.at[g])
-        )
-        sends[g + 1].start()
-    for send in sends:
-        send.wait()
 
 
 def make_weights(codes, scales, up):
     return pl.pallas_call(
         weights_kernel,
         in_specs=[HBM] * 3,
-        out_specs=[HBM] * 2,
-        out_shape=[
-            pltpu.HBM((4, F, C), BF16),
-            pltpu.HBM((4, RANK, C), BF16),
+        out_specs=[VMEM] * 2,
+        out_shape=[
+            pltpu.VMEM((4, F, C), BF16),
+            pltpu.VMEM((4, RANK, C), BF16),
         ],
         scratch_shapes=[
             pltpu.VMEM((F, C), jnp.int32),
             pltpu.VMEM((F // GROUP, 4 * C), BF16),
             pltpu.VMEM((RANK, 4 * C), BF16),
             pltpu.VMEM((4, F // GROUP, C), F32),
-            pltpu.VMEM((4, F, C), BF16),
-            pltpu.VMEM((4, RANK, C), BF16),
-            DMA((6,)),
             DMA((6,)),
         ],
         compiler_params=PARAMS,
@@ -214,22 +203,9 @@
     )(own, other)
 
 
-def turn_kernel(
-    place, got, weight_hbm, up_hbm, down_hbm, sent, back_out,
-    cot, weight, up_apart, down_t, sems,
-):
-    copy_up = pltpu.make_async_copy(up_hbm, up_apart, sems.at[4])
-    copy_down = pltpu.make_async_copy(down_hbm, down_t, sems.at[5])
-    copies = []
-    for h in range(4):
-        rows = slice(GROUP * h, GROUP * (h + 1))
-        copies.append(
-            pltpu.make_async_copy(weight_hbm.at[:, rows], weight.at[:, rows], sems.at[h])
-        )
-    copy_up.start()
+def turn_kernel(place, got, weight, up_apart, down_hbm, sent, back_out, cot, down_t, sem):
+    copy_down = pltpu.make_async_copy(down_hbm, down_t, sem)
     copy_down.start()
-    for copy in copies:
-        copy.start()
     one, two = got[:, 0:48, :].astype(F32), got[:, 48:96, :].astype(F32)
     low = jnp.where(place[1] == 0, one, two)
     high = jnp.where(place[1] == 0, two, one)
@@ -251,7 +227,6 @@
             for k in range(4):
                 at = 96 + 256 * n + 64 * k
                 cot[k, rows, :] = got[j, at : at + 64, :]
-    copy_up.wait()
     copy_down.wait()
     back = jnp.zeros((RANK, T), F32)
     for k in range(4):
@@ -260,7 +235,6 @@
     high, low = split(back)
     for h in range(4):
         rows = slice(GROUP * h, GROUP * (h + 1))
-        copies[h].wait()
         maps = down_t[:, rows]
         g = ADAPTER_SCALE * (dot_00(maps, high) + dot_00(maps, low))
         for k in range(4):
@@ -276,7 +250,7 @@
 def turn(place, got, weight, up_apart, down_t):
     return pl.pallas_call(
         turn_kernel,
-        in_specs=[SMEM, VMEM] + [HBM] * 3,
+        in_specs=[SMEM] + [VMEM] * 3 + [HBM],
         out_specs=[VMEM] * 2,
         out_shape=[
             jax.ShapeDtypeStruct((NT, 128, T), BF16),
@@ -284,15 +258,13 @@
         ],
         scratch_shapes=[
             pltpu.VMEM((4, C, T), BF16),
-            pltpu.VMEM((4, F, C), BF16),
-            pltpu.VMEM((4, RANK, C), BF16),
             pltpu.VMEM((RANK, F), BF16),
-            DMA((6,)),
+            DMA(()),
         ],
         compiler_params=PARAMS,
         cost_estimate=pl.CostEstimate(flops=600_000_000, bytes_accessed=7_000_000, transcendentals=0),
         name="turn",
-    )(place, got, *in_hbm(weight, up_apart, down_t))
+    )(place, got, *in_vmem(weight, up_apart), *in_hbm(down_t))
 
 
 def adapter_kernel(got, mixed, back, cot, down, sums):

time: 107 us -> 105 us (0.981)
  Pallas kernels: 16.9 us -> 14.8 us
    pallas_call x2, Pallas kernels: 9.2 us -> 7.02 us  [the longest x1 3.95 us: make_weights(): pl.pallas_call(weights_kernel, in_specs=[HBM] * 3, out_specs=[VMEM] * 2,...]
  transfers between devices with their start and end apart: 3 -> 3, of which waited for: 1 -> 1; matrix products, arithmetic and copies ran while one was open for 0% -> 0% of each run, Pallas kernels for 7% -> 6%
where the time goes in v6:
time: 105 us; the launch traced here: 104 us
  blocking collectives  62.9 us (60%)
  starting transfers between devices  21.7 us (21%)
  Pallas kernels  14.8 us (14%)
  waiting for transfers between devices  3.74 us (4%)
    all_gather x4, blocking collectives, gather(): lax.all_gather(value, 'dp', axis=0, axis_index_groups=list(groups.values()))  22.1 us
    all_to_all x1, blocking collectives, local(): lax.all_to_all(pack(own, other), 'tensor', 0, 0, tiled=True, axis_index_g...  20.6 us
    all_to_all x1, blocking collectives, exchange(): return lax.all_to_all(value, 'tensor', 0, 0, tiled=True)  20.2 us
    ppermute x1, starting transfers between devices, local(): other = lax.ppermute(half, 'dp', pairs)  9.12 us
    all_to_all x1, starting transfers between devices, exchange(): return lax.all_to_all(value, 'tensor', 0, 0, tiled=True)  6.52 us
    ppermute x1, starting transfers between devices, local(): lax.ppermute(give, 'tensor', [(source, source ^ 8) for source in range(NT)])  6.09 us
    pallas_call x1, Pallas kernels, make_weights(): pl.pallas_call(weights_kernel, in_specs=[HBM] * 3, out_specs=[VMEM] * 2,...  3.95 us
    ppermute x1, waiting for transfers between devices, local(): lax.ppermute(give, 'tensor', [(source, source ^ 8) for source in range(NT)])  3.74 us
  transfers between devices with their start and end apart: 3, of which 1 were waited for; matrix products, arithmetic and copies ran while one was open for 0% of the time, Pallas kernels for 6%

profile of v6, /device:TPU:6, one launch (start us, length us, event | category | flops | bytes accessed | tf_op | source)
XLA Modules:
  0.0 104.1 jit_solution(8458289795059945575)
XLA Ops:
  0.6 0.1 pad_add_fusion.place
  0.7 1.8 %sign.1 = (bf16[640,128]{1,0:T(8,128)(2,1)S(1)}, bf16[640,128]{1,0:T(8,128)(2,1)S(1)}) custom-call(s32[2]{0:T(128)S(1)} %pad_add_fusion.place, bf16[512,128]{1,0:T(8,128)(2,1)} %activ_hbm.1, s32[4,128]{1,0:T(4,128)} %bitcast.11, bf16[64,512]{1,0:T(8,128)(2,1)} %bitcast.13, bf16[256,128]{1,0:T(8,128)(2,1)} %cot.1), custom_call_target="tpu_custom_call" | custom-call | flops 60000000 | bytes 600000 | tf_op jit(solution)/shard_map/sign/pallas_call | solution.py:168
  2.5 6.1 %collective-permute-start = (bf16[640,128]{1,0:T(8,128)(2,1)S(1)}, bf16[640,128]{1,0:T(8,128)(2,1)S(1)}, u32[]{:S(2)}, u32[]{:S(2)}) collective-permute-start(bf16[640,128]{1,0:T(8,128)(2,1)S(1)} %get-tuple-element.24), channel_id=1, source_target_pairs={{0,8},{1,9},{2,10},{3,11},{4,12},{5,13},{6,14},{7,15},{8,0},{9,1},... | collective-permute-start | bytes 491528 | tf_op jit(solution)/shard_map/ppermute | solution.py:417
  8.6 4.0 %weights.1 = (bf16[4,512,1024]{2,1,0:T(8,128)(2,1)S(1)}, bf16[4,64,1024]{2,1,0:T(8,128)(2,1)S(1)}) custom-call(s32[512,1024]{1,0:T(8,128)} %codes_hbm.1, bf16[4,4096]{1,0:T(4,128)(2,1)} %scales_hbm.1, bf16[64,4096]{1,0:T(8,128)(2,1)} %up.1), custom_call_target="tpu_custom_call" | custom-call | flops 20000000 | bytes 20000000 | tf_op jit(solution)/shard_map/weights/pallas_call | solution.py:101
  12.6 3.7 %collective-permute-done.other = bf16[640,128]{1,0:T(8,128)(2,1)S(1)} collective-permute-done((bf16[640,128]{1,0:T(8,128)(2,1)S(1)}, bf16[640,128]{1,0:T(8,128)(2,1)S(1)}, u32[]{:S(2)}, u32[]{:S(2)}) %collective-permute-start) | collective-permute-done | bytes 163872 | tf_op jit(solution)/shard_map/ppermute | solution.py:417
  16.3 0.1 pack.1
  16.5 20.6 %all_to_all.15.got = bf16[8,608,128]{2,1,0:T(8,128)(2,1)S(1)} all-to-all(bf16[8,608,128]{2,1,0:T(8,128)(2,1)S(1)} %pack.1), channel_id=1, replica_groups={{0,1,2,3,4,5,6,7},{8,9,10,11,12,13,14,15},{16,17,18,19,20,21,22,23},{24..., dimensions={0} | all-to-all | bytes 2490368 | tf_op jit(solution)/shard_map/all_to_all | solution.py:421
  37.0 3.1 %turn.1 = (bf16[16,128,128]{2,1,0:T(8,128)(2,1)S(1)}, f32[64,128]{1,0:T(8,128)S(1)}) custom-call(s32[2]{0:T(128)S(1)} %pad_add_fusion.place, bf16[8,608,128]{2,1,0:T(8,128)(2,1)S(1)} %all_to_all.15.got, bf16[4,512,1024]{2,1,0:T(8,128)(2,1)S(1)} %get-tuple-element.27.weight, bf16[4,64,1024]{2,1,0:T(8,128)(2,1)S(1)} %get-tuple-element.28.up_apart, ...), custom_call_target="tpu_custom_call" | custom-call | flops 600000000 | bytes 7000000 | tf_op jit(solution)/shard_map/turn/pallas_call | solution.py:251
  40.1 20.2 %all_to_all.16.got = bf16[16,128,128]{2,1,0:T(8,128)(2,1)S(1)} all-to-all(bf16[16,128,128]{2,1,0:T(8,128)(2,1)S(1)} %get-tuple-element.29), channel_id=1, replica_groups=mesh['dp'=32,'tensor'=16] {'tensor'}, dimensions={0} | all-to-all | bytes 1048576 | tf_op jit(solution)/shard_map/all_to_all | solution.py:389
  60.3 2.5 %project.1 = (bf16[16,288,128]{2,1,0:T(8,128)(2,1)}, bf16[512,128]{1,0:T(8,128)(2,1)S(1)}) custom-call(bf16[16,128,128]{2,1,0:T(8,128)(2,1)S(1)} %all_to_all.16.got, bf16[4,512,1024]{2,1,0:T(8,128)(2,1)S(1)} %get-tuple-element.27.weight), custom_call_target="tpu_custom_call" | custom-call | flops 540000000 | bytes 6000000 | tf_op jit(solution)/shard_map/project/pallas_call | solution.py:312
  62.8 0.0 copy-start
  62.8 6.5 %all-to-all-start.2 = ((bf16[16,288,128]{2,1,0:T(8,128)(2,1)}), bf16[16,288,128]{2,1,0:T(8,128)(2,1)S(1)}, u32[]{:S(2)}, u32[]{:S(2)}) async-start(bf16[16,288,128]{2,1,0:T(8,128)(2,1)} %get-tuple-element.33), calls=%async_computation.2 | async-start | bytes 2359296 | tf_op jit(solution)/shard_map/all_to_all | solution.py:389
  69.3 0.0 copy-done
  69.4 0.4 adapter.1
  69.7 0.0 copy-start.1
  69.8 6.5 %all-gather = bf16[1536,128]{1,0:T(8,128)(2,1)S(1)} all-gather(bf16[384,128]{1,0:T(8,128)(2,1)S(1)} %convert_element_type.55), channel_id=2, replica_groups={{0,16,32,48},{64,80,96,112},{128,144,160,176},{192,208,224,240},{256,27..., dimensions={0}, use_global_device_ids=true | all-gather | bytes 491520 | tf_op jit(solution)/shard_map/all_gather | solution.py:399
  76.4 6.7 %all_gather.22 = bf16[2,192,128]{2,1,0:T(8,128)(2,1)S(1)} all-gather(bf16[1,192,128]{2,1,0:T(8,128)(2,1)S(1)} %fusion.1), channel_id=1, replica_groups={{0,64},{16,80},{32,96},{48,112},{128,192},{144,208},{160,224},{176,240}..., dimensions={0}, use_global_device_ids=true | all-gather | bytes 147456 | tf_op jit(solution)/shard_map/all_gather | solution.py:399
  83.1 6.9 %all_gather.23 = bf16[2,192,128]{2,1,0:T(8,128)(2,1)S(1)} all-gather(bf16[1,192,128]{2,1,0:T(8,128)(2,1)S(1)} %add_convert_fusion.2), channel_id=1, replica_groups={{0,192},{16,208},{32,224},{48,240},{64,128},{80,144},{96,160},{112,176}..., dimensions={0}, use_global_device_ids=true | all-gather | bytes 147456 | tf_op jit(solution)/shard_map/all_gather | solution.py:399
  90.0 9.1 %collective-permute-start.1 = (bf16[192,128]{1,0:T(8,128)(2,1)S(1)}, bf16[192,128]{1,0:T(8,128)(2,1)S(1)}, u32[]{:S(2)}, u32[]{:S(2)}) collective-permute-start(bf16[192,128]{1,0:T(8,128)(2,1)S(1)} %fusion), channel_id=1, source_target_pairs={{0,256},{16,272},{32,288},{48,304},{64,320},{80,336},{96,352},{112... | collective-permute-start | bytes 147464 | tf_op jit(solution)/shard_map/ppermute | solution.py:433
  99.1 0.0 all-to-all-done.2.got
  99.1 0.0 copy-done.1
  99.1 2.3 %finish.1 = (bf16[256,128]{1,0:T(8,128)(2,1)}, bf16[512,128]{1,0:T(8,128)(2,1)}) custom-call(s32[2]{0:T(128)S(1)} %pad_add_fusion.place, bf16[16,288,128]{2,1,0:T(8,128)(2,1)S(1)} %all-to-all-done.2.got, bf16[64,4096]{1,0:T(8,128)(2,1)} %up.1, f32[64,128]{1,0:T(8,128)S(1)} %get-tuple-element.34.down, s32[4,128]{1,0:T(4,128)S(1)} %bitcast.12), custom_call_target="tpu_custom_call" | custom-call | flops 40000000 | bytes 1700000 | tf_op jit(solution)/shard_map/finish/pallas_call | solution.py:348
  101.5 0.0 collective-permute-done.1
  101.5 1.9 %all-gather.1.sums = f32[384,128]{1,0:T(8,128)S(1)} all-gather(f32[192,128]{1,0:T(8,128)S(1)} %convert_add_fusion), channel_id=3, replica_groups={{0,16},{32,48},{64,80},{96,112},{128,144},{160,176},{192,208},{224,240}..., dimensions={0}, use_global_device_ids=true | all-gather | bytes 294912 | tf_op jit(solution)/shard_map/all_gather | solution.py:399
  103.4 0.7 gradients.1
  (6 shorter events, 0.1 us)
Async XLA Ops:
  2.5 13.8 %collective-permute-start = (bf16[640,128]{1,0:T(8,128)(2,1)S(1)}, bf16[640,128]{1,0:T(8,128)(2,1)S(1)}, u32[]{:S(2)}, u32[]{:S(2)}) collective-permute-start(bf16[640,128]{1,0:T(8,128)(2,1)S(1)} %get-tuple-element.24), channel_id=1, source_target_pairs={{0,8},{1,9},{2,10},{3,11},{4,12},{5,13},{6,14},{7,15},{8,0},{9,1},... | collective-permute-start | bytes 491528 | tf_op jit(solution)/shard_map/ppermute | solution.py:417
  62.8 6.5 %copy-start = (bf16[256,128]{1,0:T(8,128)(2,1)S(1)}, bf16[256,128]{1,0:T(8,128)(2,1)}, u32[]{:S(2)}) copy-start(bf16[256,128]{1,0:T(8,128)(2,1)} %cot.1) | copy-start | bytes 196612
  62.8 36.3 %all-to-all-start.2 = ((bf16[16,288,128]{2,1,0:T(8,128)(2,1)}), bf16[16,288,128]{2,1,0:T(8,128)(2,1)S(1)}, u32[]{:S(2)}, u32[]{:S(2)}) async-start(bf16[16,288,128]{2,1,0:T(8,128)(2,1)} %get-tuple-element.33), calls=%async_computation.2 | async-start | bytes 2359296 | tf_op jit(solution)/shard_map/all_to_all | solution.py:389
  69.7 29.4 %copy-start.1 = (s32[512]{0:T(512)S(1)}, s32[512]{0:T(512)}, u32[]{:S(2)}) copy-start(s32[512]{0:T(512)} %param.8) | copy-start | bytes 6148
  90.0 11.5 %collective-permute-start.1 = (bf16[192,128]{1,0:T(8,128)(2,1)S(1)}, bf16[192,128]{1,0:T(8,128)(2,1)S(1)}, u32[]{:S(2)}, u32[]{:S(2)}) collective-permute-start(bf16[192,128]{1,0:T(8,128)(2,1)S(1)} %fusion), channel_id=1, source_target_pairs={{0,256},{16,272},{32,288},{48,304},{64,320},{80,336},{96,352},{112... | collective-permute-start | bytes 147464 | tf_op jit(solution)/shard_map/ppermute | solution.py:433

commit v7 on v6

--- a/solution.py
+++ b/solution.py
@@ -157,8 +157,8 @@
     low, high = (
         jnp.concatenate([part[:, n] for part in parts], axis=1).reshape(384, T) for n in range(2)
     )
-    keep[0:384, :] = jnp.where(place[1] == 0, low, high).astype(BF16)
-    give[0:384, :] = jnp.where(place[1] == 0, high, low).astype(BF16)
+    keep[0:384, :] = jnp.where(place[0] < 8, low, high).astype(BF16)
+    give[0:384, :] = jnp.where(place[0] < 8, high, low).astype(BF16)
     own = dot(apart, cot[...]).astype(BF16)
     keep[384:640, :] = own
     give[384:640, :] = own
@@ -207,8 +207,8 @@
     copy_down = pltpu.make_async_copy(down_hbm, down_t, sem)
     copy_down.start()
     one, two = got[:, 0:48, :].astype(F32), got[:, 48:96, :].astype(F32)
-    low = jnp.where(place[1] == 0, one, two)
-    high = jnp.where(place[1] == 0, two, one)
+    low = jnp.where(place[0] < 8, one, two)
+    high = jnp.where(place[0] < 8, two, one)
     both = jnp.concatenate([low, high], axis=0)
     v = butterfly(both[:, 0:32].reshape(HEADS, 8, T), 6) * 0.125
     sent[:, 0:32, :] = v.reshape(NT, 32, T).astype(BF16)
@@ -221,7 +221,7 @@
     for q in range(NT):
         sent[q, 64:128, :] = down
     for n in range(2):
-        start = 512 * (place[1] ^ n)
+        start = 512 * ((place[0] >> 3) ^ n)
         for j in range(8):
             rows = pl.ds(pl.multiple_of(start + 64 * j, 64), 64)
             for k in range(4):
@@ -410,7 +410,7 @@
 def local(activ, flags, codes, scales, down_map, up, cot):
     replica = lax.axis_index("dp")
     me = lax.axis_index("tensor")
-    place = jnp.stack([me, me >> 3]).astype(jnp.int32)
+    place = me.reshape(1)
     flags = flags.reshape(4, GROUP)
     down_t = down_map.T
     own, give = sign(place, activ, flags, down_t, cot)

time: 105 us -> 104 us (level)
  Pallas kernels: 14.8 us -> 13.2 us
  transfers between devices with their start and end apart: 3 -> 3, of which waited for: 1 -> 2; matrix products, arithmetic and copies ran while one was open for 0% -> 0% of each run, Pallas kernels for 6% -> 6%
where the time goes in v7:
time: 104 us; the launch traced here: 103 us
  blocking collectives  62.9 us (60%)
  starting transfers between devices  21.7 us (21%)
  Pallas kernels  13.2 us (13%)
  waiting for transfers between devices  4.1 us (4%)
    all_gather x4, blocking collectives, gather(): lax.all_gather(value, 'dp', axis=0, axis_index_groups=list(groups.values()))  22.1 us
    all_to_all x1, blocking collectives, local(): lax.all_to_all(pack(own, other), 'tensor', 0, 0, tiled=True, axis_index_g...  20.6 us
    all_to_all x1, blocking collectives, exchange(): return lax.all_to_all(value, 'tensor', 0, 0, tiled=True)  20.2 us
    ppermute x1, starting transfers between devices, local(): other = lax.ppermute(half, 'dp', pairs)  9.11 us
    all_to_all x1, starting transfers between devices, exchange(): return lax.all_to_all(value, 'tensor', 0, 0, tiled=True)  6.51 us
    ppermute x1, starting transfers between devices, local(): lax.ppermute(give, 'tensor', [(source, source ^ 8) for source in range(NT)])  6.09 us
    pallas_call x1, Pallas kernels, make_weights(): pl.pallas_call(weights_kernel, in_specs=[HBM] * 3, out_specs=[VMEM] * 2,...  3.95 us
    ppermute x1, waiting for transfers between devices, local(): lax.ppermute(give, 'tensor', [(source, source ^ 8) for source in range(NT)])  3.74 us
  transfers between devices with their start and end apart: 3, of which 2 were waited for; matrix products, arithmetic and copies ran while one was open for 0% of the time, Pallas kernels for 6%

profile of v7, /device:TPU:6, one launch (start us, length us, event | category | flops | bytes accessed | tf_op | source)
XLA Modules:
  0.0 102.8 jit_solution(6852090974197385657)
XLA Ops:
  0.6 1.3 %sign.1 = (bf16[640,128]{1,0:T(8,128)(2,1)S(1)}, bf16[640,128]{1,0:T(8,128)(2,1)S(1)}) custom-call(s32[1]{0:T(128)} %bitcast.place, bf16[512,128]{1,0:T(8,128)(2,1)} %activ_hbm.1, s32[4,128]{1,0:T(4,128)} %bitcast.10, bf16[64,512]{1,0:T(8,128)(2,1)} %bitcast.12, bf16[256,128]{1,0:T(8,128)(2,1)} %cot.1), custom_call_target="tpu_custom_call" | custom-call | flops 60000000 | bytes 600000 | tf_op jit(solution)/shard_map/sign/pallas_call | solution.py:168
  1.9 6.1 %collective-permute-start = (bf16[640,128]{1,0:T(8,128)(2,1)S(1)}, bf16[640,128]{1,0:T(8,128)(2,1)S(1)}, u32[]{:S(2)}, u32[]{:S(2)}) collective-permute-start(bf16[640,128]{1,0:T(8,128)(2,1)S(1)} %get-tuple-element.24), channel_id=1, source_target_pairs={{0,8},{1,9},{2,10},{3,11},{4,12},{5,13},{6,14},{7,15},{8,0},{9,1},... | collective-permute-start | bytes 491528 | tf_op jit(solution)/shard_map/ppermute | solution.py:417
  8.0 4.0 %weights.1 = (bf16[4,512,1024]{2,1,0:T(8,128)(2,1)S(1)}, bf16[4,64,1024]{2,1,0:T(8,128)(2,1)S(1)}) custom-call(s32[512,1024]{1,0:T(8,128)} %codes_hbm.1, bf16[4,4096]{1,0:T(4,128)(2,1)} %scales_hbm.1, bf16[64,4096]{1,0:T(8,128)(2,1)} %up.1), custom_call_target="tpu_custom_call" | custom-call | flops 20000000 | bytes 20000000 | tf_op jit(solution)/shard_map/weights/pallas_call | solution.py:101
  11.9 3.7 %collective-permute-done.other = bf16[640,128]{1,0:T(8,128)(2,1)S(1)} collective-permute-done((bf16[640,128]{1,0:T(8,128)(2,1)S(1)}, bf16[640,128]{1,0:T(8,128)(2,1)S(1)}, u32[]{:S(2)}, u32[]{:S(2)}) %collective-permute-start) | collective-permute-done | bytes 163872 | tf_op jit(solution)/shard_map/ppermute | solution.py:417
  15.7 0.1 pack.1
  15.8 20.6 %all_to_all.15.got = bf16[8,608,128]{2,1,0:T(8,128)(2,1)S(1)} all-to-all(bf16[8,608,128]{2,1,0:T(8,128)(2,1)S(1)} %pack.1), channel_id=1, replica_groups={{0,1,2,3,4,5,6,7},{8,9,10,11,12,13,14,15},{16,17,18,19,20,21,22,23},{24..., dimensions={0} | all-to-all | bytes 2490368 | tf_op jit(solution)/shard_map/all_to_all | solution.py:421
  36.4 2.6 %turn.1 = (bf16[16,128,128]{2,1,0:T(8,128)(2,1)S(1)}, f32[64,128]{1,0:T(8,128)S(1)}) custom-call(s32[1]{0:T(128)} %bitcast.place, bf16[8,608,128]{2,1,0:T(8,128)(2,1)S(1)} %all_to_all.15.got, bf16[4,512,1024]{2,1,0:T(8,128)(2,1)S(1)} %get-tuple-element.27.weight, bf16[4,64,1024]{2,1,0:T(8,128)(2,1)S(1)} %get-tuple-element.28.up_apart, bf16[64,512]{1,0:T(8,128)(2,1)} %bitcast.13), custom_call_target="tpu_custom_call" | custom-call | flops 600000000 | bytes 7000000 | tf_op jit(solution)/shard_map/turn/pallas_call | solution.py:251
  39.0 20.2 %all_to_all.16.got = bf16[16,128,128]{2,1,0:T(8,128)(2,1)S(1)} all-to-all(bf16[16,128,128]{2,1,0:T(8,128)(2,1)S(1)} %get-tuple-element.29), channel_id=1, replica_groups=mesh['dp'=32,'tensor'=16] {'tensor'}, dimensions={0} | all-to-all | bytes 1048576 | tf_op jit(solution)/shard_map/all_to_all | solution.py:389
  59.2 2.5 %project.1 = (bf16[16,288,128]{2,1,0:T(8,128)(2,1)}, bf16[512,128]{1,0:T(8,128)(2,1)S(1)}) custom-call(bf16[16,128,128]{2,1,0:T(8,128)(2,1)S(1)} %all_to_all.16.got, bf16[4,512,1024]{2,1,0:T(8,128)(2,1)S(1)} %get-tuple-element.27.weight), custom_call_target="tpu_custom_call" | custom-call | flops 540000000 | bytes 6000000 | tf_op jit(solution)/shard_map/project/pallas_call | solution.py:312
  61.7 0.0 copy-start
  61.7 6.5 %all-to-all-start.2 = ((bf16[16,288,128]{2,1,0:T(8,128)(2,1)}), bf16[16,288,128]{2,1,0:T(8,128)(2,1)S(1)}, u32[]{:S(2)}, u32[]{:S(2)}) async-start(bf16[16,288,128]{2,1,0:T(8,128)(2,1)} %get-tuple-element.33), calls=%async_computation.2 | async-start | bytes 2359296 | tf_op jit(solution)/shard_map/all_to_all | solution.py:389
  68.2 0.0 copy-done
  68.2 0.4 adapter.1
  68.6 0.0 copy-start.1
  68.6 6.5 %all-gather = bf16[1536,128]{1,0:T(8,128)(2,1)S(1)} all-gather(bf16[384,128]{1,0:T(8,128)(2,1)S(1)} %convert_element_type.55), channel_id=2, replica_groups={{0,16,32,48},{64,80,96,112},{128,144,160,176},{192,208,224,240},{256,27..., dimensions={0}, use_global_device_ids=true | all-gather | bytes 491520 | tf_op jit(solution)/shard_map/all_gather | solution.py:399
  75.3 6.7 %all_gather.22 = bf16[2,192,128]{2,1,0:T(8,128)(2,1)S(1)} all-gather(bf16[1,192,128]{2,1,0:T(8,128)(2,1)S(1)} %fusion.1), channel_id=1, replica_groups={{0,64},{16,80},{32,96},{48,112},{128,192},{144,208},{160,224},{176,240}..., dimensions={0}, use_global_device_ids=true | all-gather | bytes 147456 | tf_op jit(solution)/shard_map/all_gather | solution.py:399
  82.0 6.9 %all_gather.23 = bf16[2,192,128]{2,1,0:T(8,128)(2,1)S(1)} all-gather(bf16[1,192,128]{2,1,0:T(8,128)(2,1)S(1)} %add_convert_fusion.2), channel_id=1, replica_groups={{0,192},{16,208},{32,224},{48,240},{64,128},{80,144},{96,160},{112,176}..., dimensions={0}, use_global_device_ids=true | all-gather | bytes 147456 | tf_op jit(solution)/shard_map/all_gather | solution.py:399
  88.9 9.1 %collective-permute-start.1 = (bf16[192,128]{1,0:T(8,128)(2,1)S(1)}, bf16[192,128]{1,0:T(8,128)(2,1)S(1)}, u32[]{:S(2)}, u32[]{:S(2)}) collective-permute-start(bf16[192,128]{1,0:T(8,128)(2,1)S(1)} %fusion), channel_id=1, source_target_pairs={{0,256},{16,272},{32,288},{48,304},{64,320},{80,336},{96,352},{112... | collective-permute-start | bytes 147464 | tf_op jit(solution)/shard_map/ppermute | solution.py:433
  98.0 0.0 all-to-all-done.2.got
  98.0 0.0 copy-done.1
  98.0 1.8 %finish.1 = (bf16[256,128]{1,0:T(8,128)(2,1)}, bf16[512,128]{1,0:T(8,128)(2,1)}) custom-call(s32[1]{0:T(128)} %bitcast.place, bf16[16,288,128]{2,1,0:T(8,128)(2,1)S(1)} %all-to-all-done.2.got, bf16[64,4096]{1,0:T(8,128)(2,1)} %up.1, f32[64,128]{1,0:T(8,128)S(1)} %get-tuple-element.34.down, s32[4,128]{1,0:T(4,128)S(1)} %bitcast.11), custom_call_target="tpu_custom_call" | custom-call | flops 40000000 | bytes 1700000 | tf_op jit(solution)/shard_map/finish/pallas_call | solution.py:348
  99.8 0.4 collective-permute-done.1
  100.2 1.9 %all-gather.1.sums = f32[384,128]{1,0:T(8,128)S(1)} all-gather(f32[192,128]{1,0:T(8,128)S(1)} %convert_add_fusion), channel_id=3, replica_groups={{0,16},{32,48},{64,80},{96,112},{128,144},{160,176},{192,208},{224,240}..., dimensions={0}, use_global_device_ids=true | all-gather | bytes 294912 | tf_op jit(solution)/shard_map/all_gather | solution.py:399
  102.1 0.7 gradients.1
  (6 shorter events, 0.1 us)
Async XLA Ops:
  1.9 13.8 %collective-permute-start = (bf16[640,128]{1,0:T(8,128)(2,1)S(1)}, bf16[640,128]{1,0:T(8,128)(2,1)S(1)}, u32[]{:S(2)}, u32[]{:S(2)}) collective-permute-start(bf16[640,128]{1,0:T(8,128)(2,1)S(1)} %get-tuple-element.24), channel_id=1, source_target_pairs={{0,8},{1,9},{2,10},{3,11},{4,12},{5,13},{6,14},{7,15},{8,0},{9,1},... | collective-permute-start | bytes 491528 | tf_op jit(solution)/shard_map/ppermute | solution.py:417
  61.7 6.5 %copy-start = (bf16[256,128]{1,0:T(8,128)(2,1)S(1)}, bf16[256,128]{1,0:T(8,128)(2,1)}, u32[]{:S(2)}) copy-start(bf16[256,128]{1,0:T(8,128)(2,1)} %cot.1) | copy-start | bytes 196612
  61.7 36.3 %all-to-all-start.2 = ((bf16[16,288,128]{2,1,0:T(8,128)(2,1)}), bf16[16,288,128]{2,1,0:T(8,128)(2,1)S(1)}, u32[]{:S(2)}, u32[]{:S(2)}) async-start(bf16[16,288,128]{2,1,0:T(8,128)(2,1)} %get-tuple-element.33), calls=%async_computation.2 | async-start | bytes 2359296 | tf_op jit(solution)/shard_map/all_to_all | solution.py:389
  68.6 29.4 %copy-start.1 = (s32[512]{0:T(512)S(1)}, s32[512]{0:T(512)}, u32[]{:S(2)}) copy-start(s32[512]{0:T(512)} %param.8) | copy-start | bytes 6148
  88.9 11.3 %collective-permute-start.1 = (bf16[192,128]{1,0:T(8,128)(2,1)S(1)}, bf16[192,128]{1,0:T(8,128)(2,1)S(1)}, u32[]{:S(2)}, u32[]{:S(2)}) collective-permute-start(bf16[192,128]{1,0:T(8,128)(2,1)S(1)} %fusion), channel_id=1, source_target_pairs={{0,256},{16,272},{32,288},{48,304},{64,320},{80,336},{96,352},{112... | collective-permute-start | bytes 147464 | tf_op jit(solution)/shard_map/ppermute | solution.py:433

commit v8 on v7

--- a/solution.py
+++ b/solution.py
@@ -63,7 +63,7 @@
 
 
 def weights_kernel(
-    codes_hbm, scales_hbm, up_hbm, weight, up_apart,
+    codes_hbm, scales_hbm, up_hbm, weight, weight_t, up_apart,
     codes, scales, up, scales_apart, sems,
 ):
     copy_scales = pltpu.make_async_copy(scales_hbm, scales, sems.at[4])
@@ -95,15 +95,17 @@
             nibble = ((codes[rows, :] >> (4 * k)) & 15) - 8
             part = nibble.astype(F32) * scales_apart[k, g : g + 1, :]
             weight[k, rows, :] = part.astype(BF16)
+            weight_t[k, :, rows] = part.T.astype(BF16)
 
 
 def make_weights(codes, scales, up):
     return pl.pallas_call(
         weights_kernel,
         in_specs=[HBM] * 3,
-        out_specs=[VMEM] * 2,
+        out_specs=[VMEM] * 3,
         out_shape=[
             pltpu.VMEM((4, F, C), BF16),
+            pltpu.VMEM((4, C, F), BF16),
             pltpu.VMEM((4, RANK, C), BF16),
         ],
         scratch_shapes=[
@@ -296,7 +298,7 @@
     )(got, mixed, back, cot)
 
 
-def project_kernel(got, weight, sent, mixed):
+def project_kernel(got, weight_t, sent, mixed):
     v = got[:, 0:32, :].astype(F32).reshape(NT, 4, 8, T)
     for h in range(4):
         mixed[GROUP * h : GROUP * (h + 1), :] = lanes_in_order(v[:, h]).astype(BF16)
@@ -304,11 +306,11 @@
     g = butterfly(g, 6) * 0.125
     sent[:, 256:288, :] = g.reshape(NT, 32, T).astype(BF16)
     for k in range(4):
-        share = dot_00(weight[k], mixed[...])
+        share = dot(weight_t[k], mixed[...])
         sent[:, 64 * k : 64 * (k + 1), :] = share.reshape(NT, 64, T).astype(BF16)
 
 
-def project(got, weight):
+def project(got, weight_t):
     return pl.pallas_call(
         project_kernel,
         in_specs=[VMEM] * 2,
@@ -320,7 +322,7 @@
         compiler_params=PARAMS,
         cost_estimate=pl.CostEstimate(flops=540_000_000, bytes_accessed=6_000_000, transcendentals=0),
         name="project",
-    )(got, *in_vmem(weight))
+    )(got, *in_vmem(weight_t))
 
 
 def finish_kernel(place, got, up, down, flags, out, input_gradient, own, sem):
@@ -415,7 +417,7 @@
     down_t = down_map.T
     own, give = sign(place, activ, flags, down_t, cot)
     other = lax.ppermute(give, "tensor", [(source, source ^ 8) for source in range(NT)])
-    weight, up_apart = make_weights(codes, scales, up)
+    weight, weight_t, up_apart = make_weights(codes, scales, up)
     other, weight = lax.optimization_barrier((other, weight))
     halves = [list(range(8)), list(range(8, NT))]
     got = lax.all_to_all(
@@ -423,7 +425,7 @@
     )
     sent, back = turn(place, got, weight, up_apart, down_t)
     got = exchange(sent)
-    sent, mixed = project(got, weight)
+    sent, mixed = project(got, weight_t)
     down, sums = adapter(got, mixed, back, cot)
     got = exchange(sent)
     half = lax.dynamic_slice_in_dim(sum_over(sums, (1, 2)), 192 * (replica & 1), 192)

time: 104 us -> 104 us (level)
  transfers between devices with their start and end apart: 3 -> 3, of which waited for: 2 -> 2; matrix products, arithmetic and copies ran while one was open for 0% -> 0% of each run, Pallas kernels for 6% -> 7%
where the time goes in v8:
time: 104 us; the launch traced here: 103 us
  blocking collectives  62.9 us (60%)
  starting transfers between devices  21.7 us (21%)
  Pallas kernels  13.8 us (13%)
  waiting for transfers between devices  3.29 us (3%)
    all_gather x4, blocking collectives, gather(): lax.all_gather(value, 'dp', axis=0, axis_index_groups=list(groups.values()))  22.1 us
    all_to_all x1, blocking collectives, local(): lax.all_to_all(pack(own, other), 'tensor', 0, 0, tiled=True, axis_index_g...  20.6 us
    all_to_all x1, blocking collectives, exchange(): return lax.all_to_all(value, 'tensor', 0, 0, tiled=True)  20.2 us
    ppermute x1, starting transfers between devices, local(): other = lax.ppermute(half, 'dp', pairs)  9.12 us
    all_to_all x1, starting transfers between devices, exchange(): return lax.all_to_all(value, 'tensor', 0, 0, tiled=True)  6.5 us
    ppermute x1, starting transfers between devices, local(): lax.ppermute(give, 'tensor', [(source, source ^ 8) for source in range(NT)])  6.09 us
    pallas_call x1, Pallas kernels, make_weights(): pl.pallas_call(weights_kernel, in_specs=[HBM] * 3, out_specs=[VMEM] * 3,...  4.76 us
    ppermute x1, waiting for transfers between devices, local(): lax.ppermute(give, 'tensor', [(source, source ^ 8) for source in range(NT)])  2.93 us
  transfers between devices with their start and end apart: 3, of which 2 were waited for; matrix products, arithmetic and copies ran while one was open for 0% of the time, Pallas kernels for 7%

profile of v8, /device:TPU:6, one launch (start us, length us, event | category | flops | bytes accessed | tf_op | source)
XLA Modules:
  0.0 102.6 jit_solution(12535787229143467929)
XLA Ops:
  0.6 1.3 %sign.1 = (bf16[640,128]{1,0:T(8,128)(2,1)S(1)}, bf16[640,128]{1,0:T(8,128)(2,1)S(1)}) custom-call(s32[1]{0:T(128)} %bitcast.place, bf16[512,128]{1,0:T(8,128)(2,1)} %activ_hbm.1, s32[4,128]{1,0:T(4,128)} %bitcast.10, bf16[64,512]{1,0:T(8,128)(2,1)} %bitcast.12, bf16[256,128]{1,0:T(8,128)(2,1)} %cot.1), custom_call_target="tpu_custom_call" | custom-call | flops 60000000 | bytes 600000 | tf_op jit(solution)/shard_map/sign/pallas_call | solution.py:170
  1.9 6.1 %collective-permute-start = (bf16[640,128]{1,0:T(8,128)(2,1)S(1)}, bf16[640,128]{1,0:T(8,128)(2,1)S(1)}, u32[]{:S(2)}, u32[]{:S(2)}) collective-permute-start(bf16[640,128]{1,0:T(8,128)(2,1)S(1)} %get-tuple-element.25), channel_id=1, source_target_pairs={{0,8},{1,9},{2,10},{3,11},{4,12},{5,13},{6,14},{7,15},{8,0},{9,1},... | collective-permute-start | bytes 491528 | tf_op jit(solution)/shard_map/ppermute | solution.py:419
  8.0 4.8 %weights.1 = (bf16[4,512,1024]{2,1,0:T(8,128)(2,1)S(1)}, bf16[4,1024,512]{2,1,0:T(8,128)(2,1)S(1)}, bf16[4,64,1024]{2,1,0:T(8,128)(2,1)S(1)}) custom-call(s32[512,1024]{1,0:T(8,128)} %codes_hbm.1, bf16[4,4096]{1,0:T(4,128)(2,1)} %scales_hbm.1, bf16[64,4096]{1,0:T(8,128)(2,1)} %up.1), custom_call_target="tpu_custom_call" | custom-call | flops 20000000 | bytes 20000000 | tf_op jit(solution)/shard_map/weights/pallas_call | solution.py:102
  12.8 2.9 %collective-permute-done.other = bf16[640,128]{1,0:T(8,128)(2,1)S(1)} collective-permute-done((bf16[640,128]{1,0:T(8,128)(2,1)S(1)}, bf16[640,128]{1,0:T(8,128)(2,1)S(1)}, u32[]{:S(2)}, u32[]{:S(2)}) %collective-permute-start) | collective-permute-done | bytes 163872 | tf_op jit(solution)/shard_map/ppermute | solution.py:419
  15.7 0.1 pack.1
  15.8 20.6 %all_to_all.15.got = bf16[8,608,128]{2,1,0:T(8,128)(2,1)S(1)} all-to-all(bf16[8,608,128]{2,1,0:T(8,128)(2,1)S(1)} %pack.1), channel_id=1, replica_groups={{0,1,2,3,4,5,6,7},{8,9,10,11,12,13,14,15},{16,17,18,19,20,21,22,23},{24..., dimensions={0} | all-to-all | bytes 2490368 | tf_op jit(solution)/shard_map/all_to_all | solution.py:423
  36.4 2.5 %turn.1 = (bf16[16,128,128]{2,1,0:T(8,128)(2,1)S(1)}, f32[64,128]{1,0:T(8,128)S(1)}) custom-call(s32[1]{0:T(128)} %bitcast.place, bf16[8,608,128]{2,1,0:T(8,128)(2,1)S(1)} %all_to_all.15.got, bf16[4,512,1024]{2,1,0:T(8,128)(2,1)S(1)} %get-tuple-element.28.weight, bf16[4,64,1024]{2,1,0:T(8,128)(2,1)S(1)} %get-tuple-element.29.up_apart, bf16[64,512]{1,0:T(8,128)(2,1)} %bitcast.13), custom_call_target="tpu_custom_call" | custom-call | flops 600000000 | bytes 7000000 | tf_op jit(solution)/shard_map/turn/pallas_call | solution.py:253
  38.9 20.2 %all_to_all.16.got = bf16[16,128,128]{2,1,0:T(8,128)(2,1)S(1)} all-to-all(bf16[16,128,128]{2,1,0:T(8,128)(2,1)S(1)} %get-tuple-element.30), channel_id=1, replica_groups=mesh['dp'=32,'tensor'=16] {'tensor'}, dimensions={0} | all-to-all | bytes 1048576 | tf_op jit(solution)/shard_map/all_to_all | solution.py:391
  59.2 2.3 %project.1 = (bf16[16,288,128]{2,1,0:T(8,128)(2,1)}, bf16[512,128]{1,0:T(8,128)(2,1)S(1)}) custom-call(bf16[16,128,128]{2,1,0:T(8,128)(2,1)S(1)} %all_to_all.16.got, bf16[4,1024,512]{2,1,0:T(8,128)(2,1)S(1)} %get-tuple-element.31.weight_t), custom_call_target="tpu_custom_call" | custom-call | flops 540000000 | bytes 6000000 | tf_op jit(solution)/shard_map/project/pallas_call | solution.py:314
  61.5 0.0 copy-start
  61.5 6.5 %all-to-all-start.2 = ((bf16[16,288,128]{2,1,0:T(8,128)(2,1)}), bf16[16,288,128]{2,1,0:T(8,128)(2,1)S(1)}, u32[]{:S(2)}, u32[]{:S(2)}) async-start(bf16[16,288,128]{2,1,0:T(8,128)(2,1)} %get-tuple-element.35), calls=%async_computation.2 | async-start | bytes 2359296 | tf_op jit(solution)/shard_map/all_to_all | solution.py:391
  68.0 0.0 copy-done
  68.0 0.4 adapter.1
  68.4 0.0 copy-start.1
  68.4 6.5 %all-gather = bf16[1536,128]{1,0:T(8,128)(2,1)S(1)} all-gather(bf16[384,128]{1,0:T(8,128)(2,1)S(1)} %convert_element_type.55), channel_id=2, replica_groups={{0,16,32,48},{64,80,96,112},{128,144,160,176},{192,208,224,240},{256,27..., dimensions={0}, use_global_device_ids=true | all-gather | bytes 491520 | tf_op jit(solution)/shard_map/all_gather | solution.py:401
  75.0 6.7 %all_gather.22 = bf16[2,192,128]{2,1,0:T(8,128)(2,1)S(1)} all-gather(bf16[1,192,128]{2,1,0:T(8,128)(2,1)S(1)} %fusion.1), channel_id=1, replica_groups={{0,64},{16,80},{32,96},{48,112},{128,192},{144,208},{160,224},{176,240}..., dimensions={0}, use_global_device_ids=true | all-gather | bytes 147456 | tf_op jit(solution)/shard_map/all_gather | solution.py:401
  81.8 6.9 %all_gather.23 = bf16[2,192,128]{2,1,0:T(8,128)(2,1)S(1)} all-gather(bf16[1,192,128]{2,1,0:T(8,128)(2,1)S(1)} %add_convert_fusion.2), channel_id=1, replica_groups={{0,192},{16,208},{32,224},{48,240},{64,128},{80,144},{96,160},{112,176}..., dimensions={0}, use_global_device_ids=true | all-gather | bytes 147456 | tf_op jit(solution)/shard_map/all_gather | solution.py:401
  88.7 9.1 %collective-permute-start.1 = (bf16[192,128]{1,0:T(8,128)(2,1)S(1)}, bf16[192,128]{1,0:T(8,128)(2,1)S(1)}, u32[]{:S(2)}, u32[]{:S(2)}) collective-permute-start(bf16[192,128]{1,0:T(8,128)(2,1)S(1)} %fusion), channel_id=1, source_target_pairs={{0,256},{16,272},{32,288},{48,304},{64,320},{80,336},{96,352},{112... | collective-permute-start | bytes 147464 | tf_op jit(solution)/shard_map/ppermute | solution.py:435
  97.8 0.0 all-to-all-done.2.got
  97.8 0.0 copy-done.1
  97.8 1.8 %finish.1 = (bf16[256,128]{1,0:T(8,128)(2,1)}, bf16[512,128]{1,0:T(8,128)(2,1)}) custom-call(s32[1]{0:T(128)} %bitcast.place, bf16[16,288,128]{2,1,0:T(8,128)(2,1)S(1)} %all-to-all-done.2.got, bf16[64,4096]{1,0:T(8,128)(2,1)} %up.1, f32[64,128]{1,0:T(8,128)S(1)} %get-tuple-element.36.down, s32[4,128]{1,0:T(4,128)S(1)} %bitcast.11), custom_call_target="tpu_custom_call" | custom-call | flops 40000000 | bytes 1700000 | tf_op jit(solution)/shard_map/finish/pallas_call | solution.py:350
  99.6 0.4 collective-permute-done.1
  100.0 1.9 %all-gather.1.sums = f32[384,128]{1,0:T(8,128)S(1)} all-gather(f32[192,128]{1,0:T(8,128)S(1)} %convert_add_fusion), channel_id=3, replica_groups={{0,16},{32,48},{64,80},{96,112},{128,144},{160,176},{192,208},{224,240}..., dimensions={0}, use_global_device_ids=true | all-gather | bytes 294912 | tf_op jit(solution)/shard_map/all_gather | solution.py:401
  101.9 0.7 gradients.1
  (6 shorter events, 0.1 us)
Async XLA Ops:
  1.9 13.8 %collective-permute-start = (bf16[640,128]{1,0:T(8,128)(2,1)S(1)}, bf16[640,128]{1,0:T(8,128)(2,1)S(1)}, u32[]{:S(2)}, u32[]{:S(2)}) collective-permute-start(bf16[640,128]{1,0:T(8,128)(2,1)S(1)} %get-tuple-element.25), channel_id=1, source_target_pairs={{0,8},{1,9},{2,10},{3,11},{4,12},{5,13},{6,14},{7,15},{8,0},{9,1},... | collective-permute-start | bytes 491528 | tf_op jit(solution)/shard_map/ppermute | solution.py:419
  61.5 6.5 %copy-start = (bf16[256,128]{1,0:T(8,128)(2,1)S(1)}, bf16[256,128]{1,0:T(8,128)(2,1)}, u32[]{:S(2)}) copy-start(bf16[256,128]{1,0:T(8,128)(2,1)} %cot.1) | copy-start | bytes 196612
  61.5 36.3 %all-to-all-start.2 = ((bf16[16,288,128]{2,1,0:T(8,128)(2,1)}), bf16[16,288,128]{2,1,0:T(8,128)(2,1)S(1)}, u32[]{:S(2)}, u32[]{:S(2)}) async-start(bf16[16,288,128]{2,1,0:T(8,128)(2,1)} %get-tuple-element.35), calls=%async_computation.2 | async-start | bytes 2359296 | tf_op jit(solution)/shard_map/all_to_all | solution.py:391
  68.4 29.4 %copy-start.1 = (s32[512]{0:T(512)S(1)}, s32[512]{0:T(512)}, u32[]{:S(2)}) copy-start(s32[512]{0:T(512)} %param.8) | copy-start | bytes 6148
  88.7 11.3 %collective-permute-start.1 = (bf16[192,128]{1,0:T(8,128)(2,1)S(1)}, bf16[192,128]{1,0:T(8,128)(2,1)S(1)}, u32[]{:S(2)}, u32[]{:S(2)}) collective-permute-start(bf16[192,128]{1,0:T(8,128)(2,1)S(1)} %fusion), channel_id=1, source_target_pairs={{0,256},{16,272},{32,288},{48,304},{64,320},{80,336},{96,352},{112... | collective-permute-start | bytes 147464 | tf_op jit(solution)/shard_map/ppermute | solution.py:435
